TPU v7x, 256 devices: a whole 4x4x8 slice. The times are simulated.
256 devices in a mesh: dp: 16 (over z, core), expert: 16 (over x, y).
Axes of the slice: x: 4, y: 4, z: 8, core: 2. Of those that a mesh axis runs over, the one named last changes fastest.
Arguments:
- tokens: bfloat16 [32768, 2048], P(('dp', 'expert')), may hold values from -6 to 6
- cotangent: bfloat16 [32768, 2048], P(('dp', 'expert')), may hold values from -1.5 to 1.5
- picks: int32 [16, 16, 256], P('dp'), may hold values from 0 to 2047, as said below
- gates: float32 [16, 16, 256], P('dp', 'expert'), may hold values from 0.25 to 1
- w_gate: bfloat16 [16, 2048, 768], P('expert'), may hold values from -0.125 to 0.125
- w_up: bfloat16 [16, 2048, 768], P('expert'), may hold values from -0.125 to 0.125
- w_down: bfloat16 [16, 768, 2048], P('expert'), may hold values from -0.21875 to 0.21875
Outputs:
- token_grads: bfloat16 [32768, 2048], P(('dp', 'expert'))
- gate_grads: float32 [16, 16, 256], P('dp', 'expert')
- grad_gate: bfloat16 [16, 2048, 768], P('expert', 'dp')
- grad_up: bfloat16 [16, 2048, 768], P('expert', 'dp')
- grad_down: bfloat16 [16, 768, 2048], P('expert', None, 'dp')
Inputs may be any that keep to these rules, and one draw needn't show every extreme that they name: Entry [g, e, c] is a token index within group g; token j * 128 + t of a group is local row t of device j along expert. An expert's 256 picks in a group are distinct and ascending. At most 24 of them lie among one device's tokens, and for every group and expert exactly 24 lie among some device's tokens.
All inputs are finite; a program needn't handle non-finite values.
Results may differ from a plain program's by a relative error of at most 0.023.
Values may be sent and summed in bfloat16 or wider, within the bound.
No kernel may reach another device: no remote copies, remote signals or barrier semaphores. Data moves between devices by JAX's collectives and lax.ppermute only.
A program may use at most 128 MiB of HBM per device.

v0:
```python
import jax
import jax.numpy as jnp
from jax import lax
from jax.experimental import pallas as pl
from jax.experimental.pallas import tpu as pltpu
from jax.sharding import PartitionSpec as P

BF16 = jnp.bfloat16
F32 = jnp.float32
I32 = jnp.int32
VMEM = pl.BlockSpec(memory_space=pltpu.VMEM)
SMEM = pl.BlockSpec(memory_space=pltpu.SMEM)


def dot_nn(left, right):
    return jnp.dot(left, right, preferred_element_type=F32)


def dot_nt(left, right):
    return lax.dot_general(left, right, (((1,), (1,)), ((), ())), preferred_element_type=F32)


def dot_tn(left, right):
    return lax.dot_general(left, right, (((0,), (0,)), ((), ())), preferred_element_type=F32)


def swap_cores(array):
    size = lax.axis_size("dp")
    return lax.ppermute(array, "dp", [(i, i ^ 1) for i in range(size)])


def next_chip(array, sign):
    size = lax.axis_size("dp")
    return lax.ppermute(array, "dp", [(i, (i + 2 * sign) % size) for i in range(size)])


def add(left, right):
    return (left.astype(F32) + right.astype(F32)).astype(BF16)


def two_way_sums(chunk_of, chips, axis):
    far = chips // 2

    def split(chunk):
        return jnp.split(chunk, 2, axis=axis)

    forward = next_chip(split(chunk_of(far))[0], 1)
    backward = next_chip(split(chunk_of(-far))[1], -1)
    for distance in range(far - 1, 0, -1):
        front, back = chunk_of(distance), chunk_of(-distance)
        if distance == far - 1:
            first, second = split(front)
            front = jnp.concatenate([add(forward, first), second], axis=axis)
            first, second = split(back)
            back = jnp.concatenate([first, add(backward, second)], axis=axis)
        else:
            front, back = add(forward, front), add(backward, back)
        forward, backward = next_chip(front, 1), next_chip(back, -1)
    return forward, backward


def finish_sums(own, forward, backward, axis):
    total = own.astype(F32)
    if forward.shape == own.shape:
        return (total + forward.astype(F32) + backward.astype(F32)).astype(BF16)
    arrived = jnp.concatenate([forward, backward], axis=axis)
    return (total + arrived.astype(F32)).astype(BF16)


def select_kernel(most, base_ref, picks_ref, tokens_ref, select_ref, out_ref):
    local = picks_ref[...] - base_ref[0]
    experts, slots = local.shape
    tok_dev = tokens_ref.shape[0]
    below = jnp.sum((local < 0).astype(F32), axis=1, keepdims=True).astype(I32)
    counter = lax.broadcasted_iota(I32, (most, 1), 0)
    spread = jnp.concatenate(
        [jnp.broadcast_to(local[e : e + 1], (most, slots)) for e in range(experts)], axis=0
    )
    wanted = jnp.concatenate([below[e : e + 1] + counter for e in range(experts)], axis=0)
    position = lax.broadcasted_iota(I32, spread.shape, 1)
    hit = (position == wanted) & (spread >= 0) & (spread < tok_dev)
    token = jnp.sum(jnp.where(hit, spread + 1, 0).astype(F32), axis=1, keepdims=True) - 1.0
    token_range = lax.broadcasted_iota(I32, (spread.shape[0], tok_dev), 1).astype(F32)
    select = (token_range == token).astype(F32).astype(BF16)
    select_ref[...] = select
    out_ref[...] = dot_nn(select, tokens_ref[...]).astype(BF16)


def gather_kernel(select_ref, tokens_ref, out_ref):
    out_ref[...] = dot_nn(select_ref[...], tokens_ref[...]).astype(BF16)


def take_kernel(most, tok_dev, own_ref, take_ref):
    slots, columns = take_ref.shape
    lane = lax.broadcasted_iota(I32, (1, columns), 1)
    source = jnp.zeros((1, columns), I32)
    for edge in range(most, columns, most):
        source = source + (lane >= edge).astype(I32)
    within = lane - source * most
    own = own_ref[...]
    start = jnp.sum((own < source * tok_dev).astype(F32), axis=0, keepdims=True)
    stop = jnp.sum((own < (source + 1) * tok_dev).astype(F32), axis=0, keepdims=True)
    slot = start + within.astype(F32)
    slot = jnp.where(slot < stop, slot, -1.0)
    slot_range = lax.broadcasted_iota(I32, (slots, columns), 0).astype(F32)
    take_ref[...] = (slot_range == slot).astype(F32).astype(BF16)


def compact_kernel(chips, place_ref, take_ref, arrived_ref, scale_ref, full_ref, keep_ref, give_ref):
    chip, core = place_ref[0], place_ref[1]
    block = arrived_ref.shape[1] // (2 * chips)
    for k in range(chips):
        columns = slice(2 * k * block, 2 * (k + 1) * block)
        value = dot_nn(take_ref[...], arrived_ref[:, columns])
        full_ref[:, columns] = value.astype(BF16)
        if scale_ref is not None:
            value = value * scale_ref[...]
        value = value.astype(BF16)
        even, odd = value[:, :block], value[:, block:]
        where = pl.ds(pl.multiple_of(lax.rem(k - chip + chips, chips) * block, block), block)

        @pl.when(core == 0)
        def _():
            keep_ref[:, where] = even
            give_ref[:, where] = odd

        @pl.when(core != 0)
        def _():
            keep_ref[:, where] = odd
            give_ref[:, where] = even


def plain_compact_kernel(chips, place_ref, take_ref, arrived_ref, full_ref, keep_ref, give_ref):
    compact_kernel(chips, place_ref, take_ref, arrived_ref, None, full_ref, keep_ref, give_ref)


def call(kernel, out_shapes, in_specs, operands, limit_mib, flops, bytes_accessed):
    return pl.pallas_call(
        kernel,
        out_shape=out_shapes,
        in_specs=in_specs,
        out_specs=jax.tree.map(lambda _: VMEM, out_shapes),
        compiler_params=pltpu.CompilerParams(vmem_limit_bytes=limit_mib * 2**20),
        cost_estimate=pl.CostEstimate(
            flops=flops, bytes_accessed=bytes_accessed, transcendentals=0
        ),
    )(*operands)


def body(tokens, cotangent, picks, gates, w_gate, w_up, w_down):
    node_count = lax.axis_size("expert")
    self_index = lax.axis_index("expert")
    dp_size = lax.axis_size("dp")
    dp_index = lax.axis_index("dp")
    chips = dp_size // 2
    place = jnp.stack([lax.shift_right_logical(dp_index, 1), dp_index & 1]).astype(I32)
    tok_dev, width = tokens.shape
    slot_count = gates.shape[2]
    most = max(2, 3 * slot_count // (2 * node_count))
    padded = node_count * most
    hidden_width = w_gate.shape[2]
    block = width // dp_size

    def shape(*dims, dtype=BF16):
        return jax.ShapeDtypeStruct(dims, dtype)

    table = picks[0]
    base = (self_index * tok_dev).astype(I32).reshape(1)
    select, out_rows = call(
        lambda *refs: select_kernel(most, *refs),
        (shape(padded, tok_dev), shape(padded, width)),
        [SMEM, VMEM, VMEM],
        (base, table, tokens),
        16, 2 * padded * tok_dev * width, 4 * padded * width,
    )
    out_grads = call(
        gather_kernel,
        shape(padded, width),
        [VMEM, VMEM],
        (select, cotangent),
        16, 2 * padded * tok_dev * width, 4 * padded * width,
    )

    def exchange(array):
        shaped = array.reshape(node_count, most, width)
        return lax.all_to_all(shaped, "expert", 0, 0, tiled=True).reshape(padded, width)

    arrived_rows = exchange(out_rows)
    arrived_grads = exchange(out_grads)

    own = lax.dynamic_index_in_dim(table, self_index, 0, keepdims=False)
    take = call(
        lambda *refs: take_kernel(most, tok_dev, *refs),
        shape(slot_count, padded),
        [VMEM],
        (own.reshape(slot_count, 1),),
        8, 8 * slot_count * padded, 2 * slot_count * padded,
    )
    compact_shapes = (
        shape(slot_count, width), shape(slot_count, width // 2), shape(slot_count, width // 2)
    )
    compact_cost = (24, 2 * slot_count * padded * width, 8 * slot_count * width)
    rows, rows_keep, rows_give = call(
        lambda *refs: plain_compact_kernel(chips, *refs),
        compact_shapes,
        [SMEM, VMEM, VMEM],
        (place, take, arrived_rows),
        *compact_cost,
    )
    rows_both = jnp.concatenate([rows_keep, swap_cores(rows_give)], axis=0)
    gate_pre = dot_nn(rows, w_gate[0])
    up_pre = dot_nn(rows, w_up[0])
    sigmoid_gate = jax.nn.sigmoid(gate_pre)
    activated = gate_pre * sigmoid_gate
    slope = up_pre * sigmoid_gate * (1.0 + gate_pre * (1.0 - sigmoid_gate))
    hidden = (activated * up_pre).astype(BF16)
    hidden_both = jnp.concatenate([hidden, swap_cores(hidden)], axis=0)

    gate_rows = gates.reshape(slot_count, 1)
    grads, scaled_keep, scaled_give = call(
        lambda *refs: compact_kernel(chips, *refs),
        compact_shapes,
        [SMEM, VMEM, VMEM, VMEM],
        (place, take, arrived_grads, gate_rows),
        *compact_cost,
    )
    scaled_both = jnp.concatenate([scaled_keep, swap_cores(scaled_give)], axis=0)
    raw_grad = dot_nt(grads, w_down[0])
    slot_grads = jnp.sum(raw_grad * hidden.astype(F32), axis=1)
    hidden_grad = gate_rows * raw_grad
    gate_pre_grad = (hidden_grad * slope).astype(BF16)
    up_pre_grad = (hidden_grad * activated).astype(BF16)
    pre_grads = jnp.concatenate([gate_pre_grad, up_pre_grad], axis=1)
    pre_both = jnp.concatenate([pre_grads, swap_cores(pre_grads)], axis=0)
    down_part = dot_tn(hidden_both, scaled_both).astype(BF16)
    pre_part = dot_tn(rows_both, pre_both).astype(BF16)

    def down_chunk(away):
        return down_part[:, away % chips * block : (away % chips + 1) * block]

    def pre_chunk(away):
        return pre_part[away % chips * block : (away % chips + 1) * block]

    if chips > 1:
        down_sums = two_way_sums(down_chunk, chips, 0)
        pre_sums = two_way_sums(pre_chunk, chips, 1)
        pre_grads, _ = lax.optimization_barrier((pre_grads, pre_part))

    gate_pre_grad, up_pre_grad = jnp.split(pre_grads, 2, axis=1)
    row_grads = (dot_nt(gate_pre_grad, w_gate[0]) + dot_nt(up_pre_grad, w_up[0])).astype(BF16)
    token_grads = dot_tn(select, exchange(dot_tn(take, row_grads).astype(BF16))).astype(BF16)

    if chips > 1:
        token_grads, down_sums, pre_sums = lax.optimization_barrier(
            (token_grads, down_sums, pre_sums)
        )
        grad_down = finish_sums(down_chunk(0), *down_sums, 0)
        grad_pre = finish_sums(pre_chunk(0), *pre_sums, 1)
    else:
        grad_down, grad_pre = down_part, pre_part
    return (
        token_grads,
        slot_grads[None, None],
        grad_pre[None, :, :hidden_width],
        grad_pre[None, :, hidden_width:],
        grad_down[None],
    )


def solution(mesh):
    return jax.shard_map(
        body,
        mesh=mesh,
        in_specs=(
            P(("dp", "expert"), None),
            P(("dp", "expert"), None),
            P("dp", None, None),
            P("dp", "expert", None),
            P("expert", None, None),
            P("expert", None, None),
            P("expert", None, None),
        ),
        out_specs=(
            P(("dp", "expert"), None),
            P("dp", "expert", None),
            P("expert", "dp", None),
            P("expert", "dp", None),
            P("expert", None, "dp"),
        ),
        check_vma=False,
    )
```

profile of v0, /device:TPU:2, one launch (start us, length us, event | category | flops | bytes accessed | tf_op | source)
XLA Modules:
  0.0 144.4 jit_solution(10030212274494983385)
XLA Ops:
  0.7 0.9 copy-done.7
  1.5 1.1 copy-done.8
  2.6 1.0 shard_map.110
  3.7 1.1 copy-done.2
  4.8 7.5 %all-to-all-start.1 = ((bf16[16,24,2048]{2,1,0:T(8,128)(2,1)}), bf16[16,24,2048]{2,1,0:T(8,128)(2,1)}, u32[]{:S(2)}, u32[]{:S(2)}) async-start(bf16[16,24,2048]{2,1,0:T(8,128)(2,1)} %bitcast.49), calls=%async_computation.1 | async-start | bytes 3145728 | tf_op jit(solution)/shard_map/all_to_all | solution.py:186
  12.3 1.0 copy-done.4
  13.9 1.2 copy-done.1
  15.1 18.7 %all-to-all-done.1 = bf16[16,24,2048]{2,1,0:T(8,128)(2,1)} async-done(((bf16[16,24,2048]{2,1,0:T(8,128)(2,1)}), bf16[16,24,2048]{2,1,0:T(8,128)(2,1)}, u32[]{:S(2)}, u32[]{:S(2)}) %all-to-all-start.1) | async-done | bytes 1572896 | tf_op jit(solution)/shard_map/all_to_all | solution.py:186
  33.8 6.6 %all-to-all-start = ((bf16[16,24,2048]{2,1,0:T(8,128)(2,1)}), bf16[16,24,2048]{2,1,0:T(8,128)(2,1)}, u32[]{:S(2)}, u32[]{:S(2)}) async-start(bf16[16,24,2048]{2,1,0:T(8,128)(2,1)} %bitcast.48), calls=%async_computation | async-start | bytes 3145728 | tf_op jit(solution)/shard_map/all_to_all | solution.py:186
  41.1 0.8 copy.12.refs_0_
  42.1 0.9 copy-done.3
  43.3 3.9 %shard_map.114 = (bf16[256,2048]{1,0:T(8,128)(2,1)S(1)}, bf16[256,1024]{1,0:T(8,128)(2,1)S(1)}, bf16[256,1024]{1,0:T(8,128)(2,1)S(1)}) custom-call(s32[2]{0:T(128)S(1)} %pad_add_fusion.refs_0_, bf16[256,384]{1,0:T(8,128)(2,1)S(1)} %shard_map.111.refs_1_, bf16[384,2048]{1,0:T(8,128)(2,1)} %bitcast.11.refs_2_), custom_call_target="tpu_custom_call" | custom-call | flops 402653184 | bytes 4194304 | tf_op jit(solution)/shard_map/pallas_call | solution.py:138
  47.2 1.9 %fusion.6 = f32[256,768]{1,0:T(8,128)} fusion(bf16[256,2048]{1,0:T(8,128)(2,1)S(1)} %get-tuple-element.22, bf16[1,2048,768]{2,1,0:T(8,128)(2,1)S(1)} %copy-done), kind=kOutput, calls=%fused_computation.7 | convolution fusion | flops 805306368 | bytes 4980736 | tf_op jit(solution)/shard_map/dot_general | solution.py:16
  49.8 1.9 %fusion.2 = f32[256,768]{1,0:T(8,128)} fusion(bf16[256,2048]{1,0:T(8,128)(2,1)S(1)} %get-tuple-element.22, bf16[1,2048,768]{2,1,0:T(8,128)(2,1)S(1)} %copy-done.13), kind=kOutput, calls=%fused_computation.3 | convolution fusion | flops 805306368 | bytes 4980736 | tf_op jit(solution)/shard_map/dot_general | solution.py:16
  51.7 8.4 %all-to-all-done = bf16[16,24,2048]{2,1,0:T(8,128)(2,1)} async-done(((bf16[16,24,2048]{2,1,0:T(8,128)(2,1)}), bf16[16,24,2048]{2,1,0:T(8,128)(2,1)}, u32[]{:S(2)}, u32[]{:S(2)}) %all-to-all-start) | async-done | bytes 1572896 | tf_op jit(solution)/shard_map/all_to_all | solution.py:186
  60.1 3.9 %shard_map.113 = (bf16[256,2048]{1,0:T(8,128)(2,1)S(1)}, bf16[256,1024]{1,0:T(8,128)(2,1)S(1)}, bf16[256,1024]{1,0:T(8,128)(2,1)S(1)}) custom-call(s32[2]{0:T(128)S(1)} %pad_add_fusion.refs_0_, bf16[256,384]{1,0:T(8,128)(2,1)S(1)} %shard_map.111.refs_1_, bf16[384,2048]{1,0:T(8,128)(2,1)} %bitcast.7.refs_2_, f32[256,1]{1,0:T(8,128)S(1)} %copy.13.refs_3_), custom_call_target="tpu_custom_call" | custom-call | flops 402653184 | bytes 4194304 | tf_op jit(solution)/shard_map/pallas_call | solution.py:138
  64.1 4.3 %multiply_reduce_fusion = (f32[256]{0:T(256)}, bf16[256,768]{1,0:T(8,128)(2,1)S(1)}, bf16[256,768]{1,0:T(8,128)(2,1)S(1)}, bf16[256,768]{1,0:T(8,128)(2,1)S(1)}) fusion(f32[256,768]{1,0:T(8,128)} %fusion.6, f32[256,768]{1,0:T(8,128)} %fusion.2, f32[256]{0:T(256)S(1)} %bitcast.53, bf16[256,2048]{1,0:T(8,128)(2,1)S(1)} %get-tuple-element.20, ...), kind=kOutput, calls=%fused_computation.32 | convolution fusion | flops 809041664 | bytes 6948864 | tf_op jit(solution)/shard_map/dot_general | solution.py:20
  69.1 1.2 collective-permute-done.2
  70.3 1.0 convolution_convert_fusion.3
  71.4 5.9 %collective-permute-start.8 = (bf16[384,128]{1,0:T(8,128)(2,1)S(1)}, bf16[384,128]{1,0:T(8,128)(2,1)S(1)}, u32[]{:S(2)}, u32[]{:S(2)}) collective-permute-start(bf16[384,128]{1,0:T(8,128)(2,1)S(1)} %get-tuple-element.52), channel_id=1, source_target_pairs={{0,224},{16,240},{32,0},{48,16},{64,32},{80,48},{96,64},{112,80},{... | collective-permute-start | bytes 294920 | tf_op jit(solution)/shard_map/ppermute | solution.py:34
  77.4 2.5 %collective-permute-done.8 = bf16[384,128]{1,0:T(8,128)(2,1)S(1)} collective-permute-done((bf16[384,128]{1,0:T(8,128)(2,1)S(1)}, bf16[384,128]{1,0:T(8,128)(2,1)S(1)}, u32[]{:S(2)}, u32[]{:S(2)}) %collective-permute-start.8) | collective-permute-done | bytes 98336 | tf_op jit(solution)/shard_map/ppermute | solution.py:34
  79.9 3.4 %collective-permute-done.4 = bf16[384,128]{1,0:T(8,128)(2,1)S(1)} collective-permute-done((bf16[384,128]{1,0:T(8,128)(2,1)S(1)}, bf16[384,128]{1,0:T(8,128)(2,1)S(1)}, u32[]{:S(2)}, u32[]{:S(2)}) %collective-permute-start.4) | collective-permute-done | bytes 98336 | tf_op jit(solution)/shard_map/ppermute | solution.py:34
  85.0 1.7 %collective-permute-start.5 = (bf16[768,128]{1,0:T(8,128)(2,1)}, bf16[768,128]{1,0:T(8,128)(2,1)}, u32[]{:S(2)}, u32[]{:S(2)}) collective-permute-start(bf16[768,128]{1,0:T(8,128)(2,1)} %pad_maximum_fusion.3), channel_id=1, source_target_pairs={{0,32},{16,48},{32,64},{48,80},{64,96},{80,112},{96,128},{112,144}... | collective-permute-start | bytes 589832 | tf_op jit(solution)/shard_map/ppermute | solution.py:34
  86.8 1.8 %convolution_convert_fusion = bf16[1024,1536]{1,0:T(8,128)(2,1)S(1)} fusion(bf16[256,1536]{1,0:T(8,128)(2,1)S(1)} %collective-permute-done.1, bf16[256,768]{1,0:T(8,128)(2,1)S(1)} %get-tuple-element.46, bf16[256,768]{1,0:T(8,128)(2,1)S(1)} %get-tuple-element.45, bf16[256,1024]{1,0:T(8,128)(2,1)S(1)} %collective-permute-done, bf16[256,1024]{1,0:T(8,128)(2,1)S(1)} %copy-done.10), kind=kOutput, calls=%fused_computation | convolution fusion | flops 1619001344 | bytes 5767168 | tf_op jit(solution)/shard_map/dot_general | solution.py:24
  88.7 1.6 %collective-permute-start.16 = (bf16[128,768]{1,0:T(8,128)(2,1)S(1)}, bf16[128,768]{1,0:T(8,128)(2,1)S(1)}, u32[]{:S(2)}, u32[]{:S(2)}) collective-permute-start(bf16[128,768]{1,0:T(8,128)(2,1)S(1)} %get-tuple-element.40), channel_id=1, source_target_pairs={{0,224},{16,240},{32,0},{48,16},{64,32},{80,48},{96,64},{112,80},{... | collective-permute-start | bytes 589832 | tf_op jit(solution)/shard_map/ppermute | solution.py:34
  90.8 2.3 %fusion = f32[256,2048]{1,0:T(8,128)} fusion(bf16[1,2048,768]{2,1,0:T(8,128)(2,1)S(1)} %copy-done.14, bf16[256,1536]{1,0:T(8,128)(2,1)S(1)} %pad_maximum_fusion), kind=kOutput, calls=%fused_computation.1 | convolution fusion | flops 805306368 | bytes 5636096 | tf_op jit(solution)/shard_map/dot_general | solution.py:20
  93.2 1.3 collective-permute-done.16
  94.5 2.6 %collective-permute-done.12 = bf16[128,768]{1,0:T(8,128)(2,1)S(1)} collective-permute-done((bf16[128,768]{1,0:T(8,128)(2,1)S(1)}, bf16[128,768]{1,0:T(8,128)(2,1)S(1)}, u32[]{:S(2)}, u32[]{:S(2)}) %collective-permute-start.12) | collective-permute-done | bytes 196640 | tf_op jit(solution)/shard_map/ppermute | solution.py:34
  97.3 0.8 pad_maximum_fusion.2
  98.2 0.8 pad_maximum_fusion.1
  99.0 1.9 %collective-permute-start.13 = (bf16[128,1536]{1,0:T(8,128)(2,1)}, bf16[128,1536]{1,0:T(8,128)(2,1)}, u32[]{:S(2)}, u32[]{:S(2)}) collective-permute-start(bf16[128,1536]{1,0:T(8,128)(2,1)} %pad_maximum_fusion.1), channel_id=1, source_target_pairs={{0,32},{16,48},{32,64},{48,80},{64,96},{80,112},{96,128},{112,144}... | collective-permute-start | bytes 1179656 | tf_op jit(solution)/shard_map/ppermute | solution.py:34
  100.9 4.4 %convolution_convert_fusion.1 = bf16[384,2048]{1,0:T(8,128)(2,1)} fusion(bf16[256,384]{1,0:T(8,128)(2,1)S(1)} %shard_map.111.refs_1_, f32[256,2048]{1,0:T(8,128)} %fusion, bf16[1,2048,768]{2,1,0:T(8,128)(2,1)S(1)} %copy-done, bf16[256,1536]{1,0:T(8,128)(2,1)} %copy-done.16), kind=kOutput, calls=%fused_computation.11 | convolution fusion | flops 1209794560 | bytes 7405568 | tf_op jit(solution)/shard_map/dot_general | solution.py:24
  105.2 5.9 %all-to-all-start.2 = ((bf16[16,24,2048]{2,1,0:T(8,128)(2,1)}), bf16[16,24,2048]{2,1,0:T(8,128)(2,1)}, u32[]{:S(2)}, u32[]{:S(2)}) async-start(bf16[16,24,2048]{2,1,0:T(8,128)(2,1)} %bitcast.51), calls=%async_computation.2 | async-start | bytes 3145728 | tf_op jit(solution)/shard_map/all_to_all | solution.py:186
  111.1 1.7 %add_convert_fusion.2 = (bf16[128,1536]{1,0:T(8,128)(2,1)S(1)}, bf16[128,1536]{1,0:T(8,128)(2,1)S(1)}) fusion(bf16[128,1536]{1,0:T(8,128)(2,1)} %collective-permute-done.17, bf16[1024,1536]{1,0:T(8,128)(2,1)} %copy-done.15, bf16[128,1536]{1,0:T(8,128)(2,1)} %collective-permute-done.13), kind=kLoop, calls=%fused_computation.34 | loop fusion | flops 1572864 | bytes 2359296 | tf_op jit(solution)/shard_map/convert_element_type | solution.py:38
  112.8 1.4 collective-permute-start.18
  114.9 1.0 add_convert_fusion.9
  116.0 2.6 %collective-permute-start.10 = (bf16[768,128]{1,0:T(8,128)(2,1)S(1)}, bf16[768,128]{1,0:T(8,128)(2,1)S(1)}, u32[]{:S(2)}, u32[]{:S(2)}) collective-permute-start(bf16[768,128]{1,0:T(8,128)(2,1)S(1)} %get-tuple-element.49), channel_id=1, source_target_pairs={{0,224},{16,240},{32,0},{48,16},{64,32},{80,48},{96,64},{112,80},{... | collective-permute-start | bytes 589832 | tf_op jit(solution)/shard_map/ppermute | solution.py:34
  118.6 4.1 %collective-permute-done.18 = bf16[128,1536]{1,0:T(8,128)(2,1)S(1)} collective-permute-done((bf16[128,1536]{1,0:T(8,128)(2,1)S(1)}, bf16[128,1536]{1,0:T(8,128)(2,1)S(1)}, u32[]{:S(2)}, u32[]{:S(2)}) %collective-permute-start.18) | collective-permute-done | bytes 393248 | tf_op jit(solution)/shard_map/ppermute | solution.py:34
  122.7 2.8 %collective-permute-done.14 = bf16[128,1536]{1,0:T(8,128)(2,1)S(1)} collective-permute-done((bf16[128,1536]{1,0:T(8,128)(2,1)S(1)}, bf16[128,1536]{1,0:T(8,128)(2,1)S(1)}, u32[]{:S(2)}, u32[]{:S(2)}) %collective-permute-start.14) | collective-permute-done | bytes 393248 | tf_op jit(solution)/shard_map/ppermute | solution.py:34
  125.5 2.2 %add_convert_fusion.1 = (bf16[128,1536]{1,0:T(8,128)(2,1)}, bf16[128,1536]{1,0:T(8,128)(2,1)}) fusion(bf16[128,1536]{1,0:T(8,128)(2,1)S(1)} %collective-permute-done.18, bf16[1024,1536]{1,0:T(8,128)(2,1)} %copy-done.15, bf16[128,1536]{1,0:T(8,128)(2,1)S(1)} %collective-permute-done.14), kind=kLoop, calls=%fused_computation.33 | loop fusion | flops 1572864 | bytes 2359296 | tf_op jit(solution)/shard_map/convert_element_type | solution.py:38
  127.7 3.2 %collective-permute-start.19 = (bf16[128,1536]{1,0:T(8,128)(2,1)}, bf16[128,1536]{1,0:T(8,128)(2,1)}, u32[]{:S(2)}, u32[]{:S(2)}) collective-permute-start(bf16[128,1536]{1,0:T(8,128)(2,1)} %get-tuple-element.35), channel_id=1, source_target_pairs={{0,224},{16,240},{32,0},{48,16},{64,32},{80,48},{96,64},{112,80},{... | collective-permute-start | bytes 1179656 | tf_op jit(solution)/shard_map/ppermute | solution.py:34
  131.0 0.8 add_convert_fusion.8
  131.7 3.2 %collective-permute-start.11 = (bf16[768,128]{1,0:T(8,128)(2,1)S(1)}, bf16[768,128]{1,0:T(8,128)(2,1)}, u32[]{:S(2)}, u32[]{:S(2)}) collective-permute-start(bf16[768,128]{1,0:T(8,128)(2,1)S(1)} %get-tuple-element.47), channel_id=1, source_target_pairs={{0,224},{16,240},{32,0},{48,16},{64,32},{80,48},{96,64},{112,80},{... | collective-permute-start | bytes 589832 | tf_op jit(solution)/shard_map/ppermute | solution.py:34
  135.0 2.7 %convolution_convert_fusion.2 = bf16[128,2048]{1,0:T(8,128)(2,1)} fusion(bf16[384,128]{1,0:T(8,128)(2,1)S(1)} %copy-done.6, bf16[384,2048]{1,0:T(8,128)(2,1)} %bitcast.15), kind=kOutput, calls=%fused_computation.14 | convolution fusion | flops 201588736 | bytes 2195456 | tf_op jit(solution)/shard_map/dot_general | solution.py:24
  137.7 2.7 %collective-permute-done.7 = bf16[768,128]{1,0:T(8,128)(2,1)} collective-permute-done((bf16[768,128]{1,0:T(8,128)(2,1)}, bf16[768,128]{1,0:T(8,128)(2,1)}, u32[]{:S(2)}, u32[]{:S(2)}) %collective-permute-start.7) | collective-permute-done | bytes 196640 | tf_op jit(solution)/shard_map/ppermute | solution.py:34
  140.4 1.4 add_convert_fusion
  141.8 0.8 slice_bitcast_fusion
  142.5 1.9 %fusion.36 = bf16[1,768,128]{2,1,0:T(8,128)(2,1)} fusion(bf16[768,128]{1,0:T(8,128)(2,1)} %collective-permute-done.11, bf16[768,128]{1,0:T(8,128)(2,1)} %collective-permute-done.7, bf16[768,1024]{1,0:T(8,128)(2,1)} %copy-done.17), kind=kLoop, calls=%fused_computation.53 | loop fusion | flops 589824 | bytes 786432 | tf_op jit(solution)/shard_map/broadcast_in_dim | solution.py:266
  (71 shorter events, 6.6 us)
Async XLA Ops:
  0.6 46.6 %copy-start = (bf16[1,2048,768]{2,1,0:T(8,128)(2,1)S(1)}, bf16[1,2048,768]{2,1,0:T(8,128)(2,1)}, u32[]{:S(2)}) copy-start(bf16[1,2048,768]{2,1,0:T(8,128)(2,1)} %param.12) | copy-start | bytes 9437188
  0.7 0.9 copy-start.7
  1.5 1.1 copy-start.8
  3.7 1.1 copy-start.2
  4.8 9.1 %copy-start.5 = (bf16[384,128]{1,0:T(8,128)(2,1)}, bf16[384,128]{1,0:T(8,128)(2,1)S(1)}, u32[]{:S(2)}) copy-start(bf16[384,128]{1,0:T(8,128)(2,1)S(1)} %get-tuple-element.19.select_ref) | copy-start | bytes 294916
  4.8 29.0 %all-to-all-start.1 = ((bf16[16,24,2048]{2,1,0:T(8,128)(2,1)}), bf16[16,24,2048]{2,1,0:T(8,128)(2,1)}, u32[]{:S(2)}, u32[]{:S(2)}) async-start(bf16[16,24,2048]{2,1,0:T(8,128)(2,1)} %bitcast.49), calls=%async_computation.1 | async-start | bytes 3145728 | tf_op jit(solution)/shard_map/all_to_all | solution.py:186
  12.3 1.0 copy-start.4
  13.9 1.2 copy-start.1
  15.1 26.9 %copy-start.19 = (f32[1,1,256]{2,1,0:T(1,128)S(1)}, f32[1,1,256]{2,1,0:T(1,128)}, u32[]{:S(2)}) copy-start(f32[1,1,256]{2,1,0:T(1,128)} %param.10) | copy-start | bytes 3076
  33.8 26.3 %all-to-all-start = ((bf16[16,24,2048]{2,1,0:T(8,128)(2,1)}), bf16[16,24,2048]{2,1,0:T(8,128)(2,1)}, u32[]{:S(2)}, u32[]{:S(2)}) async-start(bf16[16,24,2048]{2,1,0:T(8,128)(2,1)} %bitcast.48), calls=%async_computation | async-start | bytes 3145728 | tf_op jit(solution)/shard_map/all_to_all | solution.py:186
  42.1 0.9 copy-start.3
  47.2 1.9 %copy-start.9 = (bf16[256,1024]{1,0:T(8,128)(2,1)}, bf16[256,1024]{1,0:T(8,128)(2,1)S(1)}, u32[]{:S(2)}) copy-start(bf16[256,1024]{1,0:T(8,128)(2,1)S(1)} %get-tuple-element.23) | copy-start | bytes 1572868
  47.2 1.9 %copy-start.11 = (bf16[256,1024]{1,0:T(8,128)(2,1)}, bf16[256,1024]{1,0:T(8,128)(2,1)S(1)}, u32[]{:S(2)}) copy-start(bf16[256,1024]{1,0:T(8,128)(2,1)S(1)} %get-tuple-element.24) | copy-start | bytes 1572868
  47.2 2.5 %copy-start.13 = (bf16[1,2048,768]{2,1,0:T(8,128)(2,1)S(1)}, bf16[1,2048,768]{2,1,0:T(8,128)(2,1)}, u32[]{:S(2)}) copy-start(bf16[1,2048,768]{2,1,0:T(8,128)(2,1)} %param.11) | copy-start | bytes 9437188
  64.0 6.2 %collective-permute-start.3 = (bf16[256,1024]{1,0:T(8,128)(2,1)S(1)}, bf16[256,1024]{1,0:T(8,128)(2,1)S(1)}, u32[]{:S(2)}, u32[]{:S(2)}) collective-permute-start(bf16[256,1024]{1,0:T(8,128)(2,1)S(1)} %get-tuple-element.27), channel_id=1, source_target_pairs={{0,16},{16,0},{32,48},{48,32},{64,80},{80,64},{96,112},{112,96},{1... | collective-permute-start | bytes 1572872 | tf_op jit(solution)/shard_map/ppermute | solution.py:29
  68.4 1.8 %collective-permute-start.2 = (bf16[256,768]{1,0:T(8,128)(2,1)S(1)}, bf16[256,768]{1,0:T(8,128)(2,1)S(1)}, u32[]{:S(2)}, u32[]{:S(2)}) collective-permute-start(bf16[256,768]{1,0:T(8,128)(2,1)S(1)} %get-tuple-element.34), channel_id=1, source_target_pairs={{0,16},{16,0},{32,48},{48,32},{64,80},{80,64},{96,112},{112,96},{1... | collective-permute-start | bytes 1179656 | tf_op jit(solution)/shard_map/ppermute | solution.py:29
  69.0 21.9 %copy-start.16 = (bf16[256,1536]{1,0:T(8,128)(2,1)}, bf16[256,1536]{1,0:T(8,128)(2,1)S(1)}, u32[]{:S(2)}) copy-start(bf16[256,1536]{1,0:T(8,128)(2,1)S(1)} %pad_maximum_fusion) | copy-start | bytes 2359300
  69.0 17.8 %collective-permute-start.1 = (bf16[256,1536]{1,0:T(8,128)(2,1)S(1)}, bf16[256,1536]{1,0:T(8,128)(2,1)S(1)}, u32[]{:S(2)}, u32[]{:S(2)}) collective-permute-start(bf16[256,1536]{1,0:T(8,128)(2,1)S(1)} %pad_maximum_fusion), channel_id=1, source_target_pairs={{0,16},{16,0},{32,48},{48,32},{64,80},{80,64},{96,112},{112,96},{1... | collective-permute-start | bytes 2359304 | tf_op jit(solution)/shard_map/ppermute | solution.py:29
  70.2 7.1 %copy-start.12 = (bf16[256,1024]{1,0:T(8,128)(2,1)S(1)}, bf16[256,1024]{1,0:T(8,128)(2,1)}, u32[]{:S(2)}) copy-start(bf16[256,1024]{1,0:T(8,128)(2,1)} %copy-done.11) | copy-start | bytes 1572868
  71.3 15.5 %copy-start.17 = (bf16[768,1024]{1,0:T(8,128)(2,1)}, bf16[768,1024]{1,0:T(8,128)(2,1)S(1)}, u32[]{:S(2)}) copy-start(bf16[768,1024]{1,0:T(8,128)(2,1)S(1)} %convolution_convert_fusion.3) | copy-start | bytes 4718596
  71.3 15.5 %copy-start.10 = (bf16[256,1024]{1,0:T(8,128)(2,1)S(1)}, bf16[256,1024]{1,0:T(8,128)(2,1)}, u32[]{:S(2)}) copy-start(bf16[256,1024]{1,0:T(8,128)(2,1)} %copy-done.9) | copy-start | bytes 1572868
  71.4 8.5 %collective-permute-start.8 = (bf16[384,128]{1,0:T(8,128)(2,1)S(1)}, bf16[384,128]{1,0:T(8,128)(2,1)S(1)}, u32[]{:S(2)}, u32[]{:S(2)}) collective-permute-start(bf16[384,128]{1,0:T(8,128)(2,1)S(1)} %get-tuple-element.52), channel_id=1, source_target_pairs={{0,224},{16,240},{32,0},{48,16},{64,32},{80,48},{96,64},{112,80},{... | collective-permute-start | bytes 294920 | tf_op jit(solution)/shard_map/ppermute | solution.py:34
  77.3 6.0 %collective-permute-start.4 = (bf16[384,128]{1,0:T(8,128)(2,1)S(1)}, bf16[384,128]{1,0:T(8,128)(2,1)S(1)}, u32[]{:S(2)}, u32[]{:S(2)}) collective-permute-start(bf16[384,128]{1,0:T(8,128)(2,1)S(1)} %get-tuple-element.54), channel_id=1, source_target_pairs={{0,32},{16,48},{32,64},{48,80},{64,96},{80,112},{96,128},{112,144}... | collective-permute-start | bytes 294920 | tf_op jit(solution)/shard_map/ppermute | solution.py:34
  77.3 9.5 %collective-permute-start = (bf16[256,1024]{1,0:T(8,128)(2,1)S(1)}, bf16[256,1024]{1,0:T(8,128)(2,1)S(1)}, u32[]{:S(2)}, u32[]{:S(2)}) collective-permute-start(bf16[256,1024]{1,0:T(8,128)(2,1)S(1)} %copy-done.12), channel_id=1, source_target_pairs={{0,16},{16,0},{32,48},{48,32},{64,80},{80,64},{96,112},{112,96},{1... | collective-permute-start | bytes 1572872 | tf_op jit(solution)/shard_map/ppermute | solution.py:29
  84.0 30.9 %collective-permute-start.9 = (bf16[768,128]{1,0:T(8,128)(2,1)}, bf16[768,128]{1,0:T(8,128)(2,1)S(1)}, u32[]{:S(2)}, u32[]{:S(2)}) collective-permute-start(bf16[768,128]{1,0:T(8,128)(2,1)} %pad_maximum_fusion.4), channel_id=1, source_target_pairs={{0,224},{16,240},{32,0},{48,16},{64,32},{80,48},{96,64},{112,80},{... | collective-permute-start | bytes 589832 | tf_op jit(solution)/shard_map/ppermute | solution.py:34
  85.0 29.9 %collective-permute-start.5 = (bf16[768,128]{1,0:T(8,128)(2,1)}, bf16[768,128]{1,0:T(8,128)(2,1)}, u32[]{:S(2)}, u32[]{:S(2)}) collective-permute-start(bf16[768,128]{1,0:T(8,128)(2,1)} %pad_maximum_fusion.3), channel_id=1, source_target_pairs={{0,32},{16,48},{32,64},{48,80},{64,96},{80,112},{96,128},{112,144}... | collective-permute-start | bytes 589832 | tf_op jit(solution)/shard_map/ppermute | solution.py:34
  86.8 4.0 %copy-start.14 = (bf16[1,2048,768]{2,1,0:T(8,128)(2,1)S(1)}, bf16[1,2048,768]{2,1,0:T(8,128)(2,1)}, u32[]{:S(2)}) copy-start(bf16[1,2048,768]{2,1,0:T(8,128)(2,1)} %param.11) | copy-start | bytes 9437188
  88.6 8.5 %copy-start.15 = (bf16[1024,1536]{1,0:T(8,128)(2,1)}, bf16[1024,1536]{1,0:T(8,128)(2,1)S(1)}, u32[]{:S(2)}) copy-start(bf16[1024,1536]{1,0:T(8,128)(2,1)S(1)} %convolution_convert_fusion) | copy-start | bytes 9437188
  88.7 5.8 %collective-permute-start.16 = (bf16[128,768]{1,0:T(8,128)(2,1)S(1)}, bf16[128,768]{1,0:T(8,128)(2,1)S(1)}, u32[]{:S(2)}, u32[]{:S(2)}) collective-permute-start(bf16[128,768]{1,0:T(8,128)(2,1)S(1)} %get-tuple-element.40), channel_id=1, source_target_pairs={{0,224},{16,240},{32,0},{48,16},{64,32},{80,48},{96,64},{112,80},{... | collective-permute-start | bytes 589832 | tf_op jit(solution)/shard_map/ppermute | solution.py:34
  90.3 6.9 %collective-permute-start.12 = (bf16[128,768]{1,0:T(8,128)(2,1)S(1)}, bf16[128,768]{1,0:T(8,128)(2,1)S(1)}, u32[]{:S(2)}, u32[]{:S(2)}) collective-permute-start(bf16[128,768]{1,0:T(8,128)(2,1)S(1)} %get-tuple-element.42), channel_id=1, source_target_pairs={{0,32},{16,48},{32,64},{48,80},{64,96},{80,112},{96,128},{112,144}... | collective-permute-start | bytes 589832 | tf_op jit(solution)/shard_map/ppermute | solution.py:34
  98.0 13.1 %collective-permute-start.17 = (bf16[128,1536]{1,0:T(8,128)(2,1)}, bf16[128,1536]{1,0:T(8,128)(2,1)}, u32[]{:S(2)}, u32[]{:S(2)}) collective-permute-start(bf16[128,1536]{1,0:T(8,128)(2,1)} %pad_maximum_fusion.2), channel_id=1, source_target_pairs={{0,224},{16,240},{32,0},{48,16},{64,32},{80,48},{96,64},{112,80},{... | collective-permute-start | bytes 1179656 | tf_op jit(solution)/shard_map/ppermute | solution.py:34
  99.0 12.2 %collective-permute-start.13 = (bf16[128,1536]{1,0:T(8,128)(2,1)}, bf16[128,1536]{1,0:T(8,128)(2,1)}, u32[]{:S(2)}, u32[]{:S(2)}) collective-permute-start(bf16[128,1536]{1,0:T(8,128)(2,1)} %pad_maximum_fusion.1), channel_id=1, source_target_pairs={{0,32},{16,48},{32,64},{48,80},{64,96},{80,112},{96,128},{112,144}... | collective-permute-start | bytes 1179656 | tf_op jit(solution)/shard_map/ppermute | solution.py:34
  105.2 29.8 %all-to-all-start.2 = ((bf16[16,24,2048]{2,1,0:T(8,128)(2,1)}), bf16[16,24,2048]{2,1,0:T(8,128)(2,1)}, u32[]{:S(2)}, u32[]{:S(2)}) async-start(bf16[16,24,2048]{2,1,0:T(8,128)(2,1)} %bitcast.51), calls=%async_computation.2 | async-start | bytes 3145728 | tf_op jit(solution)/shard_map/all_to_all | solution.py:186
  111.1 3.8 %copy-start.18 = (bf16[768,1024]{1,0:T(8,128)(2,1)S(1)}, bf16[768,1024]{1,0:T(8,128)(2,1)}, u32[]{:S(2)}) copy-start(bf16[768,1024]{1,0:T(8,128)(2,1)} %copy-done.17) | copy-start | bytes 4718596
  112.8 9.9 %collective-permute-start.18 = (bf16[128,1536]{1,0:T(8,128)(2,1)S(1)}, bf16[128,1536]{1,0:T(8,128)(2,1)S(1)}, u32[]{:S(2)}, u32[]{:S(2)}) collective-permute-start(bf16[128,1536]{1,0:T(8,128)(2,1)S(1)} %get-tuple-element.37), channel_id=1, source_target_pairs={{0,224},{16,240},{32,0},{48,16},{64,32},{80,48},{96,64},{112,80},{... | collective-permute-start | bytes 1179656 | tf_op jit(solution)/shard_map/ppermute | solution.py:34
  114.2 20.8 %copy-start.6 = (bf16[384,128]{1,0:T(8,128)(2,1)S(1)}, bf16[384,128]{1,0:T(8,128)(2,1)}, u32[]{:S(2)}) copy-start(bf16[384,128]{1,0:T(8,128)(2,1)} %copy-done.5) | copy-start | bytes 294916
  114.2 11.3 %collective-permute-start.14 = (bf16[128,1536]{1,0:T(8,128)(2,1)S(1)}, bf16[128,1536]{1,0:T(8,128)(2,1)S(1)}, u32[]{:S(2)}, u32[]{:S(2)}) collective-permute-start(bf16[128,1536]{1,0:T(8,128)(2,1)S(1)} %get-tuple-element.38), channel_id=1, source_target_pairs={{0,32},{16,48},{32,64},{48,80},{64,96},{80,112},{96,128},{112,144}... | collective-permute-start | bytes 1179656 | tf_op jit(solution)/shard_map/ppermute | solution.py:34
  116.0 15.0 %collective-permute-start.10 = (bf16[768,128]{1,0:T(8,128)(2,1)S(1)}, bf16[768,128]{1,0:T(8,128)(2,1)S(1)}, u32[]{:S(2)}, u32[]{:S(2)}) collective-permute-start(bf16[768,128]{1,0:T(8,128)(2,1)S(1)} %get-tuple-element.49), channel_id=1, source_target_pairs={{0,224},{16,240},{32,0},{48,16},{64,32},{80,48},{96,64},{112,80},{... | collective-permute-start | bytes 589832 | tf_op jit(solution)/shard_map/ppermute | solution.py:34
  118.6 12.4 %collective-permute-start.6 = (bf16[768,128]{1,0:T(8,128)(2,1)S(1)}, bf16[768,128]{1,0:T(8,128)(2,1)S(1)}, u32[]{:S(2)}, u32[]{:S(2)}) collective-permute-start(bf16[768,128]{1,0:T(8,128)(2,1)S(1)} %get-tuple-element.50), channel_id=1, source_target_pairs={{0,32},{16,48},{32,64},{48,80},{64,96},{80,112},{96,128},{112,144}... | collective-permute-start | bytes 589832 | tf_op jit(solution)/shard_map/ppermute | solution.py:34
  127.7 12.7 %collective-permute-start.15 = (bf16[128,1536]{1,0:T(8,128)(2,1)}, bf16[128,1536]{1,0:T(8,128)(2,1)}, u32[]{:S(2)}, u32[]{:S(2)}) collective-permute-start(bf16[128,1536]{1,0:T(8,128)(2,1)} %get-tuple-element.36), channel_id=1, source_target_pairs={{0,32},{16,48},{32,64},{48,80},{64,96},{80,112},{96,128},{112,144}... | collective-permute-start | bytes 1179656 | tf_op jit(solution)/shard_map/ppermute | solution.py:34
  127.7 12.7 %collective-permute-start.19 = (bf16[128,1536]{1,0:T(8,128)(2,1)}, bf16[128,1536]{1,0:T(8,128)(2,1)}, u32[]{:S(2)}, u32[]{:S(2)}) collective-permute-start(bf16[128,1536]{1,0:T(8,128)(2,1)} %get-tuple-element.35), channel_id=1, source_target_pairs={{0,224},{16,240},{32,0},{48,16},{64,32},{80,48},{96,64},{112,80},{... | collective-permute-start | bytes 1179656 | tf_op jit(solution)/shard_map/ppermute | solution.py:34
  131.7 8.6 %collective-permute-start.7 = (bf16[768,128]{1,0:T(8,128)(2,1)}, bf16[768,128]{1,0:T(8,128)(2,1)}, u32[]{:S(2)}, u32[]{:S(2)}) collective-permute-start(bf16[768,128]{1,0:T(8,128)(2,1)} %get-tuple-element.48), channel_id=1, source_target_pairs={{0,32},{16,48},{32,64},{48,80},{64,96},{80,112},{96,128},{112,144}... | collective-permute-start | bytes 589832 | tf_op jit(solution)/shard_map/ppermute | solution.py:34
  131.7 8.6 %collective-permute-start.11 = (bf16[768,128]{1,0:T(8,128)(2,1)S(1)}, bf16[768,128]{1,0:T(8,128)(2,1)}, u32[]{:S(2)}, u32[]{:S(2)}) collective-permute-start(bf16[768,128]{1,0:T(8,128)(2,1)S(1)} %get-tuple-element.47), channel_id=1, source_target_pairs={{0,224},{16,240},{32,0},{48,16},{64,32},{80,48},{96,64},{112,80},{... | collective-permute-start | bytes 589832 | tf_op jit(solution)/shard_map/ppermute | solution.py:34
where the time goes:
time: 145 us; the launch traced here: 144 us
  waiting for transfers between devices  47.9 us (33%)
  starting transfers between devices  44.1 us (30%)
  matrix products  20.3 us (14%)
  other arithmetic  12.1 us (8%)
  Pallas kernels  9.6 us (7%)
  local copies, waits for them, and re-layouts  9.47 us (7%)
    all_to_all x3, waiting for transfers between devices, exchange(): lax.all_to_all(shaped, 'expert', 0, 0, tiled=True).reshape(padded, width)  27.1 us
    ppermute x16, starting transfers between devices, next_chip(): lax.ppermute(array, 'dp', [(i, (i + 2 * sign) % size) for i in range(size)])  23.3 us
    all_to_all x3, starting transfers between devices, exchange(): lax.all_to_all(shaped, 'expert', 0, 0, tiled=True).reshape(padded, width)  20 us
    ppermute x16, waiting for transfers between devices, next_chip(): lax.ppermute(array, 'dp', [(i, (i + 2 * sign) % size) for i in range(size)])  19.6 us
    dot_general x4, matrix products, dot_tn(): lax.dot_general(left, right, (((0,), (0,)), ((), ())), preferred_element_...  9.89 us
    pallas_call x5, Pallas kernels, call(): pl.pallas_call(kernel, out_shape=out_shapes, in_specs=in_specs, out_specs...  9.6 us
    unnamed x40, local copies, waits for them, and re-layouts  6.94 us
    dot_general x2, matrix products, dot_nt(): lax.dot_general(left, right, (((1,), (1,)), ((), ())), preferred_element_...  6.62 us
  transfers between devices with their start and end apart: 23, of which 10 were waited for; matrix products, arithmetic and copies ran while one was open for 21% of the time, Pallas kernels for 3%

commit v1 on v0

--- a/solution.py
+++ b/solution.py
@@ -34,40 +34,101 @@
     return lax.ppermute(array, "dp", [(i, (i + 2 * sign) % size) for i in range(size)])
 
 
-def add(left, right):
-    return (left.astype(F32) + right.astype(F32)).astype(BF16)
-
-
-def two_way_sums(chunk_of, chips, axis):
-    far = chips // 2
-
-    def split(chunk):
-        return jnp.split(chunk, 2, axis=axis)
-
-    forward = next_chip(split(chunk_of(far))[0], 1)
-    backward = next_chip(split(chunk_of(-far))[1], -1)
-    for distance in range(far - 1, 0, -1):
-        front, back = chunk_of(distance), chunk_of(-distance)
-        if distance == far - 1:
-            first, second = split(front)
-            front = jnp.concatenate([add(forward, first), second], axis=axis)
-            first, second = split(back)
-            back = jnp.concatenate([first, add(backward, second)], axis=axis)
-        else:
-            front, back = add(forward, front), add(backward, back)
-        forward, backward = next_chip(front, 1), next_chip(back, -1)
-    return forward, backward
-
-
-def finish_sums(own, forward, backward, axis):
-    total = own.astype(F32)
-    if forward.shape == own.shape:
-        return (total + forward.astype(F32) + backward.astype(F32)).astype(BF16)
-    arrived = jnp.concatenate([forward, backward], axis=axis)
-    return (total + arrived.astype(F32)).astype(BF16)
-
-
-def select_kernel(most, base_ref, picks_ref, tokens_ref, select_ref, out_ref):
+def f32_sum(*terms):
+    total = terms[0].astype(F32)
+    for term in terms[1:]:
+        total = total + term.astype(F32)
+    return total.astype(BF16)
+
+
+def halves_of(shape, axis):
+    half = shape[axis] // 2
+    full = [slice(None)] * len(shape)
+    first, second = list(full), list(full)
+    first[axis], second[axis] = slice(0, half), slice(half, 2 * half)
+    return tuple(first), tuple(second)
+
+
+def join_kernel(axis, forward_ref, backward_ref, front_ref, back_ref, front_out, back_out):
+    first, second = halves_of(front_ref.shape, axis)
+    front_out[first] = f32_sum(forward_ref[...], front_ref[first])
+    front_out[second] = front_ref[second]
+    back_out[first] = back_ref[first]
+    back_out[second] = f32_sum(backward_ref[...], back_ref[second])
+
+
+def add_kernel(forward_ref, backward_ref, front_ref, back_ref, front_out, back_out):
+    front_out[...] = f32_sum(forward_ref[...], front_ref[...])
+    back_out[...] = f32_sum(backward_ref[...], back_ref[...])
+
+
+def finish_kernel(axis, forward_ref, backward_ref, own_ref, *out_refs):
+    forward, backward = forward_ref[...], backward_ref[...]
+    if forward.shape != own_ref.shape:
+        both = jnp.concatenate([forward, backward], axis=axis)
+        total = f32_sum(own_ref[...], both)
+    else:
+        total = f32_sum(own_ref[...], forward, backward)
+    for index, out_ref in enumerate(out_refs):
+        extent = out_ref.shape[2]
+        out_ref[0] = total[:, index * extent : (index + 1) * extent]
+
+
+class Sums:
+    def __init__(self, part, chunk_shape, axis, chips):
+        self.part, self.chunk, self.axis, self.chips = part, chunk_shape, axis, chips
+        self.across = chunk_shape[0] == part.shape[0]
+        self.distance = chips // 2
+
+    def slice(self, away):
+        place = away % self.chips
+        if self.across:
+            return self.part[:, place * self.chunk[1] : (place + 1) * self.chunk[1]]
+        return self.part[place * self.chunk[0] : (place + 1) * self.chunk[0]]
+
+    def spec(self, away):
+        place = away % self.chips
+        return pl.BlockSpec(self.chunk, lambda step: (0, place) if self.across else (place, 0))
+
+    def send(self, front, back):
+        self.moving = (next_chip(front, 1), next_chip(back, -1))
+
+    def first(self):
+        first, second = halves_of(self.chunk, self.axis)
+        chunk = self.slice(self.distance)
+        self.send(chunk[first], chunk[second])
+
+    def combine(self, after=None):
+        arrived = self.moving
+        if after is not None:
+            arrived, _ = lax.optimization_barrier((arrived, after))
+        kernel = add_kernel
+        if self.distance == self.chips // 2:
+            kernel = lambda *refs: join_kernel(self.axis, *refs)
+        self.distance -= 1
+        out = jax.ShapeDtypeStruct(self.chunk, BF16)
+        size = self.chunk[0] * self.chunk[1]
+        return call(
+            kernel,
+            (out, out),
+            [VMEM, VMEM, self.spec(self.distance), self.spec(-self.distance)],
+            (*arrived, self.part, self.part),
+            8, 1, 1, (1,),
+        )
+
+    def finish(self, out_shapes, after):
+        arrived, _ = lax.optimization_barrier((self.moving, after))
+        size = self.chunk[0] * self.chunk[1]
+        return call(
+            lambda *refs: finish_kernel(self.axis, *refs),
+            out_shapes,
+            [VMEM, VMEM, self.spec(0)],
+            (*arrived, self.part),
+            8, 1, 1, (1,),
+        )
+
+
+def select_kernel(most, base_ref, picks_ref, tokens_ref, select_ref, turned_ref, out_ref):
     local = picks_ref[...] - base_ref[0]
     experts, slots = local.shape
     tok_dev = tokens_ref.shape[0]
@@ -81,8 +142,10 @@
     hit = (position == wanted) & (spread >= 0) & (spread < tok_dev)
     token = jnp.sum(jnp.where(hit, spread + 1, 0).astype(F32), axis=1, keepdims=True) - 1.0
     token_range = lax.broadcasted_iota(I32, (spread.shape[0], tok_dev), 1).astype(F32)
-    select = (token_range == token).astype(F32).astype(BF16)
+    hot = (token_range == token).astype(F32)
+    select = hot.astype(BF16)
     select_ref[...] = select
+    turned_ref[...] = hot.T.astype(BF16)
     out_ref[...] = dot_nn(select, tokens_ref[...]).astype(BF16)
 
 
@@ -90,7 +153,7 @@
     out_ref[...] = dot_nn(select_ref[...], tokens_ref[...]).astype(BF16)
 
 
-def take_kernel(most, tok_dev, own_ref, take_ref):
+def take_kernel(most, tok_dev, own_ref, take_ref, turned_ref):
     slots, columns = take_ref.shape
     lane = lax.broadcasted_iota(I32, (1, columns), 1)
     source = jnp.zeros((1, columns), I32)
@@ -103,7 +166,9 @@
     slot = start + within.astype(F32)
     slot = jnp.where(slot < stop, slot, -1.0)
     slot_range = lax.broadcasted_iota(I32, (slots, columns), 0).astype(F32)
-    take_ref[...] = (slot_range == slot).astype(F32).astype(BF16)
+    hot = (slot_range == slot).astype(F32)
+    take_ref[...] = hot.astype(BF16)
+    turned_ref[...] = hot.T.astype(BF16)
 
 
 def compact_kernel(chips, place_ref, take_ref, arrived_ref, scale_ref, full_ref, keep_ref, give_ref):
@@ -115,28 +180,47 @@
         full_ref[:, columns] = value.astype(BF16)
         if scale_ref is not None:
             value = value * scale_ref[...]
-        value = value.astype(BF16)
         even, odd = value[:, :block], value[:, block:]
         where = pl.ds(pl.multiple_of(lax.rem(k - chip + chips, chips) * block, block), block)
 
-        @pl.when(core == 0)
-        def _():
-            keep_ref[:, where] = even
-            give_ref[:, where] = odd
-
-        @pl.when(core != 0)
-        def _():
-            keep_ref[:, where] = odd
-            give_ref[:, where] = even
+        keep_ref[:, where] = jnp.where(core == 0, even, odd).astype(BF16)
+        give_ref[:, where] = jnp.where(core == 0, odd, even).astype(BF16)
 
 
 def plain_compact_kernel(chips, place_ref, take_ref, arrived_ref, full_ref, keep_ref, give_ref):
     compact_kernel(chips, place_ref, take_ref, arrived_ref, None, full_ref, keep_ref, give_ref)
 
 
-def call(kernel, out_shapes, in_specs, operands, limit_mib, flops, bytes_accessed):
+def grad_kernel(
+    tile, grads_ref, down_ref, gate_ref, hidden_ref, slope_ref, activated_ref, pre_ref, slot_ref
+):
+    hidden_width = down_ref.shape[0]
+    total = jnp.zeros(slot_ref.shape, F32)
+    for begin in range(0, hidden_width, tile):
+        columns = slice(begin, begin + tile)
+        raw = dot_nt(grads_ref[...], down_ref[columns, :])
+        total = total + jnp.sum(raw * hidden_ref[:, columns].astype(F32), axis=1, keepdims=True)
+        scaled = raw * gate_ref[...]
+        pre_ref[:, columns] = (scaled * slope_ref[:, columns]).astype(BF16)
+        other = slice(hidden_width + begin, hidden_width + begin + tile)
+        pre_ref[:, other] = (scaled * activated_ref[:, columns]).astype(BF16)
+    slot_ref[...] = total
+
+
+def return_kernel(tile, pre_ref, gate_ref, up_ref, turned_ref, out_ref):
+    width, hidden_width = gate_ref.shape
+    for begin in range(0, width, tile):
+        columns = slice(begin, begin + tile)
+        row_grads = dot_nt(pre_ref[:, :hidden_width], gate_ref[columns, :]) + dot_nt(
+            pre_ref[:, hidden_width:], up_ref[columns, :]
+        )
+        out_ref[:, columns] = dot_nn(turned_ref[...], row_grads.astype(BF16)).astype(BF16)
+
+
+def call(kernel, out_shapes, in_specs, operands, limit_mib, flops, bytes_accessed, grid=()):
     return pl.pallas_call(
         kernel,
+        grid=grid,
         out_shape=out_shapes,
         in_specs=in_specs,
         out_specs=jax.tree.map(lambda _: VMEM, out_shapes),
@@ -166,9 +250,9 @@
 
     table = picks[0]
     base = (self_index * tok_dev).astype(I32).reshape(1)
-    select, out_rows = call(
+    select, select_turned, out_rows = call(
         lambda *refs: select_kernel(most, *refs),
-        (shape(padded, tok_dev), shape(padded, width)),
+        (shape(padded, tok_dev), shape(tok_dev, padded), shape(padded, width)),
         [SMEM, VMEM, VMEM],
         (base, table, tokens),
         16, 2 * padded * tok_dev * width, 4 * padded * width,
@@ -189,9 +273,9 @@
     arrived_grads = exchange(out_grads)
 
     own = lax.dynamic_index_in_dim(table, self_index, 0, keepdims=False)
-    take = call(
+    take, take_turned = call(
         lambda *refs: take_kernel(most, tok_dev, *refs),
-        shape(slot_count, padded),
+        (shape(slot_count, padded), shape(padded, slot_count)),
         [VMEM],
         (own.reshape(slot_count, 1),),
         8, 8 * slot_count * padded, 2 * slot_count * padded,
@@ -199,7 +283,7 @@
     compact_shapes = (
         shape(slot_count, width), shape(slot_count, width // 2), shape(slot_count, width // 2)
     )
-    compact_cost = (24, 2 * slot_count * padded * width, 8 * slot_count * width)
+    compact_cost = (12, 2 * slot_count * padded * width, 8 * slot_count * width)
     rows, rows_keep, rows_give = call(
         lambda *refs: plain_compact_kernel(chips, *refs),
         compact_shapes,
@@ -225,45 +309,70 @@
         *compact_cost,
     )
     scaled_both = jnp.concatenate([scaled_keep, swap_cores(scaled_give)], axis=0)
-    raw_grad = dot_nt(grads, w_down[0])
-    slot_grads = jnp.sum(raw_grad * hidden.astype(F32), axis=1)
-    hidden_grad = gate_rows * raw_grad
-    gate_pre_grad = (hidden_grad * slope).astype(BF16)
-    up_pre_grad = (hidden_grad * activated).astype(BF16)
-    pre_grads = jnp.concatenate([gate_pre_grad, up_pre_grad], axis=1)
+    pre_grads, slot_grads = call(
+        lambda *refs: grad_kernel(min(256, hidden_width), *refs),
+        (shape(slot_count, 2 * hidden_width), shape(slot_count, 1, dtype=F32)),
+        [VMEM] * 6,
+        (grads, w_down[0], gate_rows, hidden, slope, activated),
+        16, 2 * slot_count * width * hidden_width, 2 * width * hidden_width,
+    )
     pre_both = jnp.concatenate([pre_grads, swap_cores(pre_grads)], axis=0)
     down_part = dot_tn(hidden_both, scaled_both).astype(BF16)
     pre_part = dot_tn(rows_both, pre_both).astype(BF16)
 
-    def down_chunk(away):
-        return down_part[:, away % chips * block : (away % chips + 1) * block]
-
-    def pre_chunk(away):
-        return pre_part[away % chips * block : (away % chips + 1) * block]
-
+    def give_back(pre_grads):
+        return call(
+            lambda *refs: return_kernel(min(256, width), *refs),
+            shape(padded, width),
+            [VMEM] * 4,
+            (pre_grads, w_gate[0], w_up[0], take_turned),
+            16, 4 * slot_count * width * hidden_width, 4 * width * hidden_width,
+        )
+
+    def collect(came_back):
+        return call(
+            gather_kernel,
+            shape(tok_dev, width),
+            [VMEM, VMEM],
+            (select_turned, came_back),
+            12, 2 * padded * tok_dev * width, 4 * padded * width,
+        )
+
+    down_shape = (shape(1, hidden_width, block),)
+    pre_shape = (shape(1, block, hidden_width), shape(1, block, hidden_width))
     if chips > 1:
-        down_sums = two_way_sums(down_chunk, chips, 0)
-        pre_sums = two_way_sums(pre_chunk, chips, 1)
-        pre_grads, _ = lax.optimization_barrier((pre_grads, pre_part))
-
-    gate_pre_grad, up_pre_grad = jnp.split(pre_grads, 2, axis=1)
-    row_grads = (dot_nt(gate_pre_grad, w_gate[0]) + dot_nt(up_pre_grad, w_up[0])).astype(BF16)
-    token_grads = dot_tn(select, exchange(dot_tn(take, row_grads).astype(BF16))).astype(BF16)
-
-    if chips > 1:
-        token_grads, down_sums, pre_sums = lax.optimization_barrier(
-            (token_grads, down_sums, pre_sums)
-        )
-        grad_down = finish_sums(down_chunk(0), *down_sums, 0)
-        grad_pre = finish_sums(pre_chunk(0), *pre_sums, 1)
+        down = Sums(down_part, (hidden_width, block), 0, chips)
+        pre = Sums(pre_part, (block, 2 * hidden_width), 1, chips)
+        down.first()
+        pre.first()
+        returned = None
+        held, _ = lax.optimization_barrier((pre_grads, pre_part))
+        returning = give_back(held)
+        latest = pre_grads
+        while down.distance > 1:
+            down_next = down.combine(latest)
+            if down.distance == chips // 2 - 2:
+                returning, _ = lax.optimization_barrier((returning, down_next))
+                returned = exchange(returning)
+            down.send(*down_next)
+            pre_next = pre.combine(down_next)
+            pre.send(*pre_next)
+            latest = pre_next
+        if returned is None:
+            returned = exchange(returning)
+        returned, _ = lax.optimization_barrier((returned, latest))
+        token_grads = collect(returned)
+        grad_down = down.finish(down_shape, token_grads)
+        grad_pre = pre.finish(pre_shape, token_grads)
     else:
-        grad_down, grad_pre = down_part, pre_part
+        token_grads = collect(exchange(give_back(pre_grads)))
+        grad_down = (down_part[None],)
+        grad_pre = tuple(half[None] for half in jnp.split(pre_part, 2, axis=1))
     return (
         token_grads,
-        slot_grads[None, None],
-        grad_pre[None, :, :hidden_width],
-        grad_pre[None, :, hidden_width:],
-        grad_down[None],
+        slot_grads.reshape(1, 1, slot_count),
+        *grad_pre,
+        *grad_down,
     )
 
 

time: 145 us -> 149 us (1.028)
  matrix products: 20.3 us -> 7.35 us
  Pallas kernels: 9.6 us -> 20.7 us
  other arithmetic: 12.1 us -> 1.65 us
  starting transfers between devices: 44.1 us -> 50.3 us
  local copies, waits for them, and re-layouts: 9.47 us -> 14.4 us
  waiting for transfers between devices: 47.9 us -> 52.6 us
    pallas_call x5 -> x16, Pallas kernels: 9.6 us -> 20.7 us  [call(): pl.pallas_call(kernel, grid=grid, out_shape=out_shapes, in_specs=in_specs...]
    convert_element_type x7 -> x0, other arithmetic: 7.2 us -> none  [the longest x6 5.82 us: add(): return (left.astype(F32) + right.astype(F32)).astype(BF16)]
    dot_general x4 -> x2, matrix products: 9.89 us -> 2.85 us  [dot_tn(): lax.dot_general(left, right, (((0,), (0,)), ((), ())), preferred_element_...]
    dot_general x2 -> x0, matrix products: 6.62 us -> none  [dot_nt(): lax.dot_general(left, right, (((1,), (1,)), ((), ())), preferred_element_...]
    ppermute x16, starting transfers between devices: 23.3 us -> 29.2 us  [next_chip(): lax.ppermute(array, 'dp', [(i, (i + 2 * sign) % size) for i in range(size)])]
    unnamed x40 -> x58, local copies, waits for them, and re-layouts: 6.94 us -> 12.7 us
    all_to_all x3, waiting for transfers between devices: 27.1 us -> 31.9 us  [exchange(): lax.all_to_all(shaped, 'expert', 0, 0, tiled=True).reshape(padded, width)]
    concatenate x5 -> x0, other arithmetic: 2.99 us -> none  [the longest x2 1.47 us: two_way_sums(): front = jnp.concatenate([add(forward, first), second], axis=axis)]
  transfers between devices with their start and end apart: 23 -> 23, of which waited for: 10 -> 6; matrix products, arithmetic and copies ran while one was open for 21% -> 6% of each run, Pallas kernels for 3% -> 9%
where the time goes in v1:
time: 149 us; the launch traced here: 148 us
  waiting for transfers between devices  52.6 us (35%)
  starting transfers between devices  50.3 us (34%)
  Pallas kernels  20.7 us (14%)
  local copies, waits for them, and re-layouts  14.4 us (10%)
  matrix products  7.35 us (5%)
  other arithmetic  1.65 us (1%)
    all_to_all x3, waiting for transfers between devices, exchange(): lax.all_to_all(shaped, 'expert', 0, 0, tiled=True).reshape(padded, width)  31.9 us
    ppermute x16, starting transfers between devices, next_chip(): lax.ppermute(array, 'dp', [(i, (i + 2 * sign) % size) for i in range(size)])  29.2 us
    pallas_call x16, Pallas kernels, call(): pl.pallas_call(kernel, grid=grid, out_shape=out_shapes, in_specs=in_specs...  20.7 us
    ppermute x16, waiting for transfers between devices, next_chip(): lax.ppermute(array, 'dp', [(i, (i + 2 * sign) % size) for i in range(size)])  20.7 us
    all_to_all x3, starting transfers between devices, exchange(): lax.all_to_all(shaped, 'expert', 0, 0, tiled=True).reshape(padded, width)  19.9 us
    unnamed x58, local copies, waits for them, and re-layouts  12.7 us
    dot_general x2, matrix products, dot_nn(): return jnp.dot(left, right, preferred_element_type=F32)  4.5 us
  transfers between devices with their start and end apart: 23, of which 6 were waited for; matrix products, arithmetic and copies ran while one was open for 6% of the time, Pallas kernels for 9%

profile of v1, /device:TPU:2, one launch (start us, length us, event | category | flops | bytes accessed | tf_op | source)
XLA Modules:
  0.0 148.0 jit_solution(2595776788333976455)
XLA Ops:
  0.7 0.8 copy-done.15
  1.4 1.0 copy-done.18
  2.5 2.2 %shard_map.110 = (bf16[384,128]{1,0:T(8,128)(2,1)S(1)}, bf16[128,384]{1,0:T(8,128)(2,1)S(1)}, bf16[384,2048]{1,0:T(8,128)(2,1)}) custom-call(s32[1]{0:T(128)} %bitcast.refs_0_, s32[16,256]{1,0:T(8,128)S(1)} %bitcast.32, bf16[128,2048]{1,0:T(8,128)(2,1)S(1)} %copy-done.18), custom_call_target="tpu_custom_call" | custom-call | flops 201326592 | bytes 3145728 | tf_op jit(solution)/shard_map/pallas_call | solution.py:221
  5.3 7.5 %all-to-all-start.1 = ((bf16[16,24,2048]{2,1,0:T(8,128)(2,1)}), bf16[16,24,2048]{2,1,0:T(8,128)(2,1)S(1)}, u32[]{:S(2)}, u32[]{:S(2)}) async-start(bf16[16,24,2048]{2,1,0:T(8,128)(2,1)} %bitcast.9), calls=%async_computation.1 | async-start | bytes 3145728 | tf_op jit(solution)/shard_map/all_to_all | solution.py:270
  13.3 1.2 copy-done.3
  14.5 19.7 %all-to-all-done.1 = bf16[16,24,2048]{2,1,0:T(8,128)(2,1)S(1)} async-done(((bf16[16,24,2048]{2,1,0:T(8,128)(2,1)}), bf16[16,24,2048]{2,1,0:T(8,128)(2,1)S(1)}, u32[]{:S(2)}, u32[]{:S(2)}) %all-to-all-start.1) | async-done | bytes 1572896 | tf_op jit(solution)/shard_map/all_to_all | solution.py:270
  34.2 6.3 %all-to-all-start = ((bf16[16,24,2048]{2,1,0:T(8,128)(2,1)}), bf16[16,24,2048]{2,1,0:T(8,128)(2,1)S(1)}, u32[]{:S(2)}, u32[]{:S(2)}) async-start(bf16[16,24,2048]{2,1,0:T(8,128)(2,1)} %bitcast.27), calls=%async_computation | async-start | bytes 3145728 | tf_op jit(solution)/shard_map/all_to_all | solution.py:270
  40.4 0.7 dynamic-slice_bitcast_fusion
  41.1 0.8 copy.12.refs_0_
  42.1 0.9 copy-done.8
  43.3 0.7 copy-done.10
  44.0 1.4 shard_map.114
  45.4 1.0 copy-done.16
  46.4 0.8 copy-done.19
  47.2 0.8 copy-done.21
  48.0 12.2 %all-to-all-done = bf16[16,24,2048]{2,1,0:T(8,128)(2,1)S(1)} async-done(((bf16[16,24,2048]{2,1,0:T(8,128)(2,1)}), bf16[16,24,2048]{2,1,0:T(8,128)(2,1)S(1)}, u32[]{:S(2)}, u32[]{:S(2)}) %all-to-all-start) | async-done | bytes 1572896 | tf_op jit(solution)/shard_map/all_to_all | solution.py:270
  60.2 1.4 shard_map.113
  61.7 3.3 %fusion.15 = f32[256,768]{1,0:T(8,128)S(1)} fusion(bf16[256,2048]{1,0:T(8,128)(2,1)} %copy-done.16, bf16[1,2048,768]{2,1,0:T(8,128)(2,1)} %param.12), kind=kOutput, calls=%fused_computation.22 | convolution fusion | flops 805306368 | bytes 4980736 | tf_op jit(solution)/shard_map/dot_general | solution.py:16
  65.1 1.2 add_multiply_fusion
  67.0 1.2 shard_map.115
  69.4 1.0 convolution_convert_fusion.1.refs_2_.refs_3_.front_ref.back_ref
  70.5 2.0 %collective-permute-start.4 = (bf16[384,128]{1,0:T(8,128)(2,1)S(1)}, bf16[384,128]{1,0:T(8,128)(2,1)S(1)}, u32[]{:S(2)}, u32[]{:S(2)}) collective-permute-start(bf16[384,128]{1,0:T(8,128)(2,1)S(1)} %get-tuple-element.100), channel_id=1, source_target_pairs={{0,32},{16,48},{32,64},{48,80},{64,96},{80,112},{96,128},{112,144}... | collective-permute-start | bytes 294920 | tf_op jit(solution)/shard_map/ppermute | solution.py:34
  72.5 4.2 %collective-permute-start.5 = (bf16[384,128]{1,0:T(8,128)(2,1)S(1)}, bf16[384,128]{1,0:T(8,128)(2,1)S(1)}, u32[]{:S(2)}, u32[]{:S(2)}) collective-permute-start(bf16[384,128]{1,0:T(8,128)(2,1)S(1)} %get-tuple-element.99), channel_id=1, source_target_pairs={{0,224},{16,240},{32,0},{48,16},{64,32},{80,48},{96,64},{112,80},{... | collective-permute-start | bytes 294920 | tf_op jit(solution)/shard_map/ppermute | solution.py:34
  76.7 3.2 %collective-permute-done.4.refs_0_ = bf16[384,128]{1,0:T(8,128)(2,1)S(1)} collective-permute-done((bf16[384,128]{1,0:T(8,128)(2,1)S(1)}, bf16[384,128]{1,0:T(8,128)(2,1)S(1)}, u32[]{:S(2)}, u32[]{:S(2)}) %collective-permute-start.4) | collective-permute-done | bytes 98336 | tf_op jit(solution)/shard_map/ppermute | solution.py:34
  79.9 1.8 %convolution_convert_fusion.refs_2_.refs_3_.front_ref.back_ref = bf16[1024,1536]{1,0:T(8,128)(2,1)S(1)} fusion(bf16[256,1536]{1,0:T(8,128)(2,1)S(1)} %collective-permute-done.1, bf16[256,1536]{1,0:T(8,128)(2,1)S(1)} %get-tuple-element.60.refs_0_, bf16[256,1024]{1,0:T(8,128)(2,1)S(1)} %collective-permute-done, bf16[256,1024]{1,0:T(8,128)(2,1)S(1)} %copy-done.20), kind=kOutput, calls=%fused_computation | convolution fusion | flops 1617428480 | bytes 5767168 | tf_op jit(solution)/shard_map/dot_general | solution.py:24
  81.9 3.3 %collective-permute-start.9 = (bf16[128,768]{1,0:T(8,128)(2,1)S(1)}, bf16[128,768]{1,0:T(8,128)(2,1)S(1)}, u32[]{:S(2)}, u32[]{:S(2)}) collective-permute-start(bf16[128,768]{1,0:T(8,128)(2,1)S(1)} %get-tuple-element.97), channel_id=1, source_target_pairs={{0,224},{16,240},{32,0},{48,16},{64,32},{80,48},{96,64},{112,80},{... | collective-permute-start | bytes 589832 | tf_op jit(solution)/shard_map/ppermute | solution.py:34
  85.4 3.2 %collective-permute-start.7 = (bf16[768,128]{1,0:T(8,128)(2,1)S(1)}, bf16[768,128]{1,0:T(8,128)(2,1)S(1)}, u32[]{:S(2)}, u32[]{:S(2)}) collective-permute-start(bf16[768,128]{1,0:T(8,128)(2,1)S(1)} %get-tuple-element.67), channel_id=1, source_target_pairs={{0,224},{16,240},{32,0},{48,16},{64,32},{80,48},{96,64},{112,80},{... | collective-permute-start | bytes 589832 | tf_op jit(solution)/shard_map/ppermute | solution.py:34
  88.6 5.0 %shard_map.116 = bf16[384,2048]{1,0:T(8,128)(2,1)S(1)} custom-call(bf16[256,1536]{1,0:T(8,128)(2,1)S(1)} %get-tuple-element.60.refs_0_, bf16[2048,768]{1,0:T(8,128)(2,1)S(1)} %bitcast.31, bf16[2048,768]{1,0:T(8,128)(2,1)S(1)} %bitcast.30, bf16[384,256]{1,0:T(8,128)(2,1)S(1)} %copy-done.11), custom_call_target="tpu_custom_call" | custom-call | flops 1610612736 | bytes 6291456 | tf_op jit(solution)/shard_map/pallas_call | solution.py:221
  93.7 1.1 copy-done.4
  94.8 0.7 copy-done.23
  96.4 0.7 copy-done.26
  97.1 6.2 %all-to-all-start.2 = ((bf16[16,24,2048]{2,1,0:T(8,128)(2,1)}), bf16[16,24,2048]{2,1,0:T(8,128)(2,1)}, u32[]{:S(2)}, u32[]{:S(2)}) async-start(bf16[16,24,2048]{2,1,0:T(8,128)(2,1)} %bitcast.28), calls=%async_computation.2 | async-start | bytes 3145728 | tf_op jit(solution)/shard_map/all_to_all | solution.py:270
  103.8 2.8 %collective-permute-start.11 = (bf16[128,1536]{1,0:T(8,128)(2,1)S(1)}, bf16[128,1536]{1,0:T(8,128)(2,1)S(1)}, u32[]{:S(2)}, u32[]{:S(2)}) collective-permute-start(bf16[128,1536]{1,0:T(8,128)(2,1)S(1)} %get-tuple-element.71), channel_id=1, source_target_pairs={{0,224},{16,240},{32,0},{48,16},{64,32},{80,48},{96,64},{112,80},{... | collective-permute-start | bytes 1179656 | tf_op jit(solution)/shard_map/ppermute | solution.py:34
  106.6 7.8 %collective-permute-done.10.forward_ref = bf16[128,1536]{1,0:T(8,128)(2,1)S(1)} collective-permute-done((bf16[128,1536]{1,0:T(8,128)(2,1)}, bf16[128,1536]{1,0:T(8,128)(2,1)S(1)}, u32[]{:S(2)}, u32[]{:S(2)}) %collective-permute-start.10) | collective-permute-done | bytes 393248 | tf_op jit(solution)/shard_map/ppermute | solution.py:34
  115.2 2.7 %collective-permute-start.13 = (bf16[128,1536]{1,0:T(8,128)(2,1)S(1)}, bf16[128,1536]{1,0:T(8,128)(2,1)S(1)}, u32[]{:S(2)}, u32[]{:S(2)}) collective-permute-start(bf16[128,1536]{1,0:T(8,128)(2,1)S(1)} %get-tuple-element.80), channel_id=1, source_target_pairs={{0,224},{16,240},{32,0},{48,16},{64,32},{80,48},{96,64},{112,80},{... | collective-permute-start | bytes 1179656 | tf_op jit(solution)/shard_map/ppermute | solution.py:34
  117.9 3.2 %collective-permute-start.15 = (bf16[768,128]{1,0:T(8,128)(2,1)S(1)}, bf16[768,128]{1,0:T(8,128)(2,1)S(1)}, u32[]{:S(2)}, u32[]{:S(2)}) collective-permute-start(bf16[768,128]{1,0:T(8,128)(2,1)S(1)} %copy-done.25), channel_id=1, source_target_pairs={{0,224},{16,240},{32,0},{48,16},{64,32},{80,48},{96,64},{112,80},{... | collective-permute-start | bytes 589832 | tf_op jit(solution)/shard_map/ppermute | solution.py:34
  121.2 7.7 %collective-permute-done.14.forward_ref = bf16[768,128]{1,0:T(8,128)(2,1)S(1)} collective-permute-done((bf16[768,128]{1,0:T(8,128)(2,1)S(1)}, bf16[768,128]{1,0:T(8,128)(2,1)S(1)}, u32[]{:S(2)}, u32[]{:S(2)}) %collective-permute-start.14) | collective-permute-done | bytes 196640 | tf_op jit(solution)/shard_map/ppermute | solution.py:34
  128.9 0.9 shard_map.121
  129.8 1.0 shard_map.122
  130.8 1.3 collective-permute-start.16
  132.2 1.9 %collective-permute-start.17 = (bf16[128,1536]{1,0:T(8,128)(2,1)}, bf16[128,1536]{1,0:T(8,128)(2,1)}, u32[]{:S(2)}, u32[]{:S(2)}) collective-permute-start(bf16[128,1536]{1,0:T(8,128)(2,1)} %get-tuple-element.88), channel_id=1, source_target_pairs={{0,224},{16,240},{32,0},{48,16},{64,32},{80,48},{96,64},{112,80},{... | collective-permute-start | bytes 1179656 | tf_op jit(solution)/shard_map/ppermute | solution.py:34
  134.2 3.1 %collective-permute-start.19 = (bf16[768,128]{1,0:T(8,128)(2,1)}, bf16[768,128]{1,0:T(8,128)(2,1)}, u32[]{:S(2)}, u32[]{:S(2)}) collective-permute-start(bf16[768,128]{1,0:T(8,128)(2,1)} %get-tuple-element.84), channel_id=1, source_target_pairs={{0,224},{16,240},{32,0},{48,16},{64,32},{80,48},{96,64},{112,80},{... | collective-permute-start | bytes 589832 | tf_op jit(solution)/shard_map/ppermute | solution.py:34
  137.3 1.6 %reduce = f32[256]{0:T(256)} reduce(f32[256,1]{1,0:T(8,128)} %copy-done.12, f32[]{:T(128)} %constant.27), dimensions={1}, to_apply=%get-tuple-element.90.reduce_sub_computation | reduce | bytes 2052 | tf_op jit(solution)/shard_map/pallas_call | solution.py:221
  138.9 0.9 copy-done.14
  139.8 2.7 %shard_map.123 = bf16[128,2048]{1,0:T(8,128)(2,1)} custom-call(bf16[128,384]{1,0:T(8,128)(2,1)S(1)} %copy-done.14, bf16[384,2048]{1,0:T(8,128)(2,1)} %bitcast.14.tokens_ref), custom_call_target="tpu_custom_call" | custom-call | flops 201326592 | bytes 3145728 | tf_op jit(solution)/shard_map/pallas_call | solution.py:221
  142.5 2.0 %collective-permute-done.18.refs_0_ = bf16[768,128]{1,0:T(8,128)(2,1)} collective-permute-done((bf16[768,128]{1,0:T(8,128)(2,1)}, bf16[768,128]{1,0:T(8,128)(2,1)}, u32[]{:S(2)}, u32[]{:S(2)}) %collective-permute-start.18) | collective-permute-done | bytes 196640 | tf_op jit(solution)/shard_map/ppermute | solution.py:34
  144.5 1.8 %shard_map.124 = (bf16[1,128,768]{2,1,0:T(8,128)(2,1)}, bf16[1,128,768]{2,1,0:T(8,128)(2,1)}) custom-call(bf16[128,1536]{1,0:T(8,128)(2,1)S(1)} %collective-permute-done.16.refs_0_, bf16[128,1536]{1,0:T(8,128)(2,1)} %collective-permute-done.17.refs_1_, bf16[1024,1536]{1,0:T(8,128)(2,1)S(1)} %convolution_convert_fusion.refs_2_.refs_3_.front_ref.back_ref), custom_call_target="tpu_custom_call" | custom-call | flops 1 | bytes 1 | tf_op jit(solution)/shard_map/pallas_call | solution.py:221
  146.3 1.8 %shard_map.125 = bf16[1,768,128]{2,1,0:T(8,128)(2,1)} custom-call(bf16[768,128]{1,0:T(8,128)(2,1)} %collective-permute-done.18.refs_0_, bf16[768,128]{1,0:T(8,128)(2,1)} %collective-permute-done.19.refs_1_, bf16[768,1024]{1,0:T(8,128)(2,1)S(1)} %copy-done.2), custom_call_target="tpu_custom_call" | custom-call | flops 1 | bytes 1 | tf_op jit(solution)/shard_map/pallas_call | solution.py:221
  (83 shorter events, 6.6 us)
Async XLA Ops:
  0.6 12.1 %copy-start.9 = (bf16[128,2048]{1,0:T(8,128)(2,1)S(1)}, bf16[128,2048]{1,0:T(8,128)(2,1)}, u32[]{:S(2)}) copy-start(bf16[128,2048]{1,0:T(8,128)(2,1)} %tokens_ref.1) | copy-start | bytes 1572868
  0.6 0.8 copy-start.15
  1.4 1.0 copy-start.18
  5.3 28.9 %all-to-all-start.1 = ((bf16[16,24,2048]{2,1,0:T(8,128)(2,1)}), bf16[16,24,2048]{2,1,0:T(8,128)(2,1)S(1)}, u32[]{:S(2)}, u32[]{:S(2)}) async-start(bf16[16,24,2048]{2,1,0:T(8,128)(2,1)} %bitcast.9), calls=%async_computation.1 | async-start | bytes 3145728 | tf_op jit(solution)/shard_map/all_to_all | solution.py:270
  13.3 1.2 copy-start.3
  14.5 27.4 %copy-start.28 = (f32[1,1,256]{2,1,0:T(1,128)S(1)}, f32[1,1,256]{2,1,0:T(1,128)}, u32[]{:S(2)}) copy-start(f32[1,1,256]{2,1,0:T(1,128)} %param.10) | copy-start | bytes 3076
  34.2 26.0 %all-to-all-start = ((bf16[16,24,2048]{2,1,0:T(8,128)(2,1)}), bf16[16,24,2048]{2,1,0:T(8,128)(2,1)S(1)}, u32[]{:S(2)}, u32[]{:S(2)}) async-start(bf16[16,24,2048]{2,1,0:T(8,128)(2,1)} %bitcast.27), calls=%async_computation | async-start | bytes 3145728 | tf_op jit(solution)/shard_map/all_to_all | solution.py:270
  42.1 0.9 copy-start.8
  43.3 0.7 copy-start.10
  45.4 1.0 copy-start.16
  46.4 0.8 copy-start.19
  47.2 0.8 copy-start.21
  61.6 7.8 %collective-permute-start.3 = (bf16[256,1024]{1,0:T(8,128)(2,1)S(1)}, bf16[256,1024]{1,0:T(8,128)(2,1)S(1)}, u32[]{:S(2)}, u32[]{:S(2)}) collective-permute-start(bf16[256,1024]{1,0:T(8,128)(2,1)S(1)} %get-tuple-element.63), channel_id=1, source_target_pairs={{0,16},{16,0},{32,48},{48,32},{64,80},{80,64},{96,112},{112,96},{1... | collective-permute-start | bytes 1572872 | tf_op jit(solution)/shard_map/ppermute | solution.py:29
  61.7 3.4 %copy-start.7 = (bf16[1,2048,768]{2,1,0:T(8,128)(2,1)S(1)}, bf16[1,2048,768]{2,1,0:T(8,128)(2,1)}, u32[]{:S(2)}) copy-start(bf16[1,2048,768]{2,1,0:T(8,128)(2,1)} %param.11) | copy-start | bytes 9437188
  61.7 3.4 %copy-start.17 = (bf16[256,2048]{1,0:T(8,128)(2,1)S(1)}, bf16[256,2048]{1,0:T(8,128)(2,1)}, u32[]{:S(2)}) copy-start(bf16[256,2048]{1,0:T(8,128)(2,1)} %copy-done.16) | copy-start | bytes 3145732
  65.1 1.9 %copy-start.5 = (bf16[1,768,2048]{2,1,0:T(8,128)(2,1)S(1)}, bf16[1,768,2048]{2,1,0:T(8,128)(2,1)}, u32[]{:S(2)}) copy-start(bf16[1,768,2048]{2,1,0:T(8,128)(2,1)} %param.13) | copy-start | bytes 9437188
  66.3 3.1 %collective-permute-start.2 = (bf16[256,768]{1,0:T(8,128)(2,1)S(1)}, bf16[256,768]{1,0:T(8,128)(2,1)S(1)}, u32[]{:S(2)}, u32[]{:S(2)}) collective-permute-start(bf16[256,768]{1,0:T(8,128)(2,1)S(1)} %get-tuple-element.102.refs_3_), channel_id=1, source_target_pairs={{0,16},{16,0},{32,48},{48,32},{64,80},{80,64},{96,112},{112,96},{1... | collective-permute-start | bytes 1179656 | tf_op jit(solution)/shard_map/ppermute | solution.py:29
  67.0 2.4 %copy-start.22 = (bf16[256,1024]{1,0:T(8,128)(2,1)S(1)}, bf16[256,1024]{1,0:T(8,128)(2,1)}, u32[]{:S(2)}) copy-start(bf16[256,1024]{1,0:T(8,128)(2,1)} %copy-done.21) | copy-start | bytes 1572868
  68.9 11.0 %collective-permute-start.1 = (bf16[256,1536]{1,0:T(8,128)(2,1)S(1)}, bf16[256,1536]{1,0:T(8,128)(2,1)S(1)}, u32[]{:S(2)}, u32[]{:S(2)}) collective-permute-start(bf16[256,1536]{1,0:T(8,128)(2,1)S(1)} %get-tuple-element.60.refs_0_), channel_id=1, source_target_pairs={{0,16},{16,0},{32,48},{48,32},{64,80},{80,64},{96,112},{112,96},{1... | collective-permute-start | bytes 2359304 | tf_op jit(solution)/shard_map/ppermute | solution.py:29
  69.4 10.5 %collective-permute-start = (bf16[256,1024]{1,0:T(8,128)(2,1)S(1)}, bf16[256,1024]{1,0:T(8,128)(2,1)S(1)}, u32[]{:S(2)}, u32[]{:S(2)}) collective-permute-start(bf16[256,1024]{1,0:T(8,128)(2,1)S(1)} %copy-done.22), channel_id=1, source_target_pairs={{0,16},{16,0},{32,48},{48,32},{64,80},{80,64},{96,112},{112,96},{1... | collective-permute-start | bytes 1572872 | tf_op jit(solution)/shard_map/ppermute | solution.py:29
  69.4 10.5 %copy-start.20 = (bf16[256,1024]{1,0:T(8,128)(2,1)S(1)}, bf16[256,1024]{1,0:T(8,128)(2,1)}, u32[]{:S(2)}) copy-start(bf16[256,1024]{1,0:T(8,128)(2,1)} %copy-done.19) | copy-start | bytes 1572868
  70.4 25.1 %copy-start = (bf16[768,1024]{1,0:T(8,128)(2,1)}, bf16[768,1024]{1,0:T(8,128)(2,1)S(1)}, u32[]{:S(2)}) copy-start(bf16[768,1024]{1,0:T(8,128)(2,1)S(1)} %convolution_convert_fusion.1.refs_2_.refs_3_.front_ref.back_ref) | copy-start | bytes 4718596
  70.5 9.4 %collective-permute-start.4 = (bf16[384,128]{1,0:T(8,128)(2,1)S(1)}, bf16[384,128]{1,0:T(8,128)(2,1)S(1)}, u32[]{:S(2)}, u32[]{:S(2)}) collective-permute-start(bf16[384,128]{1,0:T(8,128)(2,1)S(1)} %get-tuple-element.100), channel_id=1, source_target_pairs={{0,32},{16,48},{32,64},{48,80},{64,96},{80,112},{96,128},{112,144}... | collective-permute-start | bytes 294920 | tf_op jit(solution)/shard_map/ppermute | solution.py:34
  72.5 7.4 %collective-permute-start.5 = (bf16[384,128]{1,0:T(8,128)(2,1)S(1)}, bf16[384,128]{1,0:T(8,128)(2,1)S(1)}, u32[]{:S(2)}, u32[]{:S(2)}) collective-permute-start(bf16[384,128]{1,0:T(8,128)(2,1)S(1)} %get-tuple-element.99), channel_id=1, source_target_pairs={{0,224},{16,240},{32,0},{48,16},{64,32},{80,48},{96,64},{112,80},{... | collective-permute-start | bytes 294920 | tf_op jit(solution)/shard_map/ppermute | solution.py:34
  81.7 6.9 %copy-start.6 = (bf16[1,2048,768]{2,1,0:T(8,128)(2,1)S(1)}, bf16[1,2048,768]{2,1,0:T(8,128)(2,1)}, u32[]{:S(2)}) copy-start(bf16[1,2048,768]{2,1,0:T(8,128)(2,1)} %param.12) | copy-start | bytes 9437188
  81.7 6.9 %copy-start.11 = (bf16[384,256]{1,0:T(8,128)(2,1)S(1)}, bf16[384,256]{1,0:T(8,128)(2,1)}, u32[]{:S(2)}) copy-start(bf16[384,256]{1,0:T(8,128)(2,1)} %copy-done.10) | copy-start | bytes 589828
  81.8 11.8 %collective-permute-start.8 = (bf16[128,768]{1,0:T(8,128)(2,1)S(1)}, bf16[128,768]{1,0:T(8,128)(2,1)S(1)}, u32[]{:S(2)}, u32[]{:S(2)}) collective-permute-start(bf16[128,768]{1,0:T(8,128)(2,1)S(1)} %get-tuple-element.98), channel_id=1, source_target_pairs={{0,32},{16,48},{32,64},{48,80},{64,96},{80,112},{96,128},{112,144}... | collective-permute-start | bytes 589832 | tf_op jit(solution)/shard_map/ppermute | solution.py:34
  81.9 11.7 %collective-permute-start.9 = (bf16[128,768]{1,0:T(8,128)(2,1)S(1)}, bf16[128,768]{1,0:T(8,128)(2,1)S(1)}, u32[]{:S(2)}, u32[]{:S(2)}) collective-permute-start(bf16[128,768]{1,0:T(8,128)(2,1)S(1)} %get-tuple-element.97), channel_id=1, source_target_pairs={{0,224},{16,240},{32,0},{48,16},{64,32},{80,48},{96,64},{112,80},{... | collective-permute-start | bytes 589832 | tf_op jit(solution)/shard_map/ppermute | solution.py:34
  85.3 10.2 %collective-permute-start.6 = (bf16[768,128]{1,0:T(8,128)(2,1)S(1)}, bf16[768,128]{1,0:T(8,128)(2,1)S(1)}, u32[]{:S(2)}, u32[]{:S(2)}) collective-permute-start(bf16[768,128]{1,0:T(8,128)(2,1)S(1)} %get-tuple-element.66), channel_id=1, source_target_pairs={{0,32},{16,48},{32,64},{48,80},{64,96},{80,112},{96,128},{112,144}... | collective-permute-start | bytes 589832 | tf_op jit(solution)/shard_map/ppermute | solution.py:34
  85.4 10.1 %collective-permute-start.7 = (bf16[768,128]{1,0:T(8,128)(2,1)S(1)}, bf16[768,128]{1,0:T(8,128)(2,1)S(1)}, u32[]{:S(2)}, u32[]{:S(2)}) collective-permute-start(bf16[768,128]{1,0:T(8,128)(2,1)S(1)} %get-tuple-element.67), channel_id=1, source_target_pairs={{0,224},{16,240},{32,0},{48,16},{64,32},{80,48},{96,64},{112,80},{... | collective-permute-start | bytes 589832 | tf_op jit(solution)/shard_map/ppermute | solution.py:34
  93.6 1.2 copy-start.4
  94.8 0.7 copy-start.23
  97.1 41.8 %all-to-all-start.2 = ((bf16[16,24,2048]{2,1,0:T(8,128)(2,1)}), bf16[16,24,2048]{2,1,0:T(8,128)(2,1)}, u32[]{:S(2)}, u32[]{:S(2)}) async-start(bf16[16,24,2048]{2,1,0:T(8,128)(2,1)} %bitcast.28), calls=%async_computation.2 | async-start | bytes 3145728 | tf_op jit(solution)/shard_map/all_to_all | solution.py:270
  103.3 14.6 %copy-start.27 = (bf16[768,128]{1,0:T(8,128)(2,1)S(1)}, bf16[768,128]{1,0:T(8,128)(2,1)}, u32[]{:S(2)}) copy-start(bf16[768,128]{1,0:T(8,128)(2,1)} %copy-done.26) | copy-start | bytes 589828
  103.3 14.6 %copy-start.25 = (bf16[768,128]{1,0:T(8,128)(2,1)S(1)}, bf16[768,128]{1,0:T(8,128)(2,1)}, u32[]{:S(2)}) copy-start(bf16[768,128]{1,0:T(8,128)(2,1)} %copy-done.24) | copy-start | bytes 589828
  103.3 25.6 %copy-start.1 = (bf16[768,1024]{1,0:T(8,128)(2,1)S(1)}, bf16[768,1024]{1,0:T(8,128)(2,1)}, u32[]{:S(2)}) copy-start(bf16[768,1024]{1,0:T(8,128)(2,1)} %copy-done) | copy-start | bytes 4718596
  103.3 11.1 %collective-permute-start.10 = (bf16[128,1536]{1,0:T(8,128)(2,1)}, bf16[128,1536]{1,0:T(8,128)(2,1)S(1)}, u32[]{:S(2)}, u32[]{:S(2)}) collective-permute-start(bf16[128,1536]{1,0:T(8,128)(2,1)} %copy-done.23), channel_id=1, source_target_pairs={{0,32},{16,48},{32,64},{48,80},{64,96},{80,112},{96,128},{112,144}... | collective-permute-start | bytes 1179656 | tf_op jit(solution)/shard_map/ppermute | solution.py:34
  103.8 10.6 %collective-permute-start.11 = (bf16[128,1536]{1,0:T(8,128)(2,1)S(1)}, bf16[128,1536]{1,0:T(8,128)(2,1)S(1)}, u32[]{:S(2)}, u32[]{:S(2)}) collective-permute-start(bf16[128,1536]{1,0:T(8,128)(2,1)S(1)} %get-tuple-element.71), channel_id=1, source_target_pairs={{0,224},{16,240},{32,0},{48,16},{64,32},{80,48},{96,64},{112,80},{... | collective-permute-start | bytes 1179656 | tf_op jit(solution)/shard_map/ppermute | solution.py:34
  114.6 15.2 %collective-permute-start.12 = (bf16[128,1536]{1,0:T(8,128)(2,1)S(1)}, bf16[128,1536]{1,0:T(8,128)(2,1)S(1)}, u32[]{:S(2)}, u32[]{:S(2)}) collective-permute-start(bf16[128,1536]{1,0:T(8,128)(2,1)S(1)} %get-tuple-element.79), channel_id=1, source_target_pairs={{0,32},{16,48},{32,64},{48,80},{64,96},{80,112},{96,128},{112,144}... | collective-permute-start | bytes 1179656 | tf_op jit(solution)/shard_map/ppermute | solution.py:34
  115.2 14.6 %collective-permute-start.13 = (bf16[128,1536]{1,0:T(8,128)(2,1)S(1)}, bf16[128,1536]{1,0:T(8,128)(2,1)S(1)}, u32[]{:S(2)}, u32[]{:S(2)}) collective-permute-start(bf16[128,1536]{1,0:T(8,128)(2,1)S(1)} %get-tuple-element.80), channel_id=1, source_target_pairs={{0,224},{16,240},{32,0},{48,16},{64,32},{80,48},{96,64},{112,80},{... | collective-permute-start | bytes 1179656 | tf_op jit(solution)/shard_map/ppermute | solution.py:34
  117.9 11.0 %collective-permute-start.14 = (bf16[768,128]{1,0:T(8,128)(2,1)S(1)}, bf16[768,128]{1,0:T(8,128)(2,1)S(1)}, u32[]{:S(2)}, u32[]{:S(2)}) collective-permute-start(bf16[768,128]{1,0:T(8,128)(2,1)S(1)} %copy-done.27), channel_id=1, source_target_pairs={{0,32},{16,48},{32,64},{48,80},{64,96},{80,112},{96,128},{112,144}... | collective-permute-start | bytes 589832 | tf_op jit(solution)/shard_map/ppermute | solution.py:34
  117.9 11.0 %collective-permute-start.15 = (bf16[768,128]{1,0:T(8,128)(2,1)S(1)}, bf16[768,128]{1,0:T(8,128)(2,1)S(1)}, u32[]{:S(2)}, u32[]{:S(2)}) collective-permute-start(bf16[768,128]{1,0:T(8,128)(2,1)S(1)} %copy-done.25), channel_id=1, source_target_pairs={{0,224},{16,240},{32,0},{48,16},{64,32},{80,48},{96,64},{112,80},{... | collective-permute-start | bytes 589832 | tf_op jit(solution)/shard_map/ppermute | solution.py:34
  130.8 11.6 %collective-permute-start.16 = (bf16[128,1536]{1,0:T(8,128)(2,1)}, bf16[128,1536]{1,0:T(8,128)(2,1)S(1)}, u32[]{:S(2)}, u32[]{:S(2)}) collective-permute-start(bf16[128,1536]{1,0:T(8,128)(2,1)} %get-tuple-element.87), channel_id=1, source_target_pairs={{0,32},{16,48},{32,64},{48,80},{64,96},{80,112},{96,128},{112,144}... | collective-permute-start | bytes 1179656 | tf_op jit(solution)/shard_map/ppermute | solution.py:34
  132.2 10.3 %collective-permute-start.17 = (bf16[128,1536]{1,0:T(8,128)(2,1)}, bf16[128,1536]{1,0:T(8,128)(2,1)}, u32[]{:S(2)}, u32[]{:S(2)}) collective-permute-start(bf16[128,1536]{1,0:T(8,128)(2,1)} %get-tuple-element.88), channel_id=1, source_target_pairs={{0,224},{16,240},{32,0},{48,16},{64,32},{80,48},{96,64},{112,80},{... | collective-permute-start | bytes 1179656 | tf_op jit(solution)/shard_map/ppermute | solution.py:34
  134.1 10.4 %collective-permute-start.18 = (bf16[768,128]{1,0:T(8,128)(2,1)}, bf16[768,128]{1,0:T(8,128)(2,1)}, u32[]{:S(2)}, u32[]{:S(2)}) collective-permute-start(bf16[768,128]{1,0:T(8,128)(2,1)} %get-tuple-element.83), channel_id=1, source_target_pairs={{0,32},{16,48},{32,64},{48,80},{64,96},{80,112},{96,128},{112,144}... | collective-permute-start | bytes 589832 | tf_op jit(solution)/shard_map/ppermute | solution.py:34
  134.2 10.2 %collective-permute-start.19 = (bf16[768,128]{1,0:T(8,128)(2,1)}, bf16[768,128]{1,0:T(8,128)(2,1)}, u32[]{:S(2)}, u32[]{:S(2)}) collective-permute-start(bf16[768,128]{1,0:T(8,128)(2,1)} %get-tuple-element.84), channel_id=1, source_target_pairs={{0,224},{16,240},{32,0},{48,16},{64,32},{80,48},{96,64},{112,80},{... | collective-permute-start | bytes 589832 | tf_op jit(solution)/shard_map/ppermute | solution.py:34
  138.9 0.9 copy-start.14
  142.5 3.8 %copy-start.2 = (bf16[768,1024]{1,0:T(8,128)(2,1)S(1)}, bf16[768,1024]{1,0:T(8,128)(2,1)}, u32[]{:S(2)}) copy-start(bf16[768,1024]{1,0:T(8,128)(2,1)} %copy-done) | copy-start | bytes 4718596
  (4 other events, 2.6 us)

commit v2 on v1

--- a/solution.py
+++ b/solution.py
@@ -41,90 +41,80 @@
     return total.astype(BF16)
 
 
-def halves_of(shape, axis):
-    half = shape[axis] // 2
-    full = [slice(None)] * len(shape)
-    first, second = list(full), list(full)
-    first[axis], second[axis] = slice(0, half), slice(half, 2 * half)
-    return tuple(first), tuple(second)
-
-
-def join_kernel(axis, forward_ref, backward_ref, front_ref, back_ref, front_out, back_out):
-    first, second = halves_of(front_ref.shape, axis)
-    front_out[first] = f32_sum(forward_ref[...], front_ref[first])
-    front_out[second] = front_ref[second]
-    back_out[first] = back_ref[first]
-    back_out[second] = f32_sum(backward_ref[...], back_ref[second])
-
-
-def add_kernel(forward_ref, backward_ref, front_ref, back_ref, front_out, back_out):
-    front_out[...] = f32_sum(forward_ref[...], front_ref[...])
-    back_out[...] = f32_sum(backward_ref[...], back_ref[...])
-
-
-def finish_kernel(axis, forward_ref, backward_ref, own_ref, *out_refs):
+def chunk_of(pre_ref, down_ref):
+    return jnp.concatenate([pre_ref[...], down_ref[...]], axis=1)
+
+
+def split_kernel(pre_ref, down_ref, front_out, back_out):
+    half = front_out.shape[0]
+    edge = pre_ref.shape[1]
+    for out, rows in ((front_out, slice(0, half)), (back_out, slice(half, 2 * half))):
+        out[:, :edge] = pre_ref[rows, :]
+        out[:, edge:] = down_ref[rows, :]
+
+
+def join_kernel(forward_ref, backward_ref, pre_front, down_front, pre_back, down_back, front_out, back_out):
+    half = forward_ref.shape[0]
+    front, back = chunk_of(pre_front, down_front), chunk_of(pre_back, down_back)
+    front_out[:half] = f32_sum(forward_ref[...], front[:half])
+    front_out[half:] = front[half:]
+    back_out[:half] = back[:half]
+    back_out[half:] = f32_sum(backward_ref[...], back[half:])
+
+
+def add_kernel(forward_ref, backward_ref, pre_front, down_front, pre_back, down_back, front_out, back_out):
+    front_out[...] = f32_sum(forward_ref[...], chunk_of(pre_front, down_front))
+    back_out[...] = f32_sum(backward_ref[...], chunk_of(pre_back, down_back))
+
+
+def finish_kernel(forward_ref, backward_ref, pre_ref, down_ref, gate_out, up_out, down_out):
     forward, backward = forward_ref[...], backward_ref[...]
-    if forward.shape != own_ref.shape:
-        both = jnp.concatenate([forward, backward], axis=axis)
-        total = f32_sum(own_ref[...], both)
+    if forward.shape != gate_out.shape[1:2] + forward.shape[1:]:
+        arrived = jnp.concatenate([forward, backward], axis=0).astype(F32)
     else:
-        total = f32_sum(own_ref[...], forward, backward)
-    for index, out_ref in enumerate(out_refs):
-        extent = out_ref.shape[2]
-        out_ref[0] = total[:, index * extent : (index + 1) * extent]
+        arrived = forward.astype(F32) + backward.astype(F32)
+    total = chunk_of(pre_ref, down_ref).astype(F32) + arrived
+    hidden = gate_out.shape[2]
+    gate_out[0] = total[:, :hidden].astype(BF16)
+    up_out[0] = total[:, hidden : 2 * hidden].astype(BF16)
+    down_out[0] = total[:, 2 * hidden :].T.astype(BF16)
 
 
 class Sums:
-    def __init__(self, part, chunk_shape, axis, chips):
-        self.part, self.chunk, self.axis, self.chips = part, chunk_shape, axis, chips
-        self.across = chunk_shape[0] == part.shape[0]
+    def __init__(self, far, parts, block, chips):
+        self.parts, self.block, self.chips = parts, block, chips
+        self.widths = [part.shape[1] for part in parts]
         self.distance = chips // 2
-
-    def slice(self, away):
+        half = jax.ShapeDtypeStruct((block // 2, sum(self.widths)), BF16)
+        self.send(call(split_kernel, (half, half), [VMEM, VMEM], far, 8, 1, 1))
+
+    def specs(self, away):
         place = away % self.chips
-        if self.across:
-            return self.part[:, place * self.chunk[1] : (place + 1) * self.chunk[1]]
-        return self.part[place * self.chunk[0] : (place + 1) * self.chunk[0]]
-
-    def spec(self, away):
-        place = away % self.chips
-        return pl.BlockSpec(self.chunk, lambda step: (0, place) if self.across else (place, 0))
-
-    def send(self, front, back):
-        self.moving = (next_chip(front, 1), next_chip(back, -1))
-
-    def first(self):
-        first, second = halves_of(self.chunk, self.axis)
-        chunk = self.slice(self.distance)
-        self.send(chunk[first], chunk[second])
-
-    def combine(self, after=None):
-        arrived = self.moving
-        if after is not None:
-            arrived, _ = lax.optimization_barrier((arrived, after))
-        kernel = add_kernel
-        if self.distance == self.chips // 2:
-            kernel = lambda *refs: join_kernel(self.axis, *refs)
+        return [pl.BlockSpec((self.block, width), lambda step: (place, 0)) for width in self.widths]
+
+    def send(self, operands):
+        self.moving = (next_chip(operands[0], 1), next_chip(operands[1], -1))
+
+    def step(self):
+        kernel = join_kernel if self.distance == self.chips // 2 else add_kernel
         self.distance -= 1
-        out = jax.ShapeDtypeStruct(self.chunk, BF16)
-        size = self.chunk[0] * self.chunk[1]
+        out = jax.ShapeDtypeStruct((self.block, sum(self.widths)), BF16)
         return call(
             kernel,
             (out, out),
-            [VMEM, VMEM, self.spec(self.distance), self.spec(-self.distance)],
-            (*arrived, self.part, self.part),
-            8, 1, 1, (1,),
+            [VMEM, VMEM, *self.specs(self.distance), *self.specs(-self.distance)],
+            (*self.moving, *self.parts, *self.parts),
+            12, 1, 1, (1,),
         )
 
     def finish(self, out_shapes, after):
         arrived, _ = lax.optimization_barrier((self.moving, after))
-        size = self.chunk[0] * self.chunk[1]
         return call(
-            lambda *refs: finish_kernel(self.axis, *refs),
+            finish_kernel,
             out_shapes,
-            [VMEM, VMEM, self.spec(0)],
-            (*arrived, self.part),
-            8, 1, 1, (1,),
+            [VMEM, VMEM, *self.specs(0)],
+            (*arrived, *self.parts),
+            12, 1, 1, (1,),
         )
 
 
@@ -301,6 +291,9 @@
     hidden_both = jnp.concatenate([hidden, swap_cores(hidden)], axis=0)
 
     gate_rows = gates.reshape(slot_count, 1)
+    arrived_grads, hidden, slope, activated, rows_both, hidden_both = lax.optimization_barrier(
+        (arrived_grads, hidden, slope, activated, rows_both, hidden_both)
+    )
     grads, scaled_keep, scaled_give = call(
         lambda *refs: compact_kernel(chips, *refs),
         compact_shapes,
@@ -317,8 +310,12 @@
         16, 2 * slot_count * width * hidden_width, 2 * width * hidden_width,
     )
     pre_both = jnp.concatenate([pre_grads, swap_cores(pre_grads)], axis=0)
-    down_part = dot_tn(hidden_both, scaled_both).astype(BF16)
-    pre_part = dot_tn(rows_both, pre_both).astype(BF16)
+
+    def parts_of(columns):
+        return (
+            dot_tn(rows_both[:, columns], pre_both).astype(BF16),
+            dot_tn(scaled_both[:, columns], hidden_both).astype(BF16),
+        )
 
     def give_back(pre_grads):
         return call(
@@ -338,42 +335,35 @@
             12, 2 * padded * tok_dev * width, 4 * padded * width,
         )
 
-    down_shape = (shape(1, hidden_width, block),)
-    pre_shape = (shape(1, block, hidden_width), shape(1, block, hidden_width))
     if chips > 1:
-        down = Sums(down_part, (hidden_width, block), 0, chips)
-        pre = Sums(pre_part, (block, 2 * hidden_width), 1, chips)
-        down.first()
-        pre.first()
+        farthest = chips // 2
+        far = parts_of(slice(farthest * block, (farthest + 1) * block))
+        parts = parts_of(slice(None))
+        sums = Sums(far, parts, block, chips)
+        returning = give_back(pre_grads)
         returned = None
-        held, _ = lax.optimization_barrier((pre_grads, pre_part))
-        returning = give_back(held)
-        latest = pre_grads
-        while down.distance > 1:
-            down_next = down.combine(latest)
-            if down.distance == chips // 2 - 2:
-                returning, _ = lax.optimization_barrier((returning, down_next))
+        while sums.distance > 1:
+            operands = sums.step()
+            if returned is None:
+                returning, _ = lax.optimization_barrier((returning, operands))
                 returned = exchange(returning)
-            down.send(*down_next)
-            pre_next = pre.combine(down_next)
-            pre.send(*pre_next)
-            latest = pre_next
+            sums.send(operands)
+            latest = operands
         if returned is None:
-            returned = exchange(returning)
+            returned, latest = exchange(returning), returning
         returned, _ = lax.optimization_barrier((returned, latest))
         token_grads = collect(returned)
-        grad_down = down.finish(down_shape, token_grads)
-        grad_pre = pre.finish(pre_shape, token_grads)
+        weight_shapes = (
+            shape(1, block, hidden_width),
+            shape(1, block, hidden_width),
+            shape(1, hidden_width, block),
+        )
+        weight_grads = sums.finish(weight_shapes, token_grads)
     else:
         token_grads = collect(exchange(give_back(pre_grads)))
-        grad_down = (down_part[None],)
-        grad_pre = tuple(half[None] for half in jnp.split(pre_part, 2, axis=1))
-    return (
-        token_grads,
-        slot_grads.reshape(1, 1, slot_count),
-        *grad_pre,
-        *grad_down,
-    )
+        pre_part, down_part = parts_of(slice(None))
+        weight_grads = (*(half[None] for half in jnp.split(pre_part, 2, axis=1)), down_part.T[None])
+    return (token_grads, slot_grads.reshape(1, 1, slot_count), *weight_grads)
 
 
 def solution(mesh):

time: 149 us -> 137 us (0.919)
  starting transfers between devices: 50.3 us -> 37.2 us
  other arithmetic: 1.65 us -> 4.76 us
  local copies, waits for them, and re-layouts: 14.4 us -> 11.4 us
    ppermute x16 -> x8, starting transfers between devices: 29.2 us -> 16 us  [next_chip(): lax.ppermute(array, 'dp', [(i, (i + 2 * sign) % size) for i in range(size)])]
    all_to_all x3, waiting for transfers between devices: 31.9 us -> 23.7 us  [exchange(): lax.all_to_all(shaped, 'expert', 0, 0, tiled=True).reshape(padded, width)]
    ppermute x16 -> x8, waiting for transfers between devices: 20.7 us -> 25.4 us  [next_chip(): lax.ppermute(array, 'dp', [(i, (i + 2 * sign) % size) for i in range(size)])]
    concatenate x0 -> x2, other arithmetic: none -> 4.01 us  [the longest x1 2.08 us: body(): rows_both = jnp.concatenate([rows_keep, swap_cores(rows_give)], axis=0)]
    unnamed x58 -> x42, local copies, waits for them, and re-layouts: 12.7 us -> 10.4 us
    ppermute x4, waiting for transfers between devices: 0.01 us -> 2.16 us  [swap_cores(): return lax.ppermute(array, 'dp', [(i, i ^ 1) for i in range(size)])]
    pallas_call x16 -> x13, Pallas kernels: 20.7 us -> 21.6 us  [call(): pl.pallas_call(kernel, grid=grid, out_shape=out_shapes, in_specs=in_specs...]
    dot_general x2 -> x4, matrix products: 2.85 us -> 3.55 us  [dot_tn(): lax.dot_general(left, right, (((0,), (0,)), ((), ())), preferred_element_...]
  transfers between devices with their start and end apart: 23 -> 15, of which waited for: 6 -> 8; matrix products, arithmetic and copies ran while one was open for 6% -> 10% of each run, Pallas kernels for 9% -> 11%
where the time goes in v2:
time: 137 us; the launch traced here: 136 us
  waiting for transfers between devices  51.3 us (37%)
  starting transfers between devices  37.2 us (27%)
  Pallas kernels  21.6 us (16%)
  local copies, waits for them, and re-layouts  11.4 us (8%)
  matrix products  8.64 us (6%)
  other arithmetic  4.76 us (3%)
    ppermute x8, waiting for transfers between devices, next_chip(): lax.ppermute(array, 'dp', [(i, (i + 2 * sign) % size) for i in range(size)])  25.4 us
    all_to_all x3, waiting for transfers between devices, exchange(): lax.all_to_all(shaped, 'expert', 0, 0, tiled=True).reshape(padded, width)  23.7 us
    pallas_call x13, Pallas kernels, call(): pl.pallas_call(kernel, grid=grid, out_shape=out_shapes, in_specs=in_specs...  21.6 us
    all_to_all x3, starting transfers between devices, exchange(): lax.all_to_all(shaped, 'expert', 0, 0, tiled=True).reshape(padded, width)  20 us
    ppermute x8, starting transfers between devices, next_chip(): lax.ppermute(array, 'dp', [(i, (i + 2 * sign) % size) for i in range(size)])  16 us
    unnamed x42, local copies, waits for them, and re-layouts  10.4 us
    dot_general x2, matrix products, dot_nn(): return jnp.dot(left, right, preferred_element_type=F32)  5.09 us
    dot_general x4, matrix products, dot_tn(): lax.dot_general(left, right, (((0,), (0,)), ((), ())), preferred_element_...  3.55 us
  transfers between devices with their start and end apart: 15, of which 8 were waited for; matrix products, arithmetic and copies ran while one was open for 10% of the time, Pallas kernels for 11%

profile of v2, /device:TPU:2, one launch (start us, length us, event | category | flops | bytes accessed | tf_op | source)
XLA Modules:
  0.0 135.8 jit_solution(17727161935047646701)
XLA Ops:
  0.6 0.7 copy-done.15
  1.4 1.0 copy-done.16
  2.4 2.2 %shard_map.110 = (bf16[384,128]{1,0:T(8,128)(2,1)S(1)}, bf16[128,384]{1,0:T(8,128)(2,1)S(1)}, bf16[384,2048]{1,0:T(8,128)(2,1)}) custom-call(s32[1]{0:T(128)} %bitcast.refs_0_, s32[16,256]{1,0:T(8,128)S(1)} %bitcast.38, bf16[128,2048]{1,0:T(8,128)(2,1)S(1)} %copy-done.16), custom_call_target="tpu_custom_call" | custom-call | flops 201326592 | bytes 3145728 | tf_op jit(solution)/shard_map/pallas_call | solution.py:211
  4.6 0.6 copy-done.13
  5.2 7.6 %all-to-all-start.1 = ((bf16[16,24,2048]{2,1,0:T(8,128)(2,1)}), bf16[16,24,2048]{2,1,0:T(8,128)(2,1)S(1)}, u32[]{:S(2)}, u32[]{:S(2)}) async-start(bf16[16,24,2048]{2,1,0:T(8,128)(2,1)} %bitcast.7), calls=%async_computation.1 | async-start | bytes 3145728 | tf_op jit(solution)/shard_map/all_to_all | solution.py:260
  12.8 0.7 dynamic-slice_bitcast_fusion
  14.0 0.6 shard_map.112
  14.6 1.2 copy-done.3
  15.8 18.4 %all-to-all-done.1 = bf16[16,24,2048]{2,1,0:T(8,128)(2,1)S(1)} async-done(((bf16[16,24,2048]{2,1,0:T(8,128)(2,1)}), bf16[16,24,2048]{2,1,0:T(8,128)(2,1)S(1)}, u32[]{:S(2)}, u32[]{:S(2)}) %all-to-all-start.1) | async-done | bytes 1572896 | tf_op jit(solution)/shard_map/all_to_all | solution.py:260
  34.3 6.3 %all-to-all-start = ((bf16[16,24,2048]{2,1,0:T(8,128)(2,1)}), bf16[16,24,2048]{2,1,0:T(8,128)(2,1)S(1)}, u32[]{:S(2)}, u32[]{:S(2)}) async-start(bf16[16,24,2048]{2,1,0:T(8,128)(2,1)} %bitcast.33), calls=%async_computation | async-start | bytes 3145728 | tf_op jit(solution)/shard_map/all_to_all | solution.py:260
  40.5 2.2 %shard_map.113 = (bf16[256,2048]{1,0:T(8,128)(2,1)S(1)}, bf16[256,1024]{1,0:T(8,128)(2,1)S(1)}, bf16[256,1024]{1,0:T(8,128)(2,1)}) custom-call(s32[2]{0:T(128)S(1)} %pad_add_fusion.refs_0_, bf16[256,384]{1,0:T(8,128)(2,1)S(1)} %get-tuple-element.40.refs_1_, bf16[384,2048]{1,0:T(8,128)(2,1)S(1)} %bitcast.31), custom_call_target="tpu_custom_call" | custom-call | flops 402653184 | bytes 4194304 | tf_op jit(solution)/shard_map/pallas_call | solution.py:211
  42.7 0.8 copy-done.11
  43.5 3.0 %fusion.3 = f32[256,768]{1,0:T(8,128)S(1)} fusion(bf16[256,2048]{1,0:T(8,128)(2,1)S(1)} %get-tuple-element.43, bf16[1,2048,768]{2,1,0:T(8,128)(2,1)} %param.12), kind=kOutput, calls=%fused_computation.18 | convolution fusion | flops 805306368 | bytes 4980736 | tf_op jit(solution)/shard_map/dot_general | solution.py:16
  46.5 2.1 %add_multiply_fusion = (f32[256,768]{1,0:T(8,128)S(1)}, bf16[256,768]{1,0:T(8,128)(2,1)S(1)}, f32[256,768]{1,0:T(8,128)}) fusion(f32[256,768]{1,0:T(8,128)S(1)} %fusion.3, bf16[256,2048]{1,0:T(8,128)(2,1)S(1)} %get-tuple-element.43, bf16[1,2048,768]{2,1,0:T(8,128)(2,1)S(1)} %copy-done.7), kind=kOutput, calls=%fused_computation.6 | convolution fusion | flops 807469056 | bytes 6946816 | tf_op jit(solution)/shard_map/dot_general | solution.py:16
  48.6 0.5 collective-permute-start
  49.3 1.7 %collective-permute-done.1 = bf16[256,768]{1,0:T(8,128)(2,1)} collective-permute-done((bf16[256,768]{1,0:T(8,128)(2,1)S(1)}, bf16[256,768]{1,0:T(8,128)(2,1)}, u32[]{:S(2)}, u32[]{:S(2)}) %collective-permute-start.1) | collective-permute-done | bytes 393248 | tf_op jit(solution)/shard_map/ppermute | solution.py:29
  51.0 1.9 %pad_maximum_fusion.1 = bf16[512,768]{1,0:T(8,128)(2,1)} fusion(bf16[256,768]{1,0:T(8,128)(2,1)} %collective-permute-done.1, bf16[256,768]{1,0:T(8,128)(2,1)S(1)} %get-tuple-element.48.refs_3_), kind=kLoop, calls=%fused_computation.5 | loop fusion | flops 1572864 | bytes 1572864 | tf_op jit(solution)/shard_map/concatenate | solution.py:291
  52.9 2.1 %pad_maximum_fusion = bf16[512,1024]{1,0:T(8,128)(2,1)} fusion(bf16[256,1024]{1,0:T(8,128)(2,1)} %collective-permute-done, bf16[256,1024]{1,0:T(8,128)(2,1)S(1)} %copy-done.12), kind=kLoop, calls=%fused_computation.4 | loop fusion | flops 2097152 | bytes 2097152 | tf_op jit(solution)/shard_map/concatenate | solution.py:284
  55.0 5.2 %all-to-all-done = bf16[16,24,2048]{2,1,0:T(8,128)(2,1)S(1)} async-done(((bf16[16,24,2048]{2,1,0:T(8,128)(2,1)}), bf16[16,24,2048]{2,1,0:T(8,128)(2,1)S(1)}, u32[]{:S(2)}, u32[]{:S(2)}) %all-to-all-start) | async-done | bytes 1572896 | tf_op jit(solution)/shard_map/all_to_all | solution.py:260
  60.3 1.4 %shard_map.114 = (bf16[256,2048]{1,0:T(8,128)(2,1)S(1)}, bf16[256,1024]{1,0:T(8,128)(2,1)S(1)}, bf16[256,1024]{1,0:T(8,128)(2,1)S(1)}) custom-call(s32[2]{0:T(128)S(1)} %pad_add_fusion.refs_0_, bf16[256,384]{1,0:T(8,128)(2,1)S(1)} %get-tuple-element.40.refs_1_, bf16[384,2048]{1,0:T(8,128)(2,1)S(1)} %bitcast.32, f32[256,1]{1,0:T(8,128)S(1)} %copy.13.refs_3_.refs_2_), custom_call_target="tpu_custom_call" | custom-call | flops 402653184 | bytes 4194304 | tf_op jit(solution)/shard_map/pallas_call | solution.py:211
  61.8 1.9 %copy-done.5 = bf16[1,768,2048]{2,1,0:T(8,128)(2,1)S(1)} copy-done((bf16[1,768,2048]{2,1,0:T(8,128)(2,1)S(1)}, bf16[1,768,2048]{2,1,0:T(8,128)(2,1)}, u32[]{:S(2)}) %copy-start.5) | copy-done | bytes 3145752
  63.7 1.1 shard_map.115
  64.8 0.6 collective-permute-start.2
  65.5 1.0 copy-done.17
  66.9 0.4 collective-permute-done.2
  68.2 1.0 convolution_convert_fusion.2.down_front.down_back.down_ref
  69.3 2.0 %collective-permute-start.4 = (bf16[64,2304]{1,0:T(8,128)(2,1)S(1)}, bf16[64,2304]{1,0:T(8,128)(2,1)S(1)}, u32[]{:S(2)}, u32[]{:S(2)}) collective-permute-start(bf16[64,2304]{1,0:T(8,128)(2,1)S(1)} %get-tuple-element.57), channel_id=1, source_target_pairs={{0,32},{16,48},{32,64},{48,80},{64,96},{80,112},{96,128},{112,144}... | collective-permute-start | bytes 884744 | tf_op jit(solution)/shard_map/ppermute | solution.py:34
  71.3 4.2 %collective-permute-start.5 = (bf16[64,2304]{1,0:T(8,128)(2,1)S(1)}, bf16[64,2304]{1,0:T(8,128)(2,1)S(1)}, u32[]{:S(2)}, u32[]{:S(2)}) collective-permute-start(bf16[64,2304]{1,0:T(8,128)(2,1)S(1)} %get-tuple-element.58), channel_id=1, source_target_pairs={{0,224},{16,240},{32,0},{48,16},{64,32},{80,48},{96,64},{112,80},{... | collective-permute-start | bytes 884744 | tf_op jit(solution)/shard_map/ppermute | solution.py:34
  75.5 1.8 %convolution_convert_fusion.pre_front.pre_back.pre_ref = bf16[1024,1536]{1,0:T(8,128)(2,1)S(1)} fusion(bf16[512,1024]{1,0:T(8,128)(2,1)S(1)} %copy-done.18, bf16[512,1536]{1,0:T(8,128)(2,1)S(1)} %constant_dynamic-update-slice_fusion), kind=kOutput, calls=%fused_computation | convolution fusion | flops 1612185600 | bytes 5767168 | tf_op jit(solution)/shard_map/dot_general | solution.py:24
  77.3 5.1 %collective-permute-done.4.forward_ref = bf16[64,2304]{1,0:T(8,128)(2,1)S(1)} collective-permute-done((bf16[64,2304]{1,0:T(8,128)(2,1)S(1)}, bf16[64,2304]{1,0:T(8,128)(2,1)S(1)}, u32[]{:S(2)}, u32[]{:S(2)}) %collective-permute-start.4) | collective-permute-done | bytes 294944 | tf_op jit(solution)/shard_map/ppermute | solution.py:34
  82.4 1.2 shard_map.118
  83.6 3.2 %collective-permute-start.7 = (bf16[128,2304]{1,0:T(8,128)(2,1)}, bf16[128,2304]{1,0:T(8,128)(2,1)}, u32[]{:S(2)}, u32[]{:S(2)}) collective-permute-start(bf16[128,2304]{1,0:T(8,128)(2,1)} %get-tuple-element.60), channel_id=1, source_target_pairs={{0,224},{16,240},{32,0},{48,16},{64,32},{80,48},{96,64},{112,80},{... | collective-permute-start | bytes 1769480 | tf_op jit(solution)/shard_map/ppermute | solution.py:34
  86.8 5.0 %shard_map.116 = bf16[384,2048]{1,0:T(8,128)(2,1)S(1)} custom-call(bf16[256,1536]{1,0:T(8,128)(2,1)S(1)} %get-tuple-element.51.refs_0_, bf16[2048,768]{1,0:T(8,128)(2,1)S(1)} %bitcast.37, bf16[2048,768]{1,0:T(8,128)(2,1)S(1)} %bitcast.36, bf16[384,256]{1,0:T(8,128)(2,1)S(1)} %get-tuple-element.52.refs_3_), custom_call_target="tpu_custom_call" | custom-call | flops 1610612736 | bytes 6291456 | tf_op jit(solution)/shard_map/pallas_call | solution.py:211
  91.8 1.2 copy-done.4
  93.0 6.2 %all-to-all-start.2 = ((bf16[16,24,2048]{2,1,0:T(8,128)(2,1)}), bf16[16,24,2048]{2,1,0:T(8,128)(2,1)}, u32[]{:S(2)}, u32[]{:S(2)}) async-start(bf16[16,24,2048]{2,1,0:T(8,128)(2,1)} %bitcast.34), calls=%async_computation.2 | async-start | bytes 3145728 | tf_op jit(solution)/shard_map/all_to_all | solution.py:260
  99.1 0.7 collective-permute-done.6.forward_ref
  99.9 1.4 %copy-done.1 = bf16[1024,768]{1,0:T(8,128)(2,1)S(1)} copy-done((bf16[1024,768]{1,0:T(8,128)(2,1)S(1)}, bf16[1024,768]{1,0:T(8,128)(2,1)}, u32[]{:S(2)}) %copy-start.1) | copy-done | bytes 1572888
  101.3 1.5 %shard_map.119 = (bf16[128,2304]{1,0:T(8,128)(2,1)S(1)}, bf16[128,2304]{1,0:T(8,128)(2,1)S(1)}) custom-call(bf16[128,2304]{1,0:T(8,128)(2,1)} %collective-permute-done.6.forward_ref, bf16[128,2304]{1,0:T(8,128)(2,1)} %collective-permute-done.7.backward_ref, bf16[1024,1536]{1,0:T(8,128)(2,1)S(1)} %convolution_convert_fusion.pre_front.pre_back.pre_ref, ...), custom_call_target="tpu_custom_call" | custom-call | flops 1 | bytes 1 | tf_op jit(solution)/shard_map/pallas_call | solution.py:211
  102.8 1.9 %collective-permute-start.8 = (bf16[128,2304]{1,0:T(8,128)(2,1)S(1)}, bf16[128,2304]{1,0:T(8,128)(2,1)S(1)}, u32[]{:S(2)}, u32[]{:S(2)}) collective-permute-start(bf16[128,2304]{1,0:T(8,128)(2,1)S(1)} %get-tuple-element.62), channel_id=1, source_target_pairs={{0,32},{16,48},{32,64},{48,80},{64,96},{80,112},{96,128},{112,144}... | collective-permute-start | bytes 1769480 | tf_op jit(solution)/shard_map/ppermute | solution.py:34
  104.7 1.4 %collective-permute-start.9 = (bf16[128,2304]{1,0:T(8,128)(2,1)S(1)}, bf16[128,2304]{1,0:T(8,128)(2,1)S(1)}, u32[]{:S(2)}, u32[]{:S(2)}) collective-permute-start(bf16[128,2304]{1,0:T(8,128)(2,1)S(1)} %get-tuple-element.63), channel_id=1, source_target_pairs={{0,224},{16,240},{32,0},{48,16},{64,32},{80,48},{96,64},{112,80},{... | collective-permute-start | bytes 1769480 | tf_op jit(solution)/shard_map/ppermute | solution.py:34
  106.1 11.8 %collective-permute-done.8.forward_ref = bf16[128,2304]{1,0:T(8,128)(2,1)S(1)} collective-permute-done((bf16[128,2304]{1,0:T(8,128)(2,1)S(1)}, bf16[128,2304]{1,0:T(8,128)(2,1)S(1)}, u32[]{:S(2)}, u32[]{:S(2)}) %collective-permute-start.8) | collective-permute-done | bytes 589856 | tf_op jit(solution)/shard_map/ppermute | solution.py:34
  117.9 1.2 shard_map.120
  119.0 1.5 %collective-permute-start.10 = (bf16[128,2304]{1,0:T(8,128)(2,1)}, bf16[128,2304]{1,0:T(8,128)(2,1)}, u32[]{:S(2)}, u32[]{:S(2)}) collective-permute-start(bf16[128,2304]{1,0:T(8,128)(2,1)} %get-tuple-element.64), channel_id=1, source_target_pairs={{0,32},{16,48},{32,64},{48,80},{64,96},{80,112},{96,128},{112,144}... | collective-permute-start | bytes 1769480 | tf_op jit(solution)/shard_map/ppermute | solution.py:34
  120.6 1.7 %collective-permute-start.11 = (bf16[128,2304]{1,0:T(8,128)(2,1)}, bf16[128,2304]{1,0:T(8,128)(2,1)}, u32[]{:S(2)}, u32[]{:S(2)}) collective-permute-start(bf16[128,2304]{1,0:T(8,128)(2,1)} %get-tuple-element.65), channel_id=1, source_target_pairs={{0,224},{16,240},{32,0},{48,16},{64,32},{80,48},{96,64},{112,80},{... | collective-permute-start | bytes 1769480 | tf_op jit(solution)/shard_map/ppermute | solution.py:34
  122.3 0.7 reduce
  122.9 2.8 %shard_map.121 = bf16[128,2048]{1,0:T(8,128)(2,1)} custom-call(bf16[128,384]{1,0:T(8,128)(2,1)S(1)} %copy-done.14, bf16[384,2048]{1,0:T(8,128)(2,1)} %bitcast.14.tokens_ref), custom_call_target="tpu_custom_call" | custom-call | flops 201326592 | bytes 3145728 | tf_op jit(solution)/shard_map/pallas_call | solution.py:211
  125.7 7.8 %collective-permute-done.10.forward_ref = bf16[128,2304]{1,0:T(8,128)(2,1)} collective-permute-done((bf16[128,2304]{1,0:T(8,128)(2,1)}, bf16[128,2304]{1,0:T(8,128)(2,1)}, u32[]{:S(2)}, u32[]{:S(2)}) %collective-permute-start.10) | collective-permute-done | bytes 589856 | tf_op jit(solution)/shard_map/ppermute | solution.py:34
  133.5 2.3 %shard_map.122 = (bf16[1,128,768]{2,1,0:T(8,128)(2,1)}, bf16[1,128,768]{2,1,0:T(8,128)(2,1)}, bf16[1,768,128]{2,1,0:T(8,128)(2,1)}) custom-call(bf16[128,2304]{1,0:T(8,128)(2,1)} %collective-permute-done.10.forward_ref, bf16[128,2304]{1,0:T(8,128)(2,1)} %collective-permute-done.11.backward_ref, ...), custom_call_target="tpu_custom_call" | custom-call | flops 1 | bytes 1 | tf_op jit(solution)/shard_map/pallas_call | solution.py:211
  (52 shorter events, 2.2 us)
Async XLA Ops:
  0.6 0.7 copy-start.15
  1.4 1.0 copy-start.16
  4.6 0.6 copy-start.13
  5.2 8.8 %copy-start.10 = (bf16[128,2048]{1,0:T(8,128)(2,1)S(1)}, bf16[128,2048]{1,0:T(8,128)(2,1)}, u32[]{:S(2)}) copy-start(bf16[128,2048]{1,0:T(8,128)(2,1)} %tokens_ref.1) | copy-start | bytes 1572868
  5.2 29.0 %all-to-all-start.1 = ((bf16[16,24,2048]{2,1,0:T(8,128)(2,1)}), bf16[16,24,2048]{2,1,0:T(8,128)(2,1)S(1)}, u32[]{:S(2)}, u32[]{:S(2)}) async-start(bf16[16,24,2048]{2,1,0:T(8,128)(2,1)} %bitcast.7), calls=%async_computation.1 | async-start | bytes 3145728 | tf_op jit(solution)/shard_map/all_to_all | solution.py:260
  14.6 1.2 copy-start.3
  34.3 26.0 %all-to-all-start = ((bf16[16,24,2048]{2,1,0:T(8,128)(2,1)}), bf16[16,24,2048]{2,1,0:T(8,128)(2,1)S(1)}, u32[]{:S(2)}, u32[]{:S(2)}) async-start(bf16[16,24,2048]{2,1,0:T(8,128)(2,1)} %bitcast.33), calls=%async_computation | async-start | bytes 3145728 | tf_op jit(solution)/shard_map/all_to_all | solution.py:260
  42.7 0.8 copy-start.11
  43.5 3.0 %copy-start.7 = (bf16[1,2048,768]{2,1,0:T(8,128)(2,1)S(1)}, bf16[1,2048,768]{2,1,0:T(8,128)(2,1)}, u32[]{:S(2)}) copy-start(bf16[1,2048,768]{2,1,0:T(8,128)(2,1)} %param.11) | copy-start | bytes 9437188
  46.5 2.6 %copy-start.19 = (f32[1,1,256]{2,1,0:T(1,128)S(1)}, f32[1,1,256]{2,1,0:T(1,128)}, u32[]{:S(2)}) copy-start(f32[1,1,256]{2,1,0:T(1,128)} %param.10) | copy-start | bytes 3076
  48.6 2.4 %collective-permute-start.1 = (bf16[256,768]{1,0:T(8,128)(2,1)S(1)}, bf16[256,768]{1,0:T(8,128)(2,1)}, u32[]{:S(2)}, u32[]{:S(2)}) collective-permute-start(bf16[256,768]{1,0:T(8,128)(2,1)S(1)} %get-tuple-element.48.refs_3_), channel_id=1, source_target_pairs={{0,16},{16,0},{32,48},{48,32},{64,80},{80,64},{96,112},{112,96},{1... | collective-permute-start | bytes 1179656 | tf_op jit(solution)/shard_map/ppermute | solution.py:29
  48.6 4.3 %collective-permute-start = (bf16[256,1024]{1,0:T(8,128)(2,1)}, bf16[256,1024]{1,0:T(8,128)(2,1)}, u32[]{:S(2)}, u32[]{:S(2)}) collective-permute-start(bf16[256,1024]{1,0:T(8,128)(2,1)} %get-tuple-element.45), channel_id=1, source_target_pairs={{0,16},{16,0},{32,48},{48,32},{64,80},{80,64},{96,112},{112,96},{1... | collective-permute-start | bytes 1572872 | tf_op jit(solution)/shard_map/ppermute | solution.py:29
  49.3 3.7 %copy-start.12 = (bf16[256,1024]{1,0:T(8,128)(2,1)S(1)}, bf16[256,1024]{1,0:T(8,128)(2,1)}, u32[]{:S(2)}) copy-start(bf16[256,1024]{1,0:T(8,128)(2,1)} %copy-done.11) | copy-start | bytes 1572868
  60.3 1.5 %copy-start.9 = (f32[256,768]{1,0:T(8,128)S(1)}, f32[256,768]{1,0:T(8,128)}, u32[]{:S(2)}) copy-start(f32[256,768]{1,0:T(8,128)} %get-tuple-element.50.refs_5_) | copy-start | bytes 2359300
  61.7 3.8 %collective-permute-start.3 = (bf16[256,1024]{1,0:T(8,128)(2,1)S(1)}, bf16[256,1024]{1,0:T(8,128)(2,1)S(1)}, u32[]{:S(2)}, u32[]{:S(2)}) collective-permute-start(bf16[256,1024]{1,0:T(8,128)(2,1)S(1)} %get-tuple-element.55), channel_id=1, source_target_pairs={{0,16},{16,0},{32,48},{48,32},{64,80},{80,64},{96,112},{112,96},{1... | collective-permute-start | bytes 1572872 | tf_op jit(solution)/shard_map/ppermute | solution.py:29
  61.8 1.9 %copy-start.5 = (bf16[1,768,2048]{2,1,0:T(8,128)(2,1)S(1)}, bf16[1,768,2048]{2,1,0:T(8,128)(2,1)}, u32[]{:S(2)}) copy-start(bf16[1,768,2048]{2,1,0:T(8,128)(2,1)} %param.13) | copy-start | bytes 9437188
  64.8 2.5 %collective-permute-start.2 = (bf16[256,1536]{1,0:T(8,128)(2,1)S(1)}, bf16[256,1536]{1,0:T(8,128)(2,1)S(1)}, u32[]{:S(2)}, u32[]{:S(2)}) collective-permute-start(bf16[256,1536]{1,0:T(8,128)(2,1)S(1)} %get-tuple-element.51.refs_0_), channel_id=1, source_target_pairs={{0,16},{16,0},{32,48},{48,32},{64,80},{80,64},{96,112},{112,96},{1... | collective-permute-start | bytes 2359304 | tf_op jit(solution)/shard_map/ppermute | solution.py:29
  65.4 1.1 copy-start.17
  66.6 1.2 copy-start.18
  69.2 13.2 %copy-start = (bf16[1024,768]{1,0:T(8,128)(2,1)}, bf16[1024,768]{1,0:T(8,128)(2,1)S(1)}, u32[]{:S(2)}) copy-start(bf16[1024,768]{1,0:T(8,128)(2,1)S(1)} %convolution_convert_fusion.2.down_front.down_back.down_ref) | copy-start | bytes 4718596
  69.3 13.1 %collective-permute-start.4 = (bf16[64,2304]{1,0:T(8,128)(2,1)S(1)}, bf16[64,2304]{1,0:T(8,128)(2,1)S(1)}, u32[]{:S(2)}, u32[]{:S(2)}) collective-permute-start(bf16[64,2304]{1,0:T(8,128)(2,1)S(1)} %get-tuple-element.57), channel_id=1, source_target_pairs={{0,32},{16,48},{32,64},{48,80},{64,96},{80,112},{96,128},{112,144}... | collective-permute-start | bytes 884744 | tf_op jit(solution)/shard_map/ppermute | solution.py:34
  71.3 11.1 %collective-permute-start.5 = (bf16[64,2304]{1,0:T(8,128)(2,1)S(1)}, bf16[64,2304]{1,0:T(8,128)(2,1)S(1)}, u32[]{:S(2)}, u32[]{:S(2)}) collective-permute-start(bf16[64,2304]{1,0:T(8,128)(2,1)S(1)} %get-tuple-element.58), channel_id=1, source_target_pairs={{0,224},{16,240},{32,0},{48,16},{64,32},{80,48},{96,64},{112,80},{... | collective-permute-start | bytes 884744 | tf_op jit(solution)/shard_map/ppermute | solution.py:34
  82.4 4.4 %copy-start.6 = (bf16[1,2048,768]{2,1,0:T(8,128)(2,1)S(1)}, bf16[1,2048,768]{2,1,0:T(8,128)(2,1)}, u32[]{:S(2)}) copy-start(bf16[1,2048,768]{2,1,0:T(8,128)(2,1)} %param.12) | copy-start | bytes 9437188
  82.4 4.4 %copy-start.8 = (bf16[1,2048,768]{2,1,0:T(8,128)(2,1)S(1)}, bf16[1,2048,768]{2,1,0:T(8,128)(2,1)}, u32[]{:S(2)}) copy-start(bf16[1,2048,768]{2,1,0:T(8,128)(2,1)} %param.11) | copy-start | bytes 9437188
  83.6 16.3 %collective-permute-start.6 = (bf16[128,2304]{1,0:T(8,128)(2,1)}, bf16[128,2304]{1,0:T(8,128)(2,1)}, u32[]{:S(2)}, u32[]{:S(2)}) collective-permute-start(bf16[128,2304]{1,0:T(8,128)(2,1)} %get-tuple-element.59), channel_id=1, source_target_pairs={{0,32},{16,48},{32,64},{48,80},{64,96},{80,112},{96,128},{112,144}... | collective-permute-start | bytes 1769480 | tf_op jit(solution)/shard_map/ppermute | solution.py:34
  83.6 16.3 %collective-permute-start.7 = (bf16[128,2304]{1,0:T(8,128)(2,1)}, bf16[128,2304]{1,0:T(8,128)(2,1)}, u32[]{:S(2)}, u32[]{:S(2)}) collective-permute-start(bf16[128,2304]{1,0:T(8,128)(2,1)} %get-tuple-element.60), channel_id=1, source_target_pairs={{0,224},{16,240},{32,0},{48,16},{64,32},{80,48},{96,64},{112,80},{... | collective-permute-start | bytes 1769480 | tf_op jit(solution)/shard_map/ppermute | solution.py:34
  91.8 1.2 copy-start.4
  93.0 30.0 %all-to-all-start.2 = ((bf16[16,24,2048]{2,1,0:T(8,128)(2,1)}), bf16[16,24,2048]{2,1,0:T(8,128)(2,1)}, u32[]{:S(2)}, u32[]{:S(2)}) async-start(bf16[16,24,2048]{2,1,0:T(8,128)(2,1)} %bitcast.34), calls=%async_computation.2 | async-start | bytes 3145728 | tf_op jit(solution)/shard_map/all_to_all | solution.py:260
  99.8 1.4 %copy-start.1 = (bf16[1024,768]{1,0:T(8,128)(2,1)S(1)}, bf16[1024,768]{1,0:T(8,128)(2,1)}, u32[]{:S(2)}) copy-start(bf16[1024,768]{1,0:T(8,128)(2,1)} %copy-done) | copy-start | bytes 4718596
  102.8 15.1 %collective-permute-start.8 = (bf16[128,2304]{1,0:T(8,128)(2,1)S(1)}, bf16[128,2304]{1,0:T(8,128)(2,1)S(1)}, u32[]{:S(2)}, u32[]{:S(2)}) collective-permute-start(bf16[128,2304]{1,0:T(8,128)(2,1)S(1)} %get-tuple-element.62), channel_id=1, source_target_pairs={{0,32},{16,48},{32,64},{48,80},{64,96},{80,112},{96,128},{112,144}... | collective-permute-start | bytes 1769480 | tf_op jit(solution)/shard_map/ppermute | solution.py:34
  104.7 18.3 %copy-start.14 = (bf16[128,384]{1,0:T(8,128)(2,1)S(1)}, bf16[128,384]{1,0:T(8,128)(2,1)}, u32[]{:S(2)}) copy-start(bf16[128,384]{1,0:T(8,128)(2,1)} %copy-done.13) | copy-start | bytes 294916
  104.7 13.2 %collective-permute-start.9 = (bf16[128,2304]{1,0:T(8,128)(2,1)S(1)}, bf16[128,2304]{1,0:T(8,128)(2,1)S(1)}, u32[]{:S(2)}, u32[]{:S(2)}) collective-permute-start(bf16[128,2304]{1,0:T(8,128)(2,1)S(1)} %get-tuple-element.63), channel_id=1, source_target_pairs={{0,224},{16,240},{32,0},{48,16},{64,32},{80,48},{96,64},{112,80},{... | collective-permute-start | bytes 1769480 | tf_op jit(solution)/shard_map/ppermute | solution.py:34
  119.0 14.5 %collective-permute-start.10 = (bf16[128,2304]{1,0:T(8,128)(2,1)}, bf16[128,2304]{1,0:T(8,128)(2,1)}, u32[]{:S(2)}, u32[]{:S(2)}) collective-permute-start(bf16[128,2304]{1,0:T(8,128)(2,1)} %get-tuple-element.64), channel_id=1, source_target_pairs={{0,32},{16,48},{32,64},{48,80},{64,96},{80,112},{96,128},{112,144}... | collective-permute-start | bytes 1769480 | tf_op jit(solution)/shard_map/ppermute | solution.py:34
  120.6 13.0 %collective-permute-start.11 = (bf16[128,2304]{1,0:T(8,128)(2,1)}, bf16[128,2304]{1,0:T(8,128)(2,1)}, u32[]{:S(2)}, u32[]{:S(2)}) collective-permute-start(bf16[128,2304]{1,0:T(8,128)(2,1)} %get-tuple-element.65), channel_id=1, source_target_pairs={{0,224},{16,240},{32,0},{48,16},{64,32},{80,48},{96,64},{112,80},{... | collective-permute-start | bytes 1769480 | tf_op jit(solution)/shard_map/ppermute | solution.py:34
  122.9 10.6 %copy-start.2 = (bf16[1024,768]{1,0:T(8,128)(2,1)S(1)}, bf16[1024,768]{1,0:T(8,128)(2,1)}, u32[]{:S(2)}) copy-start(bf16[1024,768]{1,0:T(8,128)(2,1)} %copy-done) | copy-start | bytes 4718596

commit v3 on v2

--- a/solution.py
+++ b/solution.py
@@ -1,3 +1,5 @@
+import functools
+
 import jax
 import jax.numpy as jnp
 from jax import lax
@@ -86,7 +88,8 @@
         self.widths = [part.shape[1] for part in parts]
         self.distance = chips // 2
         half = jax.ShapeDtypeStruct((block // 2, sum(self.widths)), BF16)
-        self.send(call(split_kernel, (half, half), [VMEM, VMEM], far, 8, 1, 1))
+        self.operands = call(split_kernel, (half, half), [VMEM, VMEM], far, 8, 1, 1)
+        self.send(self.operands)
 
     def specs(self, away):
         place = away % self.chips
@@ -118,10 +121,9 @@
         )
 
 
-def select_kernel(most, base_ref, picks_ref, tokens_ref, select_ref, turned_ref, out_ref):
+def select_matrix(most, tok_dev, base_ref, picks_ref):
     local = picks_ref[...] - base_ref[0]
     experts, slots = local.shape
-    tok_dev = tokens_ref.shape[0]
     below = jnp.sum((local < 0).astype(F32), axis=1, keepdims=True).astype(I32)
     counter = lax.broadcasted_iota(I32, (most, 1), 0)
     spread = jnp.concatenate(
@@ -132,11 +134,18 @@
     hit = (position == wanted) & (spread >= 0) & (spread < tok_dev)
     token = jnp.sum(jnp.where(hit, spread + 1, 0).astype(F32), axis=1, keepdims=True) - 1.0
     token_range = lax.broadcasted_iota(I32, (spread.shape[0], tok_dev), 1).astype(F32)
-    hot = (token_range == token).astype(F32)
-    select = hot.astype(BF16)
-    select_ref[...] = select
-    turned_ref[...] = hot.T.astype(BF16)
-    out_ref[...] = dot_nn(select, tokens_ref[...]).astype(BF16)
+    return (token_range == token).astype(F32)
+
+
+def send_kernel(most, base_ref, picks_ref, tokens_ref, cotangent_ref, out_ref):
+    tok_dev, width = tokens_ref.shape
+    select = select_matrix(most, tok_dev, base_ref, picks_ref).astype(BF16)
+    out_ref[:, :width] = dot_nn(select, tokens_ref[...]).astype(BF16)
+    out_ref[:, width:] = dot_nn(select, cotangent_ref[...]).astype(BF16)
+
+
+def collect_matrix_kernel(most, base_ref, picks_ref, out_ref):
+    out_ref[...] = select_matrix(most, out_ref.shape[0], base_ref, picks_ref).T.astype(BF16)
 
 
 def gather_kernel(select_ref, tokens_ref, out_ref):
@@ -161,59 +170,66 @@
     turned_ref[...] = hot.T.astype(BF16)
 
 
-def compact_kernel(chips, place_ref, take_ref, arrived_ref, scale_ref, full_ref, keep_ref, give_ref):
+def compact_kernel(
+    chips, place_ref, take_ref, arrived_ref, scale_ref,
+    rows_ref, rows_keep, rows_give, grads_ref, scaled_keep, scaled_give,
+):
     chip, core = place_ref[0], place_ref[1]
-    block = arrived_ref.shape[1] // (2 * chips)
+    width = rows_ref.shape[1]
+    block = width // (2 * chips)
     for k in range(chips):
         columns = slice(2 * k * block, 2 * (k + 1) * block)
-        value = dot_nn(take_ref[...], arrived_ref[:, columns])
-        full_ref[:, columns] = value.astype(BF16)
-        if scale_ref is not None:
-            value = value * scale_ref[...]
-        even, odd = value[:, :block], value[:, block:]
         where = pl.ds(pl.multiple_of(lax.rem(k - chip + chips, chips) * block, block), block)
-
-        keep_ref[:, where] = jnp.where(core == 0, even, odd).astype(BF16)
-        give_ref[:, where] = jnp.where(core == 0, odd, even).astype(BF16)
-
-
-def plain_compact_kernel(chips, place_ref, take_ref, arrived_ref, full_ref, keep_ref, give_ref):
-    compact_kernel(chips, place_ref, take_ref, arrived_ref, None, full_ref, keep_ref, give_ref)
-
-
-def grad_kernel(
-    tile, grads_ref, down_ref, gate_ref, hidden_ref, slope_ref, activated_ref, pre_ref, slot_ref
+        rows = dot_nn(take_ref[...], arrived_ref[:, columns])
+        behind = slice(width + 2 * k * block, width + 2 * (k + 1) * block)
+        grads = dot_nn(take_ref[...], arrived_ref[:, behind])
+        rows_ref[:, columns] = rows.astype(BF16)
+        grads_ref[:, columns] = grads.astype(BF16)
+        for value, keep_ref, give_ref in (
+            (rows, rows_keep, rows_give), (grads * scale_ref[...], scaled_keep, scaled_give)
+        ):
+            even, odd = value[:, :block], value[:, block:]
+            keep_ref[:, where] = jnp.where(core == 0, even, odd).astype(BF16)
+            give_ref[:, where] = jnp.where(core == 0, odd, even).astype(BF16)
+
+
+def expert_kernel(
+    rows_ref, grads_ref, scale_ref, gate_ref, up_ref, down_ref, gate_grad, up_grad, hidden_ref, slot_ref
 ):
-    hidden_width = down_ref.shape[0]
-    total = jnp.zeros(slot_ref.shape, F32)
-    for begin in range(0, hidden_width, tile):
-        columns = slice(begin, begin + tile)
-        raw = dot_nt(grads_ref[...], down_ref[columns, :])
-        total = total + jnp.sum(raw * hidden_ref[:, columns].astype(F32), axis=1, keepdims=True)
-        scaled = raw * gate_ref[...]
-        pre_ref[:, columns] = (scaled * slope_ref[:, columns]).astype(BF16)
-        other = slice(hidden_width + begin, hidden_width + begin + tile)
-        pre_ref[:, other] = (scaled * activated_ref[:, columns]).astype(BF16)
-    slot_ref[...] = total
-
-
-def return_kernel(tile, pre_ref, gate_ref, up_ref, turned_ref, out_ref):
-    width, hidden_width = gate_ref.shape
-    for begin in range(0, width, tile):
-        columns = slice(begin, begin + tile)
-        row_grads = dot_nt(pre_ref[:, :hidden_width], gate_ref[columns, :]) + dot_nt(
-            pre_ref[:, hidden_width:], up_ref[columns, :]
-        )
-        out_ref[:, columns] = dot_nn(turned_ref[...], row_grads.astype(BF16)).astype(BF16)
-
-
-def call(kernel, out_shapes, in_specs, operands, limit_mib, flops, bytes_accessed, grid=()):
+    @pl.when(pl.program_id(0) == 0)
+    def _():
+        slot_ref[...] = jnp.zeros(slot_ref.shape, F32)
+
+    gate_pre = dot_nn(rows_ref[...], gate_ref[...])
+    up_pre = dot_nn(rows_ref[...], up_ref[...])
+    raw = dot_nt(grads_ref[...], down_ref[...])
+    sigmoid_gate = jax.nn.sigmoid(gate_pre)
+    activated = gate_pre * sigmoid_gate
+    hidden = (activated * up_pre).astype(BF16)
+    hidden_ref[...] = hidden
+    slot_ref[...] += jnp.sum(raw * hidden.astype(F32), axis=1, keepdims=True)
+    scaled = raw * scale_ref[...]
+    slope = up_pre * sigmoid_gate * (1.0 + gate_pre * (1.0 - sigmoid_gate))
+    gate_grad[...] = (scaled * slope).astype(BF16)
+    up_grad[...] = (scaled * activated).astype(BF16)
+
+
+def return_kernel(gate_grad, up_grad, turned_ref, gate_ref, up_ref, out_ref):
+    row_grads = dot_nt(gate_grad[...], gate_ref[...]) + dot_nt(up_grad[...], up_ref[...])
+    out_ref[...] = dot_nn(turned_ref[...], row_grads.astype(BF16)).astype(BF16)
+
+
+def call(
+    kernel, out_shapes, in_specs, operands, limit_mib, flops, bytes_accessed, grid=(), out_specs=None
+):
+    if out_specs is None:
+        out_specs = jax.tree.map(lambda _: VMEM, out_shapes)
     return pl.pallas_call(
         kernel,
         grid=grid,
         out_shape=out_shapes,
         in_specs=in_specs,
-        out_specs=jax.tree.map(lambda _: VMEM, out_shapes),
+        out_specs=out_specs,
         compiler_params=pltpu.CompilerParams(vmem_limit_bytes=limit_mib * 2**20),
         cost_estimate=pl.CostEstimate(
             flops=flops, bytes_accessed=bytes_accessed, transcendentals=0
@@ -240,75 +256,61 @@
 
     table = picks[0]
     base = (self_index * tok_dev).astype(I32).reshape(1)
-    select, select_turned, out_rows = call(
-        lambda *refs: select_kernel(most, *refs),
-        (shape(padded, tok_dev), shape(tok_dev, padded), shape(padded, width)),
-        [SMEM, VMEM, VMEM],
-        (base, table, tokens),
-        16, 2 * padded * tok_dev * width, 4 * padded * width,
-    )
-    out_grads = call(
-        gather_kernel,
-        shape(padded, width),
-        [VMEM, VMEM],
-        (select, cotangent),
-        16, 2 * padded * tok_dev * width, 4 * padded * width,
+    gate_rows = gates.reshape(slot_count, 1)
+    outgoing = call(
+        functools.partial(send_kernel, most),
+        shape(padded, 2 * width),
+        [SMEM, VMEM, VMEM, VMEM],
+        (base, table, tokens, cotangent),
+        12, 4 * padded * tok_dev * width, 8 * padded * width,
     )
 
     def exchange(array):
-        shaped = array.reshape(node_count, most, width)
-        return lax.all_to_all(shaped, "expert", 0, 0, tiled=True).reshape(padded, width)
-
-    arrived_rows = exchange(out_rows)
-    arrived_grads = exchange(out_grads)
+        shaped = array.reshape(node_count, most, array.shape[1])
+        return lax.all_to_all(shaped, "expert", 0, 0, tiled=True).reshape(array.shape)
+
+    arrived = exchange(outgoing)
 
     own = lax.dynamic_index_in_dim(table, self_index, 0, keepdims=False)
     take, take_turned = call(
-        lambda *refs: take_kernel(most, tok_dev, *refs),
+        functools.partial(take_kernel, most, tok_dev),
         (shape(slot_count, padded), shape(padded, slot_count)),
         [VMEM],
         (own.reshape(slot_count, 1),),
         8, 8 * slot_count * padded, 2 * slot_count * padded,
     )
-    compact_shapes = (
-        shape(slot_count, width), shape(slot_count, width // 2), shape(slot_count, width // 2)
-    )
-    compact_cost = (12, 2 * slot_count * padded * width, 8 * slot_count * width)
-    rows, rows_keep, rows_give = call(
-        lambda *refs: plain_compact_kernel(chips, *refs),
-        compact_shapes,
-        [SMEM, VMEM, VMEM],
-        (place, take, arrived_rows),
-        *compact_cost,
-    )
+    select_turned = call(
+        functools.partial(collect_matrix_kernel, most),
+        shape(tok_dev, padded),
+        [SMEM, VMEM],
+        (base, table),
+        8, 8 * slot_count * padded, 2 * slot_count * padded,
+    )
+    whole, part = shape(slot_count, width), shape(slot_count, width // 2)
+    rows, rows_keep, rows_give, grads, scaled_keep, scaled_give = call(
+        functools.partial(compact_kernel, chips),
+        (whole, part, part, whole, part, part),
+        [SMEM, VMEM, VMEM, VMEM],
+        (place, take, arrived, gate_rows),
+        16, 4 * slot_count * padded * width, 16 * slot_count * width,
+    )
+    tile = min(256, hidden_width)
+    narrow = shape(slot_count, hidden_width)
+    across = pl.BlockSpec((width, tile), lambda step: (0, step))
+    result = pl.BlockSpec((slot_count, tile), lambda step: (0, step))
+    gate_pre_grad, up_pre_grad, hidden, slot_grads = call(
+        expert_kernel,
+        (narrow, narrow, narrow, shape(slot_count, 1, dtype=F32)),
+        [VMEM, VMEM, VMEM, across, across, pl.BlockSpec((tile, width), lambda step: (step, 0))],
+        (rows, grads, gate_rows, w_gate[0], w_up[0], w_down[0]),
+        52, 6 * slot_count * width * hidden_width, 6 * width * hidden_width,
+        (hidden_width // tile,),
+        (result, result, result, VMEM),
+    )
+    pre_grads = jnp.concatenate([gate_pre_grad, up_pre_grad], axis=1)
     rows_both = jnp.concatenate([rows_keep, swap_cores(rows_give)], axis=0)
-    gate_pre = dot_nn(rows, w_gate[0])
-    up_pre = dot_nn(rows, w_up[0])
-    sigmoid_gate = jax.nn.sigmoid(gate_pre)
-    activated = gate_pre * sigmoid_gate
-    slope = up_pre * sigmoid_gate * (1.0 + gate_pre * (1.0 - sigmoid_gate))
-    hidden = (activated * up_pre).astype(BF16)
+    scaled_both = jnp.concatenate([scaled_keep, swap_cores(scaled_give)], axis=0)
     hidden_both = jnp.concatenate([hidden, swap_cores(hidden)], axis=0)
-
-    gate_rows = gates.reshape(slot_count, 1)
-    arrived_grads, hidden, slope, activated, rows_both, hidden_both = lax.optimization_barrier(
-        (arrived_grads, hidden, slope, activated, rows_both, hidden_both)
-    )
-    grads, scaled_keep, scaled_give = call(
-        lambda *refs: compact_kernel(chips, *refs),
-        compact_shapes,
-        [SMEM, VMEM, VMEM, VMEM],
-        (place, take, arrived_grads, gate_rows),
-        *compact_cost,
-    )
-    scaled_both = jnp.concatenate([scaled_keep, swap_cores(scaled_give)], axis=0)
-    pre_grads, slot_grads = call(
-        lambda *refs: grad_kernel(min(256, hidden_width), *refs),
-        (shape(slot_count, 2 * hidden_width), shape(slot_count, 1, dtype=F32)),
-        [VMEM] * 6,
-        (grads, w_down[0], gate_rows, hidden, slope, activated),
-        16, 2 * slot_count * width * hidden_width, 2 * width * hidden_width,
-    )
     pre_both = jnp.concatenate([pre_grads, swap_cores(pre_grads)], axis=0)
 
     def parts_of(columns):
@@ -317,13 +319,18 @@
             dot_tn(scaled_both[:, columns], hidden_both).astype(BF16),
         )
 
-    def give_back(pre_grads):
+    row_tile = min(256, width)
+    wide = pl.BlockSpec((row_tile, hidden_width), lambda step: (step, 0))
+
+    def give_back(gate_pre_grad, up_pre_grad):
         return call(
-            lambda *refs: return_kernel(min(256, width), *refs),
+            return_kernel,
             shape(padded, width),
-            [VMEM] * 4,
-            (pre_grads, w_gate[0], w_up[0], take_turned),
-            16, 4 * slot_count * width * hidden_width, 4 * width * hidden_width,
+            [VMEM, VMEM, VMEM, wide, wide],
+            (gate_pre_grad, up_pre_grad, take_turned, w_gate[0], w_up[0]),
+            12, 4 * slot_count * width * hidden_width, 4 * width * hidden_width,
+            (width // row_tile,),
+            pl.BlockSpec((padded, row_tile), lambda step: (0, step)),
         )
 
     def collect(came_back):
@@ -340,7 +347,9 @@
         far = parts_of(slice(farthest * block, (farthest + 1) * block))
         parts = parts_of(slice(None))
         sums = Sums(far, parts, block, chips)
-        returning = give_back(pre_grads)
+        held, _ = lax.optimization_barrier(((gate_pre_grad, up_pre_grad), sums.operands))
+        returning = give_back(*held)
+        sums.moving, returning = lax.optimization_barrier((sums.moving, returning))
         returned = None
         while sums.distance > 1:
             operands = sums.step()
@@ -360,7 +369,7 @@
         )
         weight_grads = sums.finish(weight_shapes, token_grads)
     else:
-        token_grads = collect(exchange(give_back(pre_grads)))
+        token_grads = collect(exchange(give_back(gate_pre_grad, up_pre_grad)))
         pre_part, down_part = parts_of(slice(None))
         weight_grads = (*(half[None] for half in jnp.split(pre_part, 2, axis=1)), down_part.T[None])
     return (token_grads, slot_grads.reshape(1, 1, slot_count), *weight_grads)

time: 137 us -> 143 us (1.044)
  waiting for transfers between devices: 51.3 us -> 64.9 us
  matrix products: 8.64 us -> 3.54 us
  Pallas kernels: 21.6 us -> 25.7 us
  other arithmetic: 4.76 us -> 0.75 us
  starting transfers between devices: 37.2 us -> 33.9 us
    all_to_all x3 -> x2, waiting for transfers between devices: 23.7 us -> 39.1 us  [exchange(): lax.all_to_all(shaped, 'expert', 0, 0, tiled=True).reshape(array.shape)]
    dot_general x2 -> x0, matrix products: 5.09 us -> none  [dot_nn(): return jnp.dot(left, right, preferred_element_type=F32)]
    pallas_call x13 -> x12, Pallas kernels: 21.6 us -> 25.7 us  [call(): pl.pallas_call(kernel, grid=grid, out_shape=out_shapes, in_specs=in_specs...]
    concatenate x2 -> x0, other arithmetic: 4.01 us -> none  [the longest x1 2.08 us: body(): rows_both = jnp.concatenate([rows_keep, swap_cores(rows_give)], axis=0)]
    all_to_all x3 -> x2, starting transfers between devices: 20 us -> 16.8 us  [exchange(): lax.all_to_all(shaped, 'expert', 0, 0, tiled=True).reshape(array.shape)]
    unnamed x42 -> x40, local copies, waits for them, and re-layouts: 10.4 us -> 10.7 us
  transfers between devices with their start and end apart: 15 -> 14, of which waited for: 8 -> 6; matrix products, arithmetic and copies ran while one was open for 10% -> 2% of each run, Pallas kernels for 11% -> 13%
where the time goes in v3:
time: 143 us; the launch traced here: 141 us
  waiting for transfers between devices  64.9 us (45%)
  starting transfers between devices  33.9 us (24%)
  Pallas kernels  25.7 us (18%)
  local copies, waits for them, and re-layouts  11.1 us (8%)
  matrix products  3.54 us (2%)
    all_to_all x2, waiting for transfers between devices, exchange(): lax.all_to_all(shaped, 'expert', 0, 0, tiled=True).reshape(array.shape)  39.1 us
    pallas_call x12, Pallas kernels, call(): pl.pallas_call(kernel, grid=grid, out_shape=out_shapes, in_specs=in_specs...  25.7 us
    ppermute x8, waiting for transfers between devices, next_chip(): lax.ppermute(array, 'dp', [(i, (i + 2 * sign) % size) for i in range(size)])  24.1 us
    all_to_all x2, starting transfers between devices, exchange(): lax.all_to_all(shaped, 'expert', 0, 0, tiled=True).reshape(array.shape)  16.8 us
    ppermute x8, starting transfers between devices, next_chip(): lax.ppermute(array, 'dp', [(i, (i + 2 * sign) % size) for i in range(size)])  15.8 us
    unnamed x40, local copies, waits for them, and re-layouts  10.7 us
    dot_general x4, matrix products, dot_tn(): lax.dot_general(left, right, (((0,), (0,)), ((), ())), preferred_element_...  3.54 us
  transfers between devices with their start and end apart: 14, of which 6 were waited for; matrix products, arithmetic and copies ran while one was open for 2% of the time, Pallas kernels for 13%

profile of v3, /device:TPU:2, one launch (start us, length us, event | category | flops | bytes accessed | tf_op | source)
XLA Modules:
  0.0 140.8 jit_solution(6567057026915447486)
XLA Ops:
  0.6 1.0 copy-done.9
  1.7 1.0 copy-done.10
  2.7 0.7 copy-done.15
  3.4 1.4 %shard_map.112 = bf16[384,4096]{1,0:T(8,128)(2,1)S(1)} custom-call(s32[1]{0:T(128)} %bitcast.base_ref, s32[16,256]{1,0:T(8,128)S(1)} %bitcast.26, bf16[128,2048]{1,0:T(8,128)(2,1)S(1)} %copy-done.9, bf16[128,2048]{1,0:T(8,128)(2,1)S(1)} %copy-done.10), custom_call_target="tpu_custom_call" | custom-call | flops 402653184 | bytes 6291456 | tf_op jit(solution)/shard_map/pallas_call | solution.py:227
  4.9 1.6 %copy-done.3 = bf16[384,4096]{1,0:T(8,128)(2,1)} copy-done((bf16[384,4096]{1,0:T(8,128)(2,1)}, bf16[384,4096]{1,0:T(8,128)(2,1)S(1)}, u32[]{:S(2)}) %copy-start.3) | copy-done | bytes 3145752
  6.5 7.6 %all-to-all-start = ((bf16[16,24,4096]{2,1,0:T(8,128)(2,1)}), bf16[16,24,4096]{2,1,0:T(8,128)(2,1)S(1)}, u32[]{:S(2)}, u32[]{:S(2)}) async-start(bf16[16,24,4096]{2,1,0:T(8,128)(2,1)} %bitcast.20), calls=%async_computation | async-start | bytes 6291456 | tf_op jit(solution)/shard_map/all_to_all | solution.py:270
  14.1 0.1 copy.12.own_ref
  14.3 0.1 copy.13.scale_ref
  14.4 0.3 shard_map.111
  14.7 0.7 copy-done.11
  15.4 0.7 copy-done.13
  16.2 39.1 %all-to-all-done = bf16[16,24,4096]{2,1,0:T(8,128)(2,1)S(1)} async-done(((bf16[16,24,4096]{2,1,0:T(8,128)(2,1)}), bf16[16,24,4096]{2,1,0:T(8,128)(2,1)S(1)}, u32[]{:S(2)}, u32[]{:S(2)}) %all-to-all-start) | async-done | bytes 3145760 | tf_op jit(solution)/shard_map/all_to_all | solution.py:270
  55.2 0.9 copy-done.12
  56.2 1.9 %shard_map.113 = (bf16[256,2048]{1,0:T(8,128)(2,1)S(1)}, bf16[256,1024]{1,0:T(8,128)(2,1)S(1)}, bf16[256,1024]{1,0:T(8,128)(2,1)S(1)}, bf16[256,2048]{1,0:T(8,12...) custom-call(s32[2]{0:T(128)S(1)} %pad_add_fusion.place_ref, bf16[256,384]{1,0:T(8,128)(2,1)S(1)} %copy-done.12, ...), custom_call_target="tpu_custom_call" | custom-call | flops 805306368 | bytes 8388608 | tf_op jit(solution)/shard_map/pallas_call | solution.py:227
  58.1 1.0 copy-done.8
  59.1 0.1 collective-permute-start
  59.2 0.5 collective-permute-start.2
  59.7 0.3 copy-done.7
  60.1 7.1 %shard_map.114 = (bf16[256,768]{1,0:T(8,128)(2,1)S(1)}, bf16[256,768]{1,0:T(8,128)(2,1)S(1)}, bf16[256,768]{1,0:T(8,128)(2,1)S(1)}, f32[256,1]{1,0:T(8,128)S(1)}) custom-call(bf16[256,2048]{1,0:T(8,128)(2,1)} %copy-done.7, bf16[256,2048]{1,0:T(8,128)(2,1)} %copy-done.8, f32[256,1]{1,0:T(8,128)S(1)} %copy.13.scale_ref, bf16[2048,768]{1,0:T(8,128)(2,1)} %bitcast.21, ...), custom_call_target="tpu_custom_call" | custom-call | flops 2415919104 | bytes 9437184 | tf_op jit(solution)/shard_map/pallas_call | solution.py:227
  67.2 0.1 collective-permute-start.3
  67.3 0.6 collective-permute-start.1
  68.0 1.0 collective-permute-done.3
  69.1 0.3 convolution_convert_fusion.3.down_ref
  69.4 0.7 collective-permute-done.1
  70.1 0.4 convolution_convert_fusion.1.pre_ref
  70.5 1.0 convolution_convert_fusion.2.down_front.down_back.down_ref
  71.6 2.0 %collective-permute-start.4 = (bf16[64,2304]{1,0:T(8,128)(2,1)S(1)}, bf16[64,2304]{1,0:T(8,128)(2,1)S(1)}, u32[]{:S(2)}, u32[]{:S(2)}) collective-permute-start(bf16[64,2304]{1,0:T(8,128)(2,1)S(1)} %get-tuple-element.47), channel_id=1, source_target_pairs={{0,32},{16,48},{32,64},{48,80},{64,96},{80,112},{96,128},{112,144}... | collective-permute-start | bytes 884744 | tf_op jit(solution)/shard_map/ppermute | solution.py:36
  73.6 4.0 %collective-permute-start.5 = (bf16[64,2304]{1,0:T(8,128)(2,1)S(1)}, bf16[64,2304]{1,0:T(8,128)(2,1)S(1)}, u32[]{:S(2)}, u32[]{:S(2)}) collective-permute-start(bf16[64,2304]{1,0:T(8,128)(2,1)S(1)} %get-tuple-element.48), channel_id=1, source_target_pairs={{0,224},{16,240},{32,0},{48,16},{64,32},{80,48},{96,64},{112,80},{... | collective-permute-start | bytes 884744 | tf_op jit(solution)/shard_map/ppermute | solution.py:36
  77.7 5.7 %shard_map.116 = bf16[384,2048]{1,0:T(8,128)(2,1)S(1)} custom-call(bf16[256,768]{1,0:T(8,128)(2,1)S(1)} %get-tuple-element.49.gate_grad, bf16[256,768]{1,0:T(8,128)(2,1)S(1)} %get-tuple-element.50.up_grad, bf16[384,256]{1,0:T(8,128)(2,1)S(1)} %copy-done.14, bf16[2048,768]{1,0:T(8,128)(2,1)S(1)} %bitcast.22, bf16[2048,768]{1,0:T(8,128)(2,1)S(1)} %bitcast.24), custom_call_target="tpu_custom_call" | custom-call | flops 1610612736 | bytes 6291456 | tf_op jit(solution)/shard_map/pallas_call | solution.py:227
  83.4 1.1 copy-done.6
  84.5 1.8 %convolution_convert_fusion.pre_front.pre_back.pre_ref = bf16[1024,1536]{1,0:T(8,128)(2,1)S(1)} fusion(bf16[512,1024]{1,0:T(8,128)(2,1)S(1)} %constant_dynamic-update-slice_fusion, bf16[256,1536]{1,0:T(8,128)(2,1)S(1)} %collective-permute-done.1, bf16[256,1536]{1,0:T(8,128)(2,1)S(1)} %constant_dynamic-update-slice_fusion.2), kind=kOutput, calls=%fused_computation | convolution fusion | flops 1615331328 | bytes 5767168 | tf_op jit(solution)/shard_map/dot_general | solution.py:26
  86.4 1.2 shard_map.117
  87.5 3.2 %collective-permute-start.7 = (bf16[128,2304]{1,0:T(8,128)(2,1)}, bf16[128,2304]{1,0:T(8,128)(2,1)}, u32[]{:S(2)}, u32[]{:S(2)}) collective-permute-start(bf16[128,2304]{1,0:T(8,128)(2,1)} %get-tuple-element.56), channel_id=1, source_target_pairs={{0,224},{16,240},{32,0},{48,16},{64,32},{80,48},{96,64},{112,80},{... | collective-permute-start | bytes 1769480 | tf_op jit(solution)/shard_map/ppermute | solution.py:36
  90.8 9.2 %all-to-all-start.1 = ((bf16[16,24,2048]{2,1,0:T(8,128)(2,1)}), bf16[16,24,2048]{2,1,0:T(8,128)(2,1)}, u32[]{:S(2)}, u32[]{:S(2)}) async-start(bf16[16,24,2048]{2,1,0:T(8,128)(2,1)} %bitcast.25), calls=%async_computation.1 | async-start | bytes 3145728 | tf_op jit(solution)/shard_map/all_to_all | solution.py:270
  100.0 4.2 %collective-permute-done.6.forward_ref = bf16[128,2304]{1,0:T(8,128)(2,1)} collective-permute-done((bf16[128,2304]{1,0:T(8,128)(2,1)}, bf16[128,2304]{1,0:T(8,128)(2,1)}, u32[]{:S(2)}, u32[]{:S(2)}) %collective-permute-start.6) | collective-permute-done | bytes 589856 | tf_op jit(solution)/shard_map/ppermute | solution.py:36
  104.1 1.4 copy-done.1
  105.5 1.5 %shard_map.118 = (bf16[128,2304]{1,0:T(8,128)(2,1)S(1)}, bf16[128,2304]{1,0:T(8,128)(2,1)S(1)}) custom-call(bf16[128,2304]{1,0:T(8,128)(2,1)} %collective-permute-done.6.forward_ref, bf16[128,2304]{1,0:T(8,128)(2,1)} %collective-permute-done.7.backward_ref, bf16[1024,1536]{1,0:T(8,128)(2,1)S(1)} %convolution_convert_fusion.pre_front.pre_back.pre_ref, ...), custom_call_target="tpu_custom_call" | custom-call | flops 1 | bytes 1 | tf_op jit(solution)/shard_map/pallas_call | solution.py:227
  107.1 0.2 collective-permute-start.8
  107.2 3.2 %collective-permute-start.9 = (bf16[128,2304]{1,0:T(8,128)(2,1)S(1)}, bf16[128,2304]{1,0:T(8,128)(2,1)S(1)}, u32[]{:S(2)}, u32[]{:S(2)}) collective-permute-start(bf16[128,2304]{1,0:T(8,128)(2,1)S(1)} %get-tuple-element.59), channel_id=1, source_target_pairs={{0,224},{16,240},{32,0},{48,16},{64,32},{80,48},{96,64},{112,80},{... | collective-permute-start | bytes 1769480 | tf_op jit(solution)/shard_map/ppermute | solution.py:36
  110.4 12.2 %collective-permute-done.8.forward_ref = bf16[128,2304]{1,0:T(8,128)(2,1)S(1)} collective-permute-done((bf16[128,2304]{1,0:T(8,128)(2,1)S(1)}, bf16[128,2304]{1,0:T(8,128)(2,1)S(1)}, u32[]{:S(2)}, u32[]{:S(2)}) %collective-permute-start.8) | collective-permute-done | bytes 589856 | tf_op jit(solution)/shard_map/ppermute | solution.py:36
  122.6 1.2 shard_map.119
  123.7 1.7 %collective-permute-start.10 = (bf16[128,2304]{1,0:T(8,128)(2,1)}, bf16[128,2304]{1,0:T(8,128)(2,1)}, u32[]{:S(2)}, u32[]{:S(2)}) collective-permute-start(bf16[128,2304]{1,0:T(8,128)(2,1)} %get-tuple-element.60), channel_id=1, source_target_pairs={{0,32},{16,48},{32,64},{48,80},{64,96},{80,112},{96,128},{112,144}... | collective-permute-start | bytes 1769480 | tf_op jit(solution)/shard_map/ppermute | solution.py:36
  125.5 1.5 %collective-permute-start.11 = (bf16[128,2304]{1,0:T(8,128)(2,1)}, bf16[128,2304]{1,0:T(8,128)(2,1)}, u32[]{:S(2)}, u32[]{:S(2)}) collective-permute-start(bf16[128,2304]{1,0:T(8,128)(2,1)} %get-tuple-element.61), channel_id=1, source_target_pairs={{0,224},{16,240},{32,0},{48,16},{64,32},{80,48},{96,64},{112,80},{... | collective-permute-start | bytes 1769480 | tf_op jit(solution)/shard_map/ppermute | solution.py:36
  127.0 0.4 shard_map.110.select_ref
  127.3 0.7 reduce
  128.0 2.8 %shard_map.120 = bf16[128,2048]{1,0:T(8,128)(2,1)} custom-call(bf16[128,384]{1,0:T(8,128)(2,1)S(1)} %shard_map.110.select_ref, bf16[384,2048]{1,0:T(8,128)(2,1)} %bitcast.12.tokens_ref), custom_call_target="tpu_custom_call" | custom-call | flops 201326592 | bytes 3145728 | tf_op jit(solution)/shard_map/pallas_call | solution.py:227
  130.8 7.7 %collective-permute-done.10.forward_ref = bf16[128,2304]{1,0:T(8,128)(2,1)} collective-permute-done((bf16[128,2304]{1,0:T(8,128)(2,1)}, bf16[128,2304]{1,0:T(8,128)(2,1)}, u32[]{:S(2)}, u32[]{:S(2)}) %collective-permute-start.10) | collective-permute-done | bytes 589856 | tf_op jit(solution)/shard_map/ppermute | solution.py:36
  138.5 2.3 %shard_map.121 = (bf16[1,128,768]{2,1,0:T(8,128)(2,1)}, bf16[1,128,768]{2,1,0:T(8,128)(2,1)}, bf16[1,768,128]{2,1,0:T(8,128)(2,1)}) custom-call(bf16[128,2304]{1,0:T(8,128)(2,1)} %collective-permute-done.10.forward_ref, bf16[128,2304]{1,0:T(8,128)(2,1)} %collective-permute-done.11.backward_ref, ...), custom_call_target="tpu_custom_call" | custom-call | flops 1 | bytes 1 | tf_op jit(solution)/shard_map/pallas_call | solution.py:227
  (45 shorter events, 0.5 us)
Async XLA Ops:
  0.6 1.0 copy-start.9
  1.7 1.0 copy-start.10
  2.7 0.7 copy-start.15
  4.9 1.6 %copy-start.3 = (bf16[384,4096]{1,0:T(8,128)(2,1)}, bf16[384,4096]{1,0:T(8,128)(2,1)S(1)}, u32[]{:S(2)}) copy-start(bf16[384,4096]{1,0:T(8,128)(2,1)S(1)} %shard_map.112) | copy-start | bytes 9437188
  6.5 7.6 %copy-start.16 = (s32[1,16,256]{2,1,0:T(8,128)S(1)}, s32[1,16,256]{2,1,0:T(8,128)}, u32[]{:S(2)}) copy-start(s32[1,16,256]{2,1,0:T(8,128)} %param.9) | copy-start | bytes 49156
  6.5 7.8 %copy-start.17 = (f32[1,1,256]{2,1,0:T(1,128)S(1)}, f32[1,1,256]{2,1,0:T(1,128)}, u32[]{:S(2)}) copy-start(f32[1,1,256]{2,1,0:T(1,128)} %param.10) | copy-start | bytes 3076
  6.5 48.7 %all-to-all-start = ((bf16[16,24,4096]{2,1,0:T(8,128)(2,1)}), bf16[16,24,4096]{2,1,0:T(8,128)(2,1)S(1)}, u32[]{:S(2)}, u32[]{:S(2)}) async-start(bf16[16,24,4096]{2,1,0:T(8,128)(2,1)} %bitcast.20), calls=%async_computation | async-start | bytes 6291456 | tf_op jit(solution)/shard_map/all_to_all | solution.py:270
  14.7 0.7 copy-start.11
  15.4 0.7 copy-start.13
  55.2 0.9 copy-start.12
  58.1 1.0 copy-start.8
  59.1 1.0 copy-start.7
  59.1 9.9 %collective-permute-start = (bf16[256,1024]{1,0:T(8,128)(2,1)S(1)}, bf16[256,1024]{1,0:T(8,128)(2,1)S(1)}, u32[]{:S(2)}, u32[]{:S(2)}) collective-permute-start(bf16[256,1024]{1,0:T(8,128)(2,1)S(1)} %get-tuple-element.39), channel_id=1, source_target_pairs={{0,16},{16,0},{32,48},{48,32},{64,80},{80,64},{96,112},{112,96},{1... | collective-permute-start | bytes 1572872 | tf_op jit(solution)/shard_map/ppermute | solution.py:31
  59.2 9.8 %collective-permute-start.2 = (bf16[256,1024]{1,0:T(8,128)(2,1)S(1)}, bf16[256,1024]{1,0:T(8,128)(2,1)S(1)}, u32[]{:S(2)}, u32[]{:S(2)}) collective-permute-start(bf16[256,1024]{1,0:T(8,128)(2,1)S(1)} %get-tuple-element.45), channel_id=1, source_target_pairs={{0,16},{16,0},{32,48},{48,32},{64,80},{80,64},{96,112},{112,96},{1... | collective-permute-start | bytes 1572872 | tf_op jit(solution)/shard_map/ppermute | solution.py:31
  67.2 1.8 %collective-permute-start.3 = (bf16[256,768]{1,0:T(8,128)(2,1)S(1)}, bf16[256,768]{1,0:T(8,128)(2,1)S(1)}, u32[]{:S(2)}, u32[]{:S(2)}) collective-permute-start(bf16[256,768]{1,0:T(8,128)(2,1)S(1)} %get-tuple-element.46), channel_id=1, source_target_pairs={{0,16},{16,0},{32,48},{48,32},{64,80},{80,64},{96,112},{112,96},{1... | collective-permute-start | bytes 1179656 | tf_op jit(solution)/shard_map/ppermute | solution.py:31
  67.3 2.8 %collective-permute-start.1 = (bf16[256,1536]{1,0:T(8,128)(2,1)S(1)}, bf16[256,1536]{1,0:T(8,128)(2,1)S(1)}, u32[]{:S(2)}, u32[]{:S(2)}) collective-permute-start(bf16[256,1536]{1,0:T(8,128)(2,1)S(1)} %constant_dynamic-update-slice_fusion.2), channel_id=1, source_target_pairs={{0,16},{16,0},{32,48},{48,32},{64,80},{80,64},{96,112},{112,96},{1... | collective-permute-start | bytes 2359304 | tf_op jit(solution)/shard_map/ppermute | solution.py:31
  70.5 7.2 %copy-start.4 = (bf16[1,2048,768]{2,1,0:T(8,128)(2,1)S(1)}, bf16[1,2048,768]{2,1,0:T(8,128)(2,1)}, u32[]{:S(2)}) copy-start(bf16[1,2048,768]{2,1,0:T(8,128)(2,1)} %param.11) | copy-start | bytes 9437188
  70.5 7.1 %copy-start.5 = (bf16[1,2048,768]{2,1,0:T(8,128)(2,1)S(1)}, bf16[1,2048,768]{2,1,0:T(8,128)(2,1)}, u32[]{:S(2)}) copy-start(bf16[1,2048,768]{2,1,0:T(8,128)(2,1)} %param.12) | copy-start | bytes 9437188
  70.5 7.1 %copy-start.14 = (bf16[384,256]{1,0:T(8,128)(2,1)S(1)}, bf16[384,256]{1,0:T(8,128)(2,1)}, u32[]{:S(2)}) copy-start(bf16[384,256]{1,0:T(8,128)(2,1)} %copy-done.13) | copy-start | bytes 589828
  71.6 14.8 %copy-start = (bf16[1024,768]{1,0:T(8,128)(2,1)}, bf16[1024,768]{1,0:T(8,128)(2,1)S(1)}, u32[]{:S(2)}) copy-start(bf16[1024,768]{1,0:T(8,128)(2,1)S(1)} %convolution_convert_fusion.2.down_front.down_back.down_ref) | copy-start | bytes 4718596
  71.6 14.7 %collective-permute-start.4 = (bf16[64,2304]{1,0:T(8,128)(2,1)S(1)}, bf16[64,2304]{1,0:T(8,128)(2,1)S(1)}, u32[]{:S(2)}, u32[]{:S(2)}) collective-permute-start(bf16[64,2304]{1,0:T(8,128)(2,1)S(1)} %get-tuple-element.47), channel_id=1, source_target_pairs={{0,32},{16,48},{32,64},{48,80},{64,96},{80,112},{96,128},{112,144}... | collective-permute-start | bytes 884744 | tf_op jit(solution)/shard_map/ppermute | solution.py:36
  73.6 12.7 %collective-permute-start.5 = (bf16[64,2304]{1,0:T(8,128)(2,1)S(1)}, bf16[64,2304]{1,0:T(8,128)(2,1)S(1)}, u32[]{:S(2)}, u32[]{:S(2)}) collective-permute-start(bf16[64,2304]{1,0:T(8,128)(2,1)S(1)} %get-tuple-element.48), channel_id=1, source_target_pairs={{0,224},{16,240},{32,0},{48,16},{64,32},{80,48},{96,64},{112,80},{... | collective-permute-start | bytes 884744 | tf_op jit(solution)/shard_map/ppermute | solution.py:36
  83.4 1.1 copy-start.6
  87.5 16.6 %collective-permute-start.6 = (bf16[128,2304]{1,0:T(8,128)(2,1)}, bf16[128,2304]{1,0:T(8,128)(2,1)}, u32[]{:S(2)}, u32[]{:S(2)}) collective-permute-start(bf16[128,2304]{1,0:T(8,128)(2,1)} %get-tuple-element.55), channel_id=1, source_target_pairs={{0,32},{16,48},{32,64},{48,80},{64,96},{80,112},{96,128},{112,144}... | collective-permute-start | bytes 1769480 | tf_op jit(solution)/shard_map/ppermute | solution.py:36
  87.5 16.6 %collective-permute-start.7 = (bf16[128,2304]{1,0:T(8,128)(2,1)}, bf16[128,2304]{1,0:T(8,128)(2,1)}, u32[]{:S(2)}, u32[]{:S(2)}) collective-permute-start(bf16[128,2304]{1,0:T(8,128)(2,1)} %get-tuple-element.56), channel_id=1, source_target_pairs={{0,224},{16,240},{32,0},{48,16},{64,32},{80,48},{96,64},{112,80},{... | collective-permute-start | bytes 1769480 | tf_op jit(solution)/shard_map/ppermute | solution.py:36
  90.8 37.3 %all-to-all-start.1 = ((bf16[16,24,2048]{2,1,0:T(8,128)(2,1)}), bf16[16,24,2048]{2,1,0:T(8,128)(2,1)}, u32[]{:S(2)}, u32[]{:S(2)}) async-start(bf16[16,24,2048]{2,1,0:T(8,128)(2,1)} %bitcast.25), calls=%async_computation.1 | async-start | bytes 3145728 | tf_op jit(solution)/shard_map/all_to_all | solution.py:270
  104.1 1.4 %copy-start.1 = (bf16[1024,768]{1,0:T(8,128)(2,1)S(1)}, bf16[1024,768]{1,0:T(8,128)(2,1)}, u32[]{:S(2)}) copy-start(bf16[1024,768]{1,0:T(8,128)(2,1)} %copy-done) | copy-start | bytes 4718596
  107.1 15.5 %collective-permute-start.8 = (bf16[128,2304]{1,0:T(8,128)(2,1)S(1)}, bf16[128,2304]{1,0:T(8,128)(2,1)S(1)}, u32[]{:S(2)}, u32[]{:S(2)}) collective-permute-start(bf16[128,2304]{1,0:T(8,128)(2,1)S(1)} %get-tuple-element.58), channel_id=1, source_target_pairs={{0,32},{16,48},{32,64},{48,80},{64,96},{80,112},{96,128},{112,144}... | collective-permute-start | bytes 1769480 | tf_op jit(solution)/shard_map/ppermute | solution.py:36
  107.2 15.3 %collective-permute-start.9 = (bf16[128,2304]{1,0:T(8,128)(2,1)S(1)}, bf16[128,2304]{1,0:T(8,128)(2,1)S(1)}, u32[]{:S(2)}, u32[]{:S(2)}) collective-permute-start(bf16[128,2304]{1,0:T(8,128)(2,1)S(1)} %get-tuple-element.59), channel_id=1, source_target_pairs={{0,224},{16,240},{32,0},{48,16},{64,32},{80,48},{96,64},{112,80},{... | collective-permute-start | bytes 1769480 | tf_op jit(solution)/shard_map/ppermute | solution.py:36
  123.7 14.8 %collective-permute-start.10 = (bf16[128,2304]{1,0:T(8,128)(2,1)}, bf16[128,2304]{1,0:T(8,128)(2,1)}, u32[]{:S(2)}, u32[]{:S(2)}) collective-permute-start(bf16[128,2304]{1,0:T(8,128)(2,1)} %get-tuple-element.60), channel_id=1, source_target_pairs={{0,32},{16,48},{32,64},{48,80},{64,96},{80,112},{96,128},{112,144}... | collective-permute-start | bytes 1769480 | tf_op jit(solution)/shard_map/ppermute | solution.py:36
  125.5 13.1 %collective-permute-start.11 = (bf16[128,2304]{1,0:T(8,128)(2,1)}, bf16[128,2304]{1,0:T(8,128)(2,1)}, u32[]{:S(2)}, u32[]{:S(2)}) collective-permute-start(bf16[128,2304]{1,0:T(8,128)(2,1)} %get-tuple-element.61), channel_id=1, source_target_pairs={{0,224},{16,240},{32,0},{48,16},{64,32},{80,48},{96,64},{112,80},{... | collective-permute-start | bytes 1769480 | tf_op jit(solution)/shard_map/ppermute | solution.py:36
  128.0 10.5 %copy-start.2 = (bf16[1024,768]{1,0:T(8,128)(2,1)S(1)}, bf16[1024,768]{1,0:T(8,128)(2,1)}, u32[]{:S(2)}) copy-start(bf16[1024,768]{1,0:T(8,128)(2,1)} %copy-done) | copy-start | bytes 4718596

commit v4 on v2

--- a/solution.py
+++ b/solution.py
@@ -1,3 +1,5 @@
+import functools
+
 import jax
 import jax.numpy as jnp
 from jax import lax
@@ -104,7 +106,7 @@
             (out, out),
             [VMEM, VMEM, *self.specs(self.distance), *self.specs(-self.distance)],
             (*self.moving, *self.parts, *self.parts),
-            12, 1, 1, (1,),
+            40, 1, 1, (1,),
         )
 
     def finish(self, out_shapes, after):
@@ -114,14 +116,13 @@
             out_shapes,
             [VMEM, VMEM, *self.specs(0)],
             (*arrived, *self.parts),
-            12, 1, 1, (1,),
-        )
-
-
-def select_kernel(most, base_ref, picks_ref, tokens_ref, select_ref, turned_ref, out_ref):
+            40, 1, 1, (1,),
+        )
+
+
+def select_matrix(most, tok_dev, base_ref, picks_ref):
     local = picks_ref[...] - base_ref[0]
     experts, slots = local.shape
-    tok_dev = tokens_ref.shape[0]
     below = jnp.sum((local < 0).astype(F32), axis=1, keepdims=True).astype(I32)
     counter = lax.broadcasted_iota(I32, (most, 1), 0)
     spread = jnp.concatenate(
@@ -132,11 +133,17 @@
     hit = (position == wanted) & (spread >= 0) & (spread < tok_dev)
     token = jnp.sum(jnp.where(hit, spread + 1, 0).astype(F32), axis=1, keepdims=True) - 1.0
     token_range = lax.broadcasted_iota(I32, (spread.shape[0], tok_dev), 1).astype(F32)
-    hot = (token_range == token).astype(F32)
-    select = hot.astype(BF16)
+    return (token_range == token).astype(F32)
+
+
+def select_kernel(most, base_ref, picks_ref, tokens_ref, select_ref, out_ref):
+    select = select_matrix(most, tokens_ref.shape[0], base_ref, picks_ref).astype(BF16)
     select_ref[...] = select
-    turned_ref[...] = hot.T.astype(BF16)
     out_ref[...] = dot_nn(select, tokens_ref[...]).astype(BF16)
+
+
+def collect_matrix_kernel(most, base_ref, picks_ref, out_ref):
+    out_ref[...] = select_matrix(most, out_ref.shape[0], base_ref, picks_ref).T.astype(BF16)
 
 
 def gather_kernel(select_ref, tokens_ref, out_ref):
@@ -197,23 +204,31 @@
     slot_ref[...] = total
 
 
-def return_kernel(tile, pre_ref, gate_ref, up_ref, turned_ref, out_ref):
+def park_kernel(array_ref, out_ref):
+    out_ref[...] = array_ref[...]
+
+
+def return_kernel(tile, pre_ref, gate_ref, up_ref, turned_ref, out_ref, held):
     width, hidden_width = gate_ref.shape
     for begin in range(0, width, tile):
         columns = slice(begin, begin + tile)
         row_grads = dot_nt(pre_ref[:, :hidden_width], gate_ref[columns, :]) + dot_nt(
             pre_ref[:, hidden_width:], up_ref[columns, :]
         )
-        out_ref[:, columns] = dot_nn(turned_ref[...], row_grads.astype(BF16)).astype(BF16)
-
-
-def call(kernel, out_shapes, in_specs, operands, limit_mib, flops, bytes_accessed, grid=()):
+        held[:, columns] = row_grads.astype(BF16)
+    for begin in range(0, width, 2 * tile):
+        columns = slice(begin, begin + 2 * tile)
+        out_ref[:, columns] = dot_nn(turned_ref[...], held[:, columns]).astype(BF16)
+
+
+def call(kernel, out_shapes, in_specs, operands, limit_mib, flops, bytes_accessed, grid=(), scratch=()):
     return pl.pallas_call(
         kernel,
         grid=grid,
         out_shape=out_shapes,
         in_specs=in_specs,
         out_specs=jax.tree.map(lambda _: VMEM, out_shapes),
+        scratch_shapes=scratch,
         compiler_params=pltpu.CompilerParams(vmem_limit_bytes=limit_mib * 2**20),
         cost_estimate=pl.CostEstimate(
             flops=flops, bytes_accessed=bytes_accessed, transcendentals=0
@@ -240,9 +255,9 @@
 
     table = picks[0]
     base = (self_index * tok_dev).astype(I32).reshape(1)
-    select, select_turned, out_rows = call(
+    select, out_rows = call(
         lambda *refs: select_kernel(most, *refs),
-        (shape(padded, tok_dev), shape(tok_dev, padded), shape(padded, width)),
+        (shape(padded, tok_dev), shape(padded, width)),
         [SMEM, VMEM, VMEM],
         (base, table, tokens),
         16, 2 * padded * tok_dev * width, 4 * padded * width,
@@ -268,6 +283,13 @@
         (shape(slot_count, padded), shape(padded, slot_count)),
         [VMEM],
         (own.reshape(slot_count, 1),),
+        8, 8 * slot_count * padded, 2 * slot_count * padded,
+    )
+    select_turned = call(
+        functools.partial(collect_matrix_kernel, most),
+        shape(tok_dev, padded),
+        [SMEM, VMEM],
+        (base, table),
         8, 8 * slot_count * padded, 2 * slot_count * padded,
     )
     compact_shapes = (
@@ -291,8 +313,17 @@
     hidden_both = jnp.concatenate([hidden, swap_cores(hidden)], axis=0)
 
     gate_rows = gates.reshape(slot_count, 1)
-    arrived_grads, hidden, slope, activated, rows_both, hidden_both = lax.optimization_barrier(
-        (arrived_grads, hidden, slope, activated, rows_both, hidden_both)
+    down_weight = call(
+        park_kernel,
+        shape(hidden_width, width),
+        [VMEM],
+        (w_down[0],),
+        8, 1, 4 * width * hidden_width,
+    )
+    arrived_grads, hidden, slope, activated, rows_both, hidden_both, down_weight = (
+        lax.optimization_barrier(
+            (arrived_grads, hidden, slope, activated, rows_both, hidden_both, down_weight)
+        )
     )
     grads, scaled_keep, scaled_give = call(
         lambda *refs: compact_kernel(chips, *refs),
@@ -306,7 +337,7 @@
         lambda *refs: grad_kernel(min(256, hidden_width), *refs),
         (shape(slot_count, 2 * hidden_width), shape(slot_count, 1, dtype=F32)),
         [VMEM] * 6,
-        (grads, w_down[0], gate_rows, hidden, slope, activated),
+        (grads, down_weight, gate_rows, hidden, slope, activated),
         16, 2 * slot_count * width * hidden_width, 2 * width * hidden_width,
     )
     pre_both = jnp.concatenate([pre_grads, swap_cores(pre_grads)], axis=0)
@@ -319,11 +350,12 @@
 
     def give_back(pre_grads):
         return call(
-            lambda *refs: return_kernel(min(256, width), *refs),
+            functools.partial(return_kernel, min(256, width)),
             shape(padded, width),
             [VMEM] * 4,
             (pre_grads, w_gate[0], w_up[0], take_turned),
             16, 4 * slot_count * width * hidden_width, 4 * width * hidden_width,
+            scratch=(pltpu.VMEM((slot_count, width), BF16),),
         )
 
     def collect(came_back):

time: 137 us -> 138 us (level)
    ppermute x8, waiting for transfers between devices: 25.4 us -> 28.1 us  [next_chip(): lax.ppermute(array, 'dp', [(i, (i + 2 * sign) % size) for i in range(size)])]
    ppermute x4, waiting for transfers between devices: 2.16 us -> 0.65 us  [swap_cores(): return lax.ppermute(array, 'dp', [(i, i ^ 1) for i in range(size)])]
    unnamed x42 -> x58, local copies, waits for them, and re-layouts: 10.4 us -> 9.85 us
    pallas_call x13 -> x15, Pallas kernels: 21.6 us -> 21.5 us  [call(): pl.pallas_call(kernel, grid=grid, out_shape=out_shapes, in_specs=in_specs...]
  transfers between devices with their start and end apart: 15 -> 15, of which waited for: 8 -> 8; matrix products, arithmetic and copies ran while one was open for 10% -> 10% of each run, Pallas kernels for 11% -> 10%
where the time goes in v4:
time: 138 us; the launch traced here: 137 us
  waiting for transfers between devices  52.1 us (38%)
  starting transfers between devices  37.3 us (27%)
  Pallas kernels  21.5 us (16%)
  local copies, waits for them, and re-layouts  11.6 us (8%)
  matrix products  8.93 us (6%)
  other arithmetic  4.79 us (3%)
    ppermute x8, waiting for transfers between devices, next_chip(): lax.ppermute(array, 'dp', [(i, (i + 2 * sign) % size) for i in range(size)])  28.1 us
    all_to_all x3, waiting for transfers between devices, exchange(): lax.all_to_all(shaped, 'expert', 0, 0, tiled=True).reshape(padded, width)  23.3 us
    pallas_call x15, Pallas kernels, call(): pl.pallas_call(kernel, grid=grid, out_shape=out_shapes, in_specs=in_specs...  21.5 us
    all_to_all x3, starting transfers between devices, exchange(): lax.all_to_all(shaped, 'expert', 0, 0, tiled=True).reshape(padded, width)  20.1 us
    ppermute x8, starting transfers between devices, next_chip(): lax.ppermute(array, 'dp', [(i, (i + 2 * sign) % size) for i in range(size)])  16 us
    unnamed x58, local copies, waits for them, and re-layouts  9.85 us
    dot_general x2, matrix products, dot_nn(): return jnp.dot(left, right, preferred_element_type=F32)  5.39 us
    dot_general x4, matrix products, dot_tn(): lax.dot_general(left, right, (((0,), (0,)), ((), ())), preferred_element_...  3.54 us
  transfers between devices with their start and end apart: 15, of which 8 were waited for; matrix products, arithmetic and copies ran while one was open for 10% of the time, Pallas kernels for 10%

profile of v4, /device:TPU:2, one launch (start us, length us, event | category | flops | bytes accessed | tf_op | source)
XLA Modules:
  0.0 137.1 jit_solution(11195703928169256884)
XLA Ops:
  0.6 0.7 copy-done.21
  1.4 1.0 copy-done.25
  2.4 2.2 %shard_map.112 = (bf16[384,128]{1,0:T(8,128)(2,1)S(1)}, bf16[384,2048]{1,0:T(8,128)(2,1)}) custom-call(s32[1]{0:T(128)} %bitcast.base_ref.refs_0_, s32[16,256]{1,0:T(8,128)S(1)} %bitcast.36, bf16[128,2048]{1,0:T(8,128)(2,1)S(1)} %copy-done.25), custom_call_target="tpu_custom_call" | custom-call | flops 201326592 | bytes 3145728 | tf_op jit(solution)/shard_map/pallas_call | solution.py:225
  4.6 7.6 %all-to-all-start.1 = ((bf16[16,24,2048]{2,1,0:T(8,128)(2,1)}), bf16[16,24,2048]{2,1,0:T(8,128)(2,1)S(1)}, u32[]{:S(2)}, u32[]{:S(2)}) async-start(bf16[16,24,2048]{2,1,0:T(8,128)(2,1)} %bitcast.7), calls=%async_computation.1 | async-start | bytes 3145728 | tf_op jit(solution)/shard_map/all_to_all | solution.py:275
  12.7 0.7 copy-done.17
  13.3 1.7 %shard_map.113 = bf16[384,2048]{1,0:T(8,128)(2,1)} custom-call(bf16[384,128]{1,0:T(8,128)(2,1)S(1)} %get-tuple-element.40.select_ref, bf16[128,2048]{1,0:T(8,128)(2,1)S(1)} %copy-done.14), custom_call_target="tpu_custom_call" | custom-call | flops 201326592 | bytes 3145728 | tf_op jit(solution)/shard_map/pallas_call | solution.py:225
  15.1 18.5 %all-to-all-done.1 = bf16[16,24,2048]{2,1,0:T(8,128)(2,1)S(1)} async-done(((bf16[16,24,2048]{2,1,0:T(8,128)(2,1)}), bf16[16,24,2048]{2,1,0:T(8,128)(2,1)S(1)}, u32[]{:S(2)}, u32[]{:S(2)}) %all-to-all-start.1) | async-done | bytes 1572896 | tf_op jit(solution)/shard_map/all_to_all | solution.py:275
  33.6 6.6 %all-to-all-start = ((bf16[16,24,2048]{2,1,0:T(8,128)(2,1)}), bf16[16,24,2048]{2,1,0:T(8,128)(2,1)}, u32[]{:S(2)}, u32[]{:S(2)}) async-start(bf16[16,24,2048]{2,1,0:T(8,128)(2,1)} %bitcast.5), calls=%async_computation | async-start | bytes 3145728 | tf_op jit(solution)/shard_map/all_to_all | solution.py:275
  40.2 2.1 %shard_map.114 = (bf16[256,2048]{1,0:T(8,128)(2,1)S(1)}, bf16[256,1024]{1,0:T(8,128)(2,1)S(1)}, bf16[256,1024]{1,0:T(8,128)(2,1)}) custom-call(s32[2]{0:T(128)S(1)} %pad_add_fusion.refs_0_, bf16[256,384]{1,0:T(8,128)(2,1)S(1)} %get-tuple-element.39.refs_1_, bf16[384,2048]{1,0:T(8,128)(2,1)S(1)} %bitcast.31), custom_call_target="tpu_custom_call" | custom-call | flops 402653184 | bytes 4194304 | tf_op jit(solution)/shard_map/pallas_call | solution.py:225
  42.4 0.8 copy-done.15
  43.2 3.0 %fusion.3 = f32[256,768]{1,0:T(8,128)S(1)} fusion(bf16[256,2048]{1,0:T(8,128)(2,1)S(1)} %get-tuple-element.42, bf16[1,2048,768]{2,1,0:T(8,128)(2,1)} %param.12), kind=kOutput, calls=%fused_computation.18 | convolution fusion | flops 805306368 | bytes 4980736 | tf_op jit(solution)/shard_map/dot_general | solution.py:18
  46.2 2.4 %add_multiply_fusion = (f32[256,768]{1,0:T(8,128)}, bf16[256,768]{1,0:T(8,128)(2,1)S(1)}, f32[256,768]{1,0:T(8,128)}) fusion(f32[256,768]{1,0:T(8,128)S(1)} %fusion.3, bf16[256,2048]{1,0:T(8,128)(2,1)S(1)} %get-tuple-element.42, bf16[1,2048,768]{2,1,0:T(8,128)(2,1)S(1)} %copy-done.6), kind=kOutput, calls=%fused_computation.6 | convolution fusion | flops 807469056 | bytes 6946816 | tf_op jit(solution)/shard_map/dot_general | solution.py:18
  48.6 0.5 collective-permute-start
  49.3 1.5 %copy.13.refs_3_.refs_2_ = f32[256,1]{1,0:T(8,128)} copy(f32[256,1]{0,1:T(1,128)} %bitcast.38) | data formatting | bytes 2048 | tf_op jit(solution)/shard_map/reshape | solution.py:315
  51.0 2.0 %pad_maximum_fusion.1 = bf16[512,768]{1,0:T(8,128)(2,1)} fusion(bf16[256,768]{1,0:T(8,128)(2,1)} %collective-permute-done.1, bf16[256,768]{1,0:T(8,128)(2,1)S(1)} %get-tuple-element.48.refs_3_), kind=kLoop, calls=%fused_computation.5 | loop fusion | flops 1572864 | bytes 1572864 | tf_op jit(solution)/shard_map/concatenate | solution.py:313
  52.9 2.1 %pad_maximum_fusion = bf16[512,1024]{1,0:T(8,128)(2,1)} fusion(bf16[256,1024]{1,0:T(8,128)(2,1)} %collective-permute-done, bf16[256,1024]{1,0:T(8,128)(2,1)S(1)} %copy-done.16), kind=kLoop, calls=%fused_computation.4 | loop fusion | flops 2097152 | bytes 2097152 | tf_op jit(solution)/shard_map/concatenate | solution.py:306
  55.0 4.8 %all-to-all-done = bf16[16,24,2048]{2,1,0:T(8,128)(2,1)} async-done(((bf16[16,24,2048]{2,1,0:T(8,128)(2,1)}), bf16[16,24,2048]{2,1,0:T(8,128)(2,1)}, u32[]{:S(2)}, u32[]{:S(2)}) %all-to-all-start) | async-done | bytes 1572896 | tf_op jit(solution)/shard_map/all_to_all | solution.py:275
  59.9 0.9 copy-done.8
  60.8 0.9 copy-done.13
  61.7 0.7 copy-done.24
  62.4 2.4 %shard_map.116 = (bf16[256,2048]{1,0:T(8,128)(2,1)S(1)}, bf16[256,1024]{1,0:T(8,128)(2,1)S(1)}, bf16[256,1024]{1,0:T(8,128)(2,1)S(1)}) custom-call(s32[2]{0:T(128)S(1)} %copy-done.24, bf16[256,384]{1,0:T(8,128)(2,1)S(1)} %copy-done.13, bf16[384,2048]{1,0:T(8,128)(2,1)} %bitcast.6.refs_2_, f32[256,1]{1,0:T(8,128)S(1)} %copy-done.8), custom_call_target="tpu_custom_call" | custom-call | flops 402653184 | bytes 4194304 | tf_op jit(solution)/shard_map/pallas_call | solution.py:225
  64.9 1.2 shard_map.117
  66.1 0.6 collective-permute-start.2
  66.8 1.0 copy-done.26
  68.1 0.4 collective-permute-done.2
  69.4 1.0 convolution_convert_fusion.2.down_front.down_back.down_ref
  70.5 2.0 %collective-permute-start.4 = (bf16[64,2304]{1,0:T(8,128)(2,1)S(1)}, bf16[64,2304]{1,0:T(8,128)(2,1)S(1)}, u32[]{:S(2)}, u32[]{:S(2)}) collective-permute-start(bf16[64,2304]{1,0:T(8,128)(2,1)S(1)} %get-tuple-element.57), channel_id=1, source_target_pairs={{0,32},{16,48},{32,64},{48,80},{64,96},{80,112},{96,128},{112,144}... | collective-permute-start | bytes 884744 | tf_op jit(solution)/shard_map/ppermute | solution.py:36
  72.5 4.2 %collective-permute-start.5 = (bf16[64,2304]{1,0:T(8,128)(2,1)S(1)}, bf16[64,2304]{1,0:T(8,128)(2,1)S(1)}, u32[]{:S(2)}, u32[]{:S(2)}) collective-permute-start(bf16[64,2304]{1,0:T(8,128)(2,1)S(1)} %get-tuple-element.58), channel_id=1, source_target_pairs={{0,224},{16,240},{32,0},{48,16},{64,32},{80,48},{96,64},{112,80},{... | collective-permute-start | bytes 884744 | tf_op jit(solution)/shard_map/ppermute | solution.py:36
  76.7 1.8 %convolution_convert_fusion.pre_front.pre_back.pre_ref = bf16[1024,1536]{1,0:T(8,128)(2,1)S(1)} fusion(bf16[512,1024]{1,0:T(8,128)(2,1)S(1)} %copy-done.27, bf16[512,1536]{1,0:T(8,128)(2,1)S(1)} %constant_dynamic-update-slice_fusion), kind=kOutput, calls=%fused_computation | convolution fusion | flops 1612185600 | bytes 5767168 | tf_op jit(solution)/shard_map/dot_general | solution.py:26
  78.6 5.1 %collective-permute-done.4.forward_ref = bf16[64,2304]{1,0:T(8,128)(2,1)S(1)} collective-permute-done((bf16[64,2304]{1,0:T(8,128)(2,1)S(1)}, bf16[64,2304]{1,0:T(8,128)(2,1)S(1)}, u32[]{:S(2)}, u32[]{:S(2)}) %collective-permute-start.4) | collective-permute-done | bytes 294944 | tf_op jit(solution)/shard_map/ppermute | solution.py:36
  83.7 1.1 shard_map.120
  84.8 3.2 %collective-permute-start.7 = (bf16[128,2304]{1,0:T(8,128)(2,1)}, bf16[128,2304]{1,0:T(8,128)(2,1)}, u32[]{:S(2)}, u32[]{:S(2)}) collective-permute-start(bf16[128,2304]{1,0:T(8,128)(2,1)} %get-tuple-element.60), channel_id=1, source_target_pairs={{0,224},{16,240},{32,0},{48,16},{64,32},{80,48},{96,64},{112,80},{... | collective-permute-start | bytes 1769480 | tf_op jit(solution)/shard_map/ppermute | solution.py:36
  88.1 2.2 %shard_map.118 = bf16[384,2048]{1,0:T(8,128)(2,1)S(1)} custom-call(bf16[256,1536]{1,0:T(8,128)(2,1)S(1)} %get-tuple-element.51.pre_ref, bf16[2048,768]{1,0:T(8,128)(2,1)S(1)} %bitcast.35, bf16[2048,768]{1,0:T(8,128)(2,1)S(1)} %bitcast.34, bf16[384,256]{1,0:T(8,128)(2,1)S(1)} %copy-done.18), custom_call_target="tpu_custom_call" | custom-call | flops 1610612736 | bytes 6291456 | tf_op jit(solution)/shard_map/pallas_call | solution.py:225
  90.3 1.1 copy-done.3
  91.5 5.9 %all-to-all-start.2 = ((bf16[16,24,2048]{2,1,0:T(8,128)(2,1)}), bf16[16,24,2048]{2,1,0:T(8,128)(2,1)}, u32[]{:S(2)}, u32[]{:S(2)}) async-start(bf16[16,24,2048]{2,1,0:T(8,128)(2,1)} %bitcast.32), calls=%async_computation.2 | async-start | bytes 3145728 | tf_op jit(solution)/shard_map/all_to_all | solution.py:275
  97.4 3.7 %collective-permute-done.6.forward_ref = bf16[128,2304]{1,0:T(8,128)(2,1)} collective-permute-done((bf16[128,2304]{1,0:T(8,128)(2,1)}, bf16[128,2304]{1,0:T(8,128)(2,1)}, u32[]{:S(2)}, u32[]{:S(2)}) %collective-permute-start.6) | collective-permute-done | bytes 589856 | tf_op jit(solution)/shard_map/ppermute | solution.py:36
  101.1 1.4 %copy-done.1 = bf16[1024,768]{1,0:T(8,128)(2,1)S(1)} copy-done((bf16[1024,768]{1,0:T(8,128)(2,1)S(1)}, bf16[1024,768]{1,0:T(8,128)(2,1)}, u32[]{:S(2)}) %copy-start.1) | copy-done | bytes 1572888
  102.5 1.5 %shard_map.121 = (bf16[128,2304]{1,0:T(8,128)(2,1)S(1)}, bf16[128,2304]{1,0:T(8,128)(2,1)S(1)}) custom-call(bf16[128,2304]{1,0:T(8,128)(2,1)} %collective-permute-done.6.forward_ref, bf16[128,2304]{1,0:T(8,128)(2,1)} %collective-permute-done.7.backward_ref, bf16[1024,1536]{1,0:T(8,128)(2,1)S(1)} %convolution_convert_fusion.pre_front.pre_back.pre_ref, ...), custom_call_target="tpu_custom_call" | custom-call | flops 1 | bytes 1 | tf_op jit(solution)/shard_map/pallas_call | solution.py:225
  104.0 1.9 %collective-permute-start.8 = (bf16[128,2304]{1,0:T(8,128)(2,1)S(1)}, bf16[128,2304]{1,0:T(8,128)(2,1)S(1)}, u32[]{:S(2)}, u32[]{:S(2)}) collective-permute-start(bf16[128,2304]{1,0:T(8,128)(2,1)S(1)} %get-tuple-element.62), channel_id=1, source_target_pairs={{0,32},{16,48},{32,64},{48,80},{64,96},{80,112},{96,128},{112,144}... | collective-permute-start | bytes 1769480 | tf_op jit(solution)/shard_map/ppermute | solution.py:36
  105.9 1.4 %collective-permute-start.9 = (bf16[128,2304]{1,0:T(8,128)(2,1)S(1)}, bf16[128,2304]{1,0:T(8,128)(2,1)S(1)}, u32[]{:S(2)}, u32[]{:S(2)}) collective-permute-start(bf16[128,2304]{1,0:T(8,128)(2,1)S(1)} %get-tuple-element.63), channel_id=1, source_target_pairs={{0,224},{16,240},{32,0},{48,16},{64,32},{80,48},{96,64},{112,80},{... | collective-permute-start | bytes 1769480 | tf_op jit(solution)/shard_map/ppermute | solution.py:36
  107.3 11.8 %collective-permute-done.8.forward_ref = bf16[128,2304]{1,0:T(8,128)(2,1)S(1)} collective-permute-done((bf16[128,2304]{1,0:T(8,128)(2,1)S(1)}, bf16[128,2304]{1,0:T(8,128)(2,1)S(1)}, u32[]{:S(2)}, u32[]{:S(2)}) %collective-permute-start.8) | collective-permute-done | bytes 589856 | tf_op jit(solution)/shard_map/ppermute | solution.py:36
  119.2 1.1 shard_map.122
  120.3 1.5 %collective-permute-start.10 = (bf16[128,2304]{1,0:T(8,128)(2,1)}, bf16[128,2304]{1,0:T(8,128)(2,1)}, u32[]{:S(2)}, u32[]{:S(2)}) collective-permute-start(bf16[128,2304]{1,0:T(8,128)(2,1)} %get-tuple-element.64), channel_id=1, source_target_pairs={{0,32},{16,48},{32,64},{48,80},{64,96},{80,112},{96,128},{112,144}... | collective-permute-start | bytes 1769480 | tf_op jit(solution)/shard_map/ppermute | solution.py:36
  121.8 1.7 %collective-permute-start.11 = (bf16[128,2304]{1,0:T(8,128)(2,1)}, bf16[128,2304]{1,0:T(8,128)(2,1)}, u32[]{:S(2)}, u32[]{:S(2)}) collective-permute-start(bf16[128,2304]{1,0:T(8,128)(2,1)} %get-tuple-element.65), channel_id=1, source_target_pairs={{0,224},{16,240},{32,0},{48,16},{64,32},{80,48},{96,64},{112,80},{... | collective-permute-start | bytes 1769480 | tf_op jit(solution)/shard_map/ppermute | solution.py:36
  123.9 0.7 reduce
  124.6 2.8 %shard_map.123 = bf16[128,2048]{1,0:T(8,128)(2,1)} custom-call(bf16[128,384]{1,0:T(8,128)(2,1)S(1)} %shard_map.110.select_ref, bf16[384,2048]{1,0:T(8,128)(2,1)} %bitcast.14.tokens_ref), custom_call_target="tpu_custom_call" | custom-call | flops 201326592 | bytes 3145728 | tf_op jit(solution)/shard_map/pallas_call | solution.py:225
  127.4 7.5 %collective-permute-done.10.forward_ref = bf16[128,2304]{1,0:T(8,128)(2,1)} collective-permute-done((bf16[128,2304]{1,0:T(8,128)(2,1)}, bf16[128,2304]{1,0:T(8,128)(2,1)}, u32[]{:S(2)}, u32[]{:S(2)}) %collective-permute-start.10) | collective-permute-done | bytes 589856 | tf_op jit(solution)/shard_map/ppermute | solution.py:36
  134.8 2.3 %shard_map.124 = (bf16[1,128,768]{2,1,0:T(8,128)(2,1)}, bf16[1,128,768]{2,1,0:T(8,128)(2,1)}, bf16[1,768,128]{2,1,0:T(8,128)(2,1)}) custom-call(bf16[128,2304]{1,0:T(8,128)(2,1)} %collective-permute-done.10.forward_ref, bf16[128,2304]{1,0:T(8,128)(2,1)} %collective-permute-done.11.backward_ref, ...), custom_call_target="tpu_custom_call" | custom-call | flops 1 | bytes 1 | tf_op jit(solution)/shard_map/pallas_call | solution.py:225
  (70 shorter events, 2.8 us)
Async XLA Ops:
  0.6 0.7 copy-start.21
  1.4 1.0 copy-start.25
  4.6 7.6 %copy-start.22 = (s32[1,16,256]{2,1,0:T(8,128)S(1)}, s32[1,16,256]{2,1,0:T(8,128)}, u32[]{:S(2)}) copy-start(s32[1,16,256]{2,1,0:T(8,128)} %param.9) | copy-start | bytes 49156
  4.6 8.8 %copy-start.14 = (bf16[128,2048]{1,0:T(8,128)(2,1)S(1)}, bf16[128,2048]{1,0:T(8,128)(2,1)}, u32[]{:S(2)}) copy-start(bf16[128,2048]{1,0:T(8,128)(2,1)} %tokens_ref.1) | copy-start | bytes 1572868
  4.6 29.0 %all-to-all-start.1 = ((bf16[16,24,2048]{2,1,0:T(8,128)(2,1)}), bf16[16,24,2048]{2,1,0:T(8,128)(2,1)S(1)}, u32[]{:S(2)}, u32[]{:S(2)}) async-start(bf16[16,24,2048]{2,1,0:T(8,128)(2,1)} %bitcast.7), calls=%async_computation.1 | async-start | bytes 3145728 | tf_op jit(solution)/shard_map/all_to_all | solution.py:275
  12.6 0.7 copy-start.17
  13.3 26.9 %copy-start.12 = (bf16[256,384]{1,0:T(8,128)(2,1)}, bf16[256,384]{1,0:T(8,128)(2,1)S(1)}, u32[]{:S(2)}) copy-start(bf16[256,384]{1,0:T(8,128)(2,1)S(1)} %get-tuple-element.39.refs_1_) | copy-start | bytes 589828
  15.1 25.1 %copy-start.23 = (s32[2]{0:T(128)}, s32[2]{0:T(128)S(1)}, u32[]{:S(2)}) copy-start(s32[2]{0:T(128)S(1)} %pad_add_fusion.refs_0_) | copy-start | bytes 28
  33.6 26.3 %all-to-all-start = ((bf16[16,24,2048]{2,1,0:T(8,128)(2,1)}), bf16[16,24,2048]{2,1,0:T(8,128)(2,1)}, u32[]{:S(2)}, u32[]{:S(2)}) async-start(bf16[16,24,2048]{2,1,0:T(8,128)(2,1)} %bitcast.5), calls=%async_computation | async-start | bytes 3145728 | tf_op jit(solution)/shard_map/all_to_all | solution.py:275
  42.4 0.8 copy-start.15
  43.2 3.0 %copy-start.6 = (bf16[1,2048,768]{2,1,0:T(8,128)(2,1)S(1)}, bf16[1,2048,768]{2,1,0:T(8,128)(2,1)}, u32[]{:S(2)}) copy-start(bf16[1,2048,768]{2,1,0:T(8,128)(2,1)} %param.11) | copy-start | bytes 9437188
  46.2 2.9 %copy-start.4 = (bf16[1,768,2048]{2,1,0:T(8,128)(2,1)S(1)}, bf16[1,768,2048]{2,1,0:T(8,128)(2,1)}, u32[]{:S(2)}) copy-start(bf16[1,768,2048]{2,1,0:T(8,128)(2,1)} %param.13) | copy-start | bytes 9437188
  48.6 2.4 %collective-permute-start.1 = (bf16[256,768]{1,0:T(8,128)(2,1)S(1)}, bf16[256,768]{1,0:T(8,128)(2,1)}, u32[]{:S(2)}, u32[]{:S(2)}) collective-permute-start(bf16[256,768]{1,0:T(8,128)(2,1)S(1)} %get-tuple-element.48.refs_3_), channel_id=1, source_target_pairs={{0,16},{16,0},{32,48},{48,32},{64,80},{80,64},{96,112},{112,96},{1... | collective-permute-start | bytes 1179656 | tf_op jit(solution)/shard_map/ppermute | solution.py:31
  48.6 4.3 %collective-permute-start = (bf16[256,1024]{1,0:T(8,128)(2,1)}, bf16[256,1024]{1,0:T(8,128)(2,1)}, u32[]{:S(2)}, u32[]{:S(2)}) collective-permute-start(bf16[256,1024]{1,0:T(8,128)(2,1)} %get-tuple-element.44), channel_id=1, source_target_pairs={{0,16},{16,0},{32,48},{48,32},{64,80},{80,64},{96,112},{112,96},{1... | collective-permute-start | bytes 1572872 | tf_op jit(solution)/shard_map/ppermute | solution.py:31
  50.8 2.1 %copy-start.16 = (bf16[256,1024]{1,0:T(8,128)(2,1)S(1)}, bf16[256,1024]{1,0:T(8,128)(2,1)}, u32[]{:S(2)}) copy-start(bf16[256,1024]{1,0:T(8,128)(2,1)} %copy-done.15) | copy-start | bytes 1572868
  59.9 0.9 copy-start.8
  60.8 0.9 copy-start.13
  61.7 0.7 copy-start.24
  62.4 2.5 %copy-start.9 = (f32[256,1]{1,0:T(8,128)S(1)}, f32[256,1]{1,0:T(8,128)}, u32[]{:S(2)}) copy-start(f32[256,1]{1,0:T(8,128)} %copy.13.refs_3_.refs_2_) | copy-start | bytes 3076
  62.4 2.5 %copy-start.10 = (f32[256,768]{1,0:T(8,128)S(1)}, f32[256,768]{1,0:T(8,128)}, u32[]{:S(2)}) copy-start(f32[256,768]{1,0:T(8,128)} %get-tuple-element.49.refs_4_) | copy-start | bytes 2359300
  62.4 2.5 %copy-start.11 = (f32[256,768]{1,0:T(8,128)S(1)}, f32[256,768]{1,0:T(8,128)}, u32[]{:S(2)}) copy-start(f32[256,768]{1,0:T(8,128)} %get-tuple-element.50.refs_5_) | copy-start | bytes 2359300
  64.8 2.0 %collective-permute-start.3 = (bf16[256,1024]{1,0:T(8,128)(2,1)S(1)}, bf16[256,1024]{1,0:T(8,128)(2,1)S(1)}, u32[]{:S(2)}, u32[]{:S(2)}) collective-permute-start(bf16[256,1024]{1,0:T(8,128)(2,1)S(1)} %get-tuple-element.55), channel_id=1, source_target_pairs={{0,16},{16,0},{32,48},{48,32},{64,80},{80,64},{96,112},{112,96},{1... | collective-permute-start | bytes 1572872 | tf_op jit(solution)/shard_map/ppermute | solution.py:31
  66.1 0.8 copy-start.19
  66.1 2.5 %collective-permute-start.2 = (bf16[256,1536]{1,0:T(8,128)(2,1)S(1)}, bf16[256,1536]{1,0:T(8,128)(2,1)S(1)}, u32[]{:S(2)}, u32[]{:S(2)}) collective-permute-start(bf16[256,1536]{1,0:T(8,128)(2,1)S(1)} %get-tuple-element.51.pre_ref), channel_id=1, source_target_pairs={{0,16},{16,0},{32,48},{48,32},{64,80},{80,64},{96,112},{112,96},{1... | collective-permute-start | bytes 2359304 | tf_op jit(solution)/shard_map/ppermute | solution.py:31
  66.7 1.1 copy-start.26
  67.8 1.2 copy-start.27
  70.5 13.2 %copy-start = (bf16[1024,768]{1,0:T(8,128)(2,1)}, bf16[1024,768]{1,0:T(8,128)(2,1)S(1)}, u32[]{:S(2)}) copy-start(bf16[1024,768]{1,0:T(8,128)(2,1)S(1)} %convolution_convert_fusion.2.down_front.down_back.down_ref) | copy-start | bytes 4718596
  70.5 13.2 %collective-permute-start.4 = (bf16[64,2304]{1,0:T(8,128)(2,1)S(1)}, bf16[64,2304]{1,0:T(8,128)(2,1)S(1)}, u32[]{:S(2)}, u32[]{:S(2)}) collective-permute-start(bf16[64,2304]{1,0:T(8,128)(2,1)S(1)} %get-tuple-element.57), channel_id=1, source_target_pairs={{0,32},{16,48},{32,64},{48,80},{64,96},{80,112},{96,128},{112,144}... | collective-permute-start | bytes 884744 | tf_op jit(solution)/shard_map/ppermute | solution.py:36
  72.5 11.2 %collective-permute-start.5 = (bf16[64,2304]{1,0:T(8,128)(2,1)S(1)}, bf16[64,2304]{1,0:T(8,128)(2,1)S(1)}, u32[]{:S(2)}, u32[]{:S(2)}) collective-permute-start(bf16[64,2304]{1,0:T(8,128)(2,1)S(1)} %get-tuple-element.58), channel_id=1, source_target_pairs={{0,224},{16,240},{32,0},{48,16},{64,32},{80,48},{96,64},{112,80},{... | collective-permute-start | bytes 884744 | tf_op jit(solution)/shard_map/ppermute | solution.py:36
  78.6 9.5 %copy-start.18 = (bf16[384,256]{1,0:T(8,128)(2,1)S(1)}, bf16[384,256]{1,0:T(8,128)(2,1)}, u32[]{:S(2)}) copy-start(bf16[384,256]{1,0:T(8,128)(2,1)} %copy-done.17) | copy-start | bytes 589828
  83.7 4.4 %copy-start.5 = (bf16[1,2048,768]{2,1,0:T(8,128)(2,1)S(1)}, bf16[1,2048,768]{2,1,0:T(8,128)(2,1)}, u32[]{:S(2)}) copy-start(bf16[1,2048,768]{2,1,0:T(8,128)(2,1)} %param.12) | copy-start | bytes 9437188
  83.7 4.4 %copy-start.7 = (bf16[1,2048,768]{2,1,0:T(8,128)(2,1)S(1)}, bf16[1,2048,768]{2,1,0:T(8,128)(2,1)}, u32[]{:S(2)}) copy-start(bf16[1,2048,768]{2,1,0:T(8,128)(2,1)} %param.11) | copy-start | bytes 9437188
  84.8 16.3 %collective-permute-start.6 = (bf16[128,2304]{1,0:T(8,128)(2,1)}, bf16[128,2304]{1,0:T(8,128)(2,1)}, u32[]{:S(2)}, u32[]{:S(2)}) collective-permute-start(bf16[128,2304]{1,0:T(8,128)(2,1)} %get-tuple-element.59), channel_id=1, source_target_pairs={{0,32},{16,48},{32,64},{48,80},{64,96},{80,112},{96,128},{112,144}... | collective-permute-start | bytes 1769480 | tf_op jit(solution)/shard_map/ppermute | solution.py:36
  84.8 16.3 %collective-permute-start.7 = (bf16[128,2304]{1,0:T(8,128)(2,1)}, bf16[128,2304]{1,0:T(8,128)(2,1)}, u32[]{:S(2)}, u32[]{:S(2)}) collective-permute-start(bf16[128,2304]{1,0:T(8,128)(2,1)} %get-tuple-element.60), channel_id=1, source_target_pairs={{0,224},{16,240},{32,0},{48,16},{64,32},{80,48},{96,64},{112,80},{... | collective-permute-start | bytes 1769480 | tf_op jit(solution)/shard_map/ppermute | solution.py:36
  90.3 1.2 copy-start.3
  91.5 33.2 %all-to-all-start.2 = ((bf16[16,24,2048]{2,1,0:T(8,128)(2,1)}), bf16[16,24,2048]{2,1,0:T(8,128)(2,1)}, u32[]{:S(2)}, u32[]{:S(2)}) async-start(bf16[16,24,2048]{2,1,0:T(8,128)(2,1)} %bitcast.32), calls=%async_computation.2 | async-start | bytes 3145728 | tf_op jit(solution)/shard_map/all_to_all | solution.py:275
  101.1 1.4 %copy-start.1 = (bf16[1024,768]{1,0:T(8,128)(2,1)S(1)}, bf16[1024,768]{1,0:T(8,128)(2,1)}, u32[]{:S(2)}) copy-start(bf16[1024,768]{1,0:T(8,128)(2,1)} %copy-done) | copy-start | bytes 4718596
  104.0 15.1 %collective-permute-start.8 = (bf16[128,2304]{1,0:T(8,128)(2,1)S(1)}, bf16[128,2304]{1,0:T(8,128)(2,1)S(1)}, u32[]{:S(2)}, u32[]{:S(2)}) collective-permute-start(bf16[128,2304]{1,0:T(8,128)(2,1)S(1)} %get-tuple-element.62), channel_id=1, source_target_pairs={{0,32},{16,48},{32,64},{48,80},{64,96},{80,112},{96,128},{112,144}... | collective-permute-start | bytes 1769480 | tf_op jit(solution)/shard_map/ppermute | solution.py:36
  105.9 18.0 %copy-start.20 = (f32[256,1]{1,0:T(8,128)S(1)}, f32[256,1]{1,0:T(8,128)}, u32[]{:S(2)}) copy-start(f32[256,1]{1,0:T(8,128)} %copy-done.19) | copy-start | bytes 3076
  105.9 13.2 %collective-permute-start.9 = (bf16[128,2304]{1,0:T(8,128)(2,1)S(1)}, bf16[128,2304]{1,0:T(8,128)(2,1)S(1)}, u32[]{:S(2)}, u32[]{:S(2)}) collective-permute-start(bf16[128,2304]{1,0:T(8,128)(2,1)S(1)} %get-tuple-element.63), channel_id=1, source_target_pairs={{0,224},{16,240},{32,0},{48,16},{64,32},{80,48},{96,64},{112,80},{... | collective-permute-start | bytes 1769480 | tf_op jit(solution)/shard_map/ppermute | solution.py:36
  120.3 14.5 %collective-permute-start.10 = (bf16[128,2304]{1,0:T(8,128)(2,1)}, bf16[128,2304]{1,0:T(8,128)(2,1)}, u32[]{:S(2)}, u32[]{:S(2)}) collective-permute-start(bf16[128,2304]{1,0:T(8,128)(2,1)} %get-tuple-element.64), channel_id=1, source_target_pairs={{0,32},{16,48},{32,64},{48,80},{64,96},{80,112},{96,128},{112,144}... | collective-permute-start | bytes 1769480 | tf_op jit(solution)/shard_map/ppermute | solution.py:36
  121.8 13.0 %collective-permute-start.11 = (bf16[128,2304]{1,0:T(8,128)(2,1)}, bf16[128,2304]{1,0:T(8,128)(2,1)}, u32[]{:S(2)}, u32[]{:S(2)}) collective-permute-start(bf16[128,2304]{1,0:T(8,128)(2,1)} %get-tuple-element.65), channel_id=1, source_target_pairs={{0,224},{16,240},{32,0},{48,16},{64,32},{80,48},{96,64},{112,80},{... | collective-permute-start | bytes 1769480 | tf_op jit(solution)/shard_map/ppermute | solution.py:36
  124.6 10.2 %copy-start.2 = (bf16[1024,768]{1,0:T(8,128)(2,1)S(1)}, bf16[1024,768]{1,0:T(8,128)(2,1)}, u32[]{:S(2)}) copy-start(bf16[1024,768]{1,0:T(8,128)(2,1)} %copy-done) | copy-start | bytes 4718596

commit v5 on v4

--- a/solution.py
+++ b/solution.py
@@ -47,12 +47,17 @@
     return jnp.concatenate([pre_ref[...], down_ref[...]], axis=1)
 
 
-def split_kernel(pre_ref, down_ref, front_out, back_out):
+def far_kernel(
+    rows_own, rows_got, scaled_own, scaled_got, pre_own, pre_got, hidden_own, hidden_got,
+    front_out, back_out,
+):
     half = front_out.shape[0]
-    edge = pre_ref.shape[1]
+    edge = pre_own.shape[1]
+    pre = dot_tn(rows_own[...], pre_own[...]) + dot_tn(rows_got[...], pre_got[...])
+    down = dot_tn(scaled_own[...], hidden_own[...]) + dot_tn(scaled_got[...], hidden_got[...])
     for out, rows in ((front_out, slice(0, half)), (back_out, slice(half, 2 * half))):
-        out[:, :edge] = pre_ref[rows, :]
-        out[:, edge:] = down_ref[rows, :]
+        out[:, :edge] = pre[rows].astype(BF16)
+        out[:, edge:] = down[rows].astype(BF16)
 
 
 def join_kernel(forward_ref, backward_ref, pre_front, down_front, pre_back, down_back, front_out, back_out):
@@ -83,12 +88,18 @@
 
 
 class Sums:
-    def __init__(self, far, parts, block, chips):
-        self.parts, self.block, self.chips = parts, block, chips
-        self.widths = [part.shape[1] for part in parts]
+    def __init__(self, sides, widths, block, chips):
+        self.block, self.chips, self.widths = block, chips, widths
         self.distance = chips // 2
-        half = jax.ShapeDtypeStruct((block // 2, sum(self.widths)), BF16)
-        self.send(call(split_kernel, (half, half), [VMEM, VMEM], far, 8, 1, 1))
+        half = jax.ShapeDtypeStruct((block // 2, sum(widths)), BF16)
+        slots = sides[0].shape[0]
+        chunk = pl.BlockSpec((slots, block), lambda step: (0, chips // 2))
+        whole = [pl.BlockSpec(side.shape, lambda step: (0, 0)) for side in sides[4:]]
+        self.operands = call(
+            far_kernel, (half, half), [chunk] * 4 + whole, sides,
+            54, 4 * slots * block * sum(widths), 4 * slots * sum(widths), (1,),
+        )
+        self.send(self.operands)
 
     def specs(self, away):
         place = away % self.chips
@@ -150,26 +161,35 @@
     out_ref[...] = dot_nn(select_ref[...], tokens_ref[...]).astype(BF16)
 
 
-def take_kernel(most, tok_dev, own_ref, take_ref, turned_ref):
+def as_column(row):
+    size = row.shape[1]
+    same = lax.broadcasted_iota(I32, (size, size), 0) == lax.broadcasted_iota(I32, (size, size), 1)
+    return jnp.sum(jnp.where(same, row, 0.0), axis=1, keepdims=True)
+
+
+def take_kernel(most, tok_dev, picks_ref, gates_ref, take_ref, turned_ref, gate_ref):
     slots, columns = take_ref.shape
     lane = lax.broadcasted_iota(I32, (1, columns), 1)
     source = jnp.zeros((1, columns), I32)
     for edge in range(most, columns, most):
         source = source + (lane >= edge).astype(I32)
     within = lane - source * most
-    own = own_ref[...]
-    start = jnp.sum((own < source * tok_dev).astype(F32), axis=0, keepdims=True)
-    stop = jnp.sum((own < (source + 1) * tok_dev).astype(F32), axis=0, keepdims=True)
+    bound = (source * tok_dev).astype(F32)
+    own = as_column(picks_ref[pl.ds(lax.axis_index("expert"), 1), :].astype(F32))
+    start = jnp.sum((own < bound).astype(F32), axis=0, keepdims=True)
+    stop = jnp.sum((own < bound + tok_dev).astype(F32), axis=0, keepdims=True)
     slot = start + within.astype(F32)
     slot = jnp.where(slot < stop, slot, -1.0)
     slot_range = lax.broadcasted_iota(I32, (slots, columns), 0).astype(F32)
     hot = (slot_range == slot).astype(F32)
     take_ref[...] = hot.astype(BF16)
     turned_ref[...] = hot.T.astype(BF16)
-
-
-def compact_kernel(chips, place_ref, take_ref, arrived_ref, scale_ref, full_ref, keep_ref, give_ref):
-    chip, core = place_ref[0], place_ref[1]
+    gate_ref[...] = as_column(gates_ref[...])
+
+
+def compact_kernel(chips, take_ref, arrived_ref, scale_ref, full_ref, keep_ref, give_ref):
+    dp_index = lax.axis_index("dp")
+    chip, core = lax.shift_right_logical(dp_index, 1), dp_index & 1
     block = arrived_ref.shape[1] // (2 * chips)
     for k in range(chips):
         columns = slice(2 * k * block, 2 * (k + 1) * block)
@@ -184,13 +204,28 @@
         give_ref[:, where] = jnp.where(core == 0, odd, even).astype(BF16)
 
 
-def plain_compact_kernel(chips, place_ref, take_ref, arrived_ref, full_ref, keep_ref, give_ref):
-    compact_kernel(chips, place_ref, take_ref, arrived_ref, None, full_ref, keep_ref, give_ref)
+def plain_compact_kernel(chips, take_ref, arrived_ref, full_ref, keep_ref, give_ref):
+    compact_kernel(chips, take_ref, arrived_ref, None, full_ref, keep_ref, give_ref)
 
 
 def grad_kernel(
-    tile, grads_ref, down_ref, gate_ref, hidden_ref, slope_ref, activated_ref, pre_ref, slot_ref
+    chips, tile, arrived_ref, take_hbm, gate_hbm, down_hbm, hidden_hbm, slope_hbm, activated_hbm,
+    keep_ref, give_ref, pre_ref, slot_ref,
+    take_ref, gate_ref, down_ref, hidden_ref, slope_ref, activated_ref, grads_ref, arrivals,
 ):
+    sources = (take_hbm, gate_hbm, down_hbm, hidden_hbm, slope_hbm, activated_hbm)
+    targets = (take_ref, gate_ref, down_ref, hidden_ref, slope_ref, activated_ref)
+    copies = [
+        pltpu.make_async_copy(source, target, arrivals.at[index])
+        for index, (source, target) in enumerate(zip(sources, targets))
+    ]
+    for copy in copies:
+        copy.start()
+    copies[0].wait()
+    copies[1].wait()
+    compact_kernel(chips, take_ref, arrived_ref, gate_ref, grads_ref, keep_ref, give_ref)
+    for copy in copies[2:]:
+        copy.wait()
     hidden_width = down_ref.shape[0]
     total = jnp.zeros(slot_ref.shape, F32)
     for begin in range(0, hidden_width, tile):
@@ -204,8 +239,16 @@
     slot_ref[...] = total
 
 
-def park_kernel(array_ref, out_ref):
-    out_ref[...] = array_ref[...]
+def forward_kernel(tile, rows_ref, gate_ref, up_ref, hidden_ref, slope_ref, activated_ref):
+    for begin in range(0, gate_ref.shape[1], tile):
+        columns = slice(begin, begin + tile)
+        gate_pre = dot_nn(rows_ref[...], gate_ref[:, columns])
+        up_pre = dot_nn(rows_ref[...], up_ref[:, columns])
+        sigmoid_gate = jax.nn.sigmoid(gate_pre)
+        activated = gate_pre * sigmoid_gate
+        hidden_ref[:, columns] = (activated * up_pre).astype(BF16)
+        activated_ref[:, columns] = activated
+        slope_ref[:, columns] = up_pre * sigmoid_gate * (1.0 + gate_pre * (1.0 - sigmoid_gate))
 
 
 def return_kernel(tile, pre_ref, gate_ref, up_ref, turned_ref, out_ref, held):
@@ -242,7 +285,6 @@
     dp_size = lax.axis_size("dp")
     dp_index = lax.axis_index("dp")
     chips = dp_size // 2
-    place = jnp.stack([lax.shift_right_logical(dp_index, 1), dp_index & 1]).astype(I32)
     tok_dev, width = tokens.shape
     slot_count = gates.shape[2]
     most = max(2, 3 * slot_count // (2 * node_count))
@@ -277,12 +319,12 @@
     arrived_rows = exchange(out_rows)
     arrived_grads = exchange(out_grads)
 
-    own = lax.dynamic_index_in_dim(table, self_index, 0, keepdims=False)
-    take, take_turned = call(
-        lambda *refs: take_kernel(most, tok_dev, *refs),
-        (shape(slot_count, padded), shape(padded, slot_count)),
-        [VMEM],
-        (own.reshape(slot_count, 1),),
+    held_table, arrived_rows = lax.optimization_barrier((table, arrived_rows))
+    take, take_turned, gate_rows = call(
+        functools.partial(take_kernel, most, tok_dev),
+        (shape(slot_count, padded), shape(padded, slot_count), shape(slot_count, 1, dtype=F32)),
+        [VMEM, VMEM],
+        (held_table, gates.reshape(1, slot_count)),
         8, 8 * slot_count * padded, 2 * slot_count * padded,
     )
     select_turned = call(
@@ -295,57 +337,58 @@
     compact_shapes = (
         shape(slot_count, width), shape(slot_count, width // 2), shape(slot_count, width // 2)
     )
+    origin = lambda step: (0, 0)
     compact_cost = (12, 2 * slot_count * padded * width, 8 * slot_count * width)
     rows, rows_keep, rows_give = call(
         lambda *refs: plain_compact_kernel(chips, *refs),
         compact_shapes,
-        [SMEM, VMEM, VMEM],
-        (place, take, arrived_rows),
+        [pl.BlockSpec(take.shape, origin), VMEM],
+        (take, arrived_rows),
         *compact_cost,
-    )
-    rows_both = jnp.concatenate([rows_keep, swap_cores(rows_give)], axis=0)
-    gate_pre = dot_nn(rows, w_gate[0])
-    up_pre = dot_nn(rows, w_up[0])
-    sigmoid_gate = jax.nn.sigmoid(gate_pre)
-    activated = gate_pre * sigmoid_gate
-    slope = up_pre * sigmoid_gate * (1.0 + gate_pre * (1.0 - sigmoid_gate))
-    hidden = (activated * up_pre).astype(BF16)
-    hidden_both = jnp.concatenate([hidden, swap_cores(hidden)], axis=0)
-
-    gate_rows = gates.reshape(slot_count, 1)
-    down_weight = call(
-        park_kernel,
-        shape(hidden_width, width),
-        [VMEM],
-        (w_down[0],),
-        8, 1, 4 * width * hidden_width,
-    )
-    arrived_grads, hidden, slope, activated, rows_both, hidden_both, down_weight = (
-        lax.optimization_barrier(
-            (arrived_grads, hidden, slope, activated, rows_both, hidden_both, down_weight)
-        )
-    )
-    grads, scaled_keep, scaled_give = call(
-        lambda *refs: compact_kernel(chips, *refs),
-        compact_shapes,
-        [SMEM, VMEM, VMEM, VMEM],
-        (place, take, arrived_grads, gate_rows),
-        *compact_cost,
-    )
-    scaled_both = jnp.concatenate([scaled_keep, swap_cores(scaled_give)], axis=0)
-    pre_grads, slot_grads = call(
-        lambda *refs: grad_kernel(min(256, hidden_width), *refs),
-        (shape(slot_count, 2 * hidden_width), shape(slot_count, 1, dtype=F32)),
-        [VMEM] * 6,
-        (grads, down_weight, gate_rows, hidden, slope, activated),
-        16, 2 * slot_count * width * hidden_width, 2 * width * hidden_width,
-    )
-    pre_both = jnp.concatenate([pre_grads, swap_cores(pre_grads)], axis=0)
-
-    def parts_of(columns):
+        grid=(1,),
+    )
+    narrow = (slot_count, hidden_width)
+    hidden, slope, activated = call(
+        functools.partial(forward_kernel, min(256, hidden_width)),
+        (shape(*narrow), shape(*narrow, dtype=F32), shape(*narrow, dtype=F32)),
+        [VMEM] * 3,
+        (rows, w_gate[0], w_up[0]),
+        16, 4 * slot_count * width * hidden_width, 4 * width * hidden_width,
+    )
+    rows_got, hidden_got = swap_cores(rows_give), swap_cores(hidden)
+    arrived_grads, hidden, slope, activated, rows_got, hidden_got = lax.optimization_barrier(
+        (arrived_grads, hidden, slope, activated, rows_got, hidden_got)
+    )
+    operands = (take, gate_rows, w_down[0], hidden, slope, activated)
+    scaled_keep, scaled_give, pre_grads, slot_grads = call(
+        functools.partial(grad_kernel, chips, min(256, hidden_width)),
+        (
+            shape(slot_count, width // 2),
+            shape(slot_count, width // 2),
+            shape(slot_count, 2 * hidden_width),
+            shape(slot_count, 1, dtype=F32),
+        ),
+        [VMEM] + [pl.BlockSpec(memory_space=pl.ANY)] * 6,
+        (arrived_grads, *operands),
+        54,
+        2 * slot_count * width * (padded + hidden_width),
+        2 * width * hidden_width,
+        scratch=(
+            *(pltpu.VMEM(operand.shape, operand.dtype) for operand in operands),
+            pltpu.VMEM((slot_count, width), BF16),
+            pltpu.SemaphoreType.DMA((6,)),
+        ),
+    )
+    scaled_got = swap_cores(scaled_give)
+    pre_got = swap_cores(pre_grads)
+    sides = (
+        rows_keep, rows_got, scaled_keep, scaled_got, pre_grads, pre_got, hidden, hidden_got
+    )
+
+    def whole_parts(sides):
+        pairs = [jnp.concatenate(sides[2 * k : 2 * k + 2], axis=0) for k in range(4)]
         return (
-            dot_tn(rows_both[:, columns], pre_both).astype(BF16),
-            dot_tn(scaled_both[:, columns], hidden_both).astype(BF16),
+            dot_tn(pairs[0], pairs[2]).astype(BF16), dot_tn(pairs[1], pairs[3]).astype(BF16)
         )
 
     def give_back(pre_grads):
@@ -368,10 +411,9 @@
         )
 
     if chips > 1:
-        farthest = chips // 2
-        far = parts_of(slice(farthest * block, (farthest + 1) * block))
-        parts = parts_of(slice(None))
-        sums = Sums(far, parts, block, chips)
+        sums = Sums(sides, [2 * hidden_width, hidden_width], block, chips)
+        held_sides, _ = lax.optimization_barrier((sides, sums.operands))
+        sums.parts = whole_parts(held_sides)
         returning = give_back(pre_grads)
         returned = None
         while sums.distance > 1:
@@ -393,7 +435,7 @@
         weight_grads = sums.finish(weight_shapes, token_grads)
     else:
         token_grads = collect(exchange(give_back(pre_grads)))
-        pre_part, down_part = parts_of(slice(None))
+        pre_part, down_part = whole_parts(sides)
         weight_grads = (*(half[None] for half in jnp.split(pre_part, 2, axis=1)), down_part.T[None])
     return (token_grads, slot_grads.reshape(1, 1, slot_count), *weight_grads)
 

time: 138 us -> 143 us (1.036)
  Pallas kernels: 21.5 us -> 27.6 us
  other arithmetic: 4.79 us -> 0.68 us
  matrix products: 8.93 us -> 5.31 us
  local copies, waits for them, and re-layouts: 11.6 us -> 15.1 us
  waiting for transfers between devices: 52.1 us -> 55.6 us
    pallas_call x15 -> x14, Pallas kernels: 21.5 us -> 27.6 us  [call(): pl.pallas_call(kernel, grid=grid, out_shape=out_shapes, in_specs=in_specs...]
    dot_general x2 -> x0, matrix products: 5.39 us -> none  [dot_nn(): return jnp.dot(left, right, preferred_element_type=F32)]
    unnamed x58 -> x68, local copies, waits for them, and re-layouts: 9.85 us -> 15.1 us
    all_to_all x3, waiting for transfers between devices: 23.3 us -> 27.7 us  [exchange(): lax.all_to_all(shaped, 'expert', 0, 0, tiled=True).reshape(padded, width)]
    concatenate x2 -> x0, other arithmetic: 4.04 us -> none  [the longest x1 2.09 us: body(): rows_both = jnp.concatenate([rows_keep, swap_cores(rows_give)], axis=0)]
    ppermute x8, waiting for transfers between devices: 28.1 us -> 25.2 us  [next_chip(): lax.ppermute(array, 'dp', [(i, (i + 2 * sign) % size) for i in range(size)])]
    ppermute x4, waiting for transfers between devices: 0.65 us -> 2.74 us  [swap_cores(): return lax.ppermute(array, 'dp', [(i, i ^ 1) for i in range(size)])]
    dot_general x4 -> x2, matrix products: 3.54 us -> 5.31 us  [dot_tn(): lax.dot_general(left, right, (((0,), (0,)), ((), ())), preferred_element_...]
  transfers between devices with their start and end apart: 15 -> 15, of which waited for: 8 -> 7; matrix products, arithmetic and copies ran while one was open for 10% -> 4% of each run, Pallas kernels for 10% -> 9%
where the time goes in v5:
time: 143 us; the launch traced here: 142 us
  waiting for transfers between devices  55.6 us (39%)
  starting transfers between devices  37.3 us (26%)
  Pallas kernels  27.6 us (19%)
  local copies, waits for them, and re-layouts  15.1 us (11%)
  matrix products  5.31 us (4%)
    all_to_all x3, waiting for transfers between devices, exchange(): lax.all_to_all(shaped, 'expert', 0, 0, tiled=True).reshape(padded, width)  27.7 us
    pallas_call x14, Pallas kernels, call(): pl.pallas_call(kernel, grid=grid, out_shape=out_shapes, in_specs=in_specs...  27.6 us
    ppermute x8, waiting for transfers between devices, next_chip(): lax.ppermute(array, 'dp', [(i, (i + 2 * sign) % size) for i in range(size)])  25.2 us
    all_to_all x3, starting transfers between devices, exchange(): lax.all_to_all(shaped, 'expert', 0, 0, tiled=True).reshape(padded, width)  20.3 us
    ppermute x8, starting transfers between devices, next_chip(): lax.ppermute(array, 'dp', [(i, (i + 2 * sign) % size) for i in range(size)])  15.9 us
    unnamed x68, local copies, waits for them, and re-layouts  15.1 us
    dot_general x2, matrix products, dot_tn(): lax.dot_general(left, right, (((0,), (0,)), ((), ())), preferred_element_...  5.31 us
  transfers between devices with their start and end apart: 15, of which 7 were waited for; matrix products, arithmetic and copies ran while one was open for 4% of the time, Pallas kernels for 9%

profile of v5, /device:TPU:2, one launch (start us, length us, event | category | flops | bytes accessed | tf_op | source)
XLA Modules:
  0.0 142.4 jit_solution(11314567404013708334)
XLA Ops:
  0.7 0.8 copy-done.23
  1.4 1.0 copy-done.26
  2.5 2.2 %shard_map.111 = (bf16[384,128]{1,0:T(8,128)(2,1)S(1)}, bf16[384,2048]{1,0:T(8,128)(2,1)}) custom-call(s32[1]{0:T(128)} %bitcast.base_ref.refs_0_, s32[16,256]{1,0:T(8,128)S(1)} %bitcast.20, bf16[128,2048]{1,0:T(8,128)(2,1)S(1)} %copy-done.26), custom_call_target="tpu_custom_call" | custom-call | flops 201326592 | bytes 3145728 | tf_op jit(solution)/shard_map/pallas_call | solution.py:268
  4.7 7.5 %all-to-all-start.1 = ((bf16[16,24,2048]{2,1,0:T(8,128)(2,1)}), bf16[16,24,2048]{2,1,0:T(8,128)(2,1)S(1)}, u32[]{:S(2)}, u32[]{:S(2)}) async-start(bf16[16,24,2048]{2,1,0:T(8,128)(2,1)} %bitcast.4), calls=%async_computation.1 | async-start | bytes 3145728 | tf_op jit(solution)/shard_map/all_to_all | solution.py:317
  12.1 0.6 shard_map.112
  12.7 1.1 copy-done.7
  13.8 19.7 %all-to-all-done.1 = bf16[16,24,2048]{2,1,0:T(8,128)(2,1)S(1)} async-done(((bf16[16,24,2048]{2,1,0:T(8,128)(2,1)}), bf16[16,24,2048]{2,1,0:T(8,128)(2,1)S(1)}, u32[]{:S(2)}, u32[]{:S(2)}) %all-to-all-start.1) | async-done | bytes 1572896 | tf_op jit(solution)/shard_map/all_to_all | solution.py:317
  33.5 1.2 copy-done.8
  34.7 6.9 %all-to-all-start = ((bf16[16,24,2048]{2,1,0:T(8,128)(2,1)}), bf16[16,24,2048]{2,1,0:T(8,128)(2,1)}, u32[]{:S(2)}, u32[]{:S(2)}) async-start(bf16[16,24,2048]{2,1,0:T(8,128)(2,1)} %bitcast.17), calls=%async_computation | async-start | bytes 3145728 | tf_op jit(solution)/shard_map/all_to_all | solution.py:317
  42.0 0.7 copy-done.20
  42.6 0.7 copy-done.22
  43.3 1.5 %copy-done.9 = bf16[16,24,2048]{2,1,0:T(8,128)(2,1)S(1)} copy-done((bf16[16,24,2048]{2,1,0:T(8,128)(2,1)S(1)}, bf16[16,24,2048]{2,1,0:T(8,128)(2,1)}, u32[]{:S(2)}) %copy-start.9) | copy-done | bytes 1572888
  44.8 1.6 %shard_map.114 = (bf16[256,2048]{1,0:T(8,128)(2,1)S(1)}, bf16[256,1024]{1,0:T(8,128)(2,1)S(1)}, bf16[256,1024]{1,0:T(8,128)(2,1)}) custom-call(bf16[256,384]{1,0:T(8,128)(2,1)S(1)} %get-tuple-element.54.refs_0_.take_hbm, bf16[384,2048]{1,0:T(8,128)(2,1)S(1)} %bitcast.18), custom_call_target="tpu_custom_call" | custom-call | flops 402653184 | bytes 4194304 | tf_op jit(solution)/shard_map/pallas_call | solution.py:268
  46.4 0.8 copy-done.17
  47.2 1.9 %copy-done.5 = bf16[1,2048,768]{2,1,0:T(8,128)(2,1)S(1)} copy-done((bf16[1,2048,768]{2,1,0:T(8,128)(2,1)S(1)}, bf16[1,2048,768]{2,1,0:T(8,128)(2,1)}, u32[]{:S(2)}) %copy-start.5) | copy-done | bytes 3145752
  49.1 1.8 %shard_map.115 = (bf16[256,768]{1,0:T(8,128)(2,1)S(1)}, f32[256,768]{1,0:T(8,128)S(1)}, f32[256,768]{1,0:T(8,128)S(1)}) custom-call(bf16[256,2048]{1,0:T(8,128)(2,1)S(1)} %get-tuple-element.56.rows_ref, bf16[2048,768]{1,0:T(8,128)(2,1)S(1)} %bitcast.13, bf16[2048,768]{1,0:T(8,128)(2,1)S(1)} %bitcast.15), custom_call_target="tpu_custom_call" | custom-call | flops 1610612736 | bytes 6291456 | tf_op jit(solution)/shard_map/pallas_call | solution.py:268
  50.9 0.9 copy-done.15
  51.8 0.9 copy-done.16
  52.7 0.5 collective-permute-start.1
  53.2 8.0 %all-to-all-done = bf16[16,24,2048]{2,1,0:T(8,128)(2,1)} async-done(((bf16[16,24,2048]{2,1,0:T(8,128)(2,1)}), bf16[16,24,2048]{2,1,0:T(8,128)(2,1)}, u32[]{:S(2)}, u32[]{:S(2)}) %all-to-all-start) | async-done | bytes 1572896 | tf_op jit(solution)/shard_map/all_to_all | solution.py:317
  61.3 6.5 %shard_map.116 = (bf16[256,1024]{1,0:T(8,128)(2,1)}, bf16[256,1024]{1,0:T(8,128)(2,1)}, bf16[256,1536]{1,0:T(8,128)(2,1)}, f32[256,1]{1,0:T(8,128)}) custom-call(bf16[384,2048]{1,0:T(8,128)(2,1)} %bitcast.3.arrived_ref, bf16[256,384]{1,0:T(8,128)(2,1)} %copy-done.14, f32[256,1]{1,0:T(8,128)} %copy-done.22, bf16[768,2048]{1,0:T(8,128)(2,1)} %bitcast.24, ...), custom_call_target="tpu_custom_call" | custom-call | flops 1207959552 | bytes 3145728 | tf_op jit(solution)/shard_map/pallas_call | solution.py:268
  67.9 0.5 collective-permute-start.2
  68.4 2.7 %collective-permute-done.2.scaled_got = bf16[256,1024]{1,0:T(8,128)(2,1)S(1)} collective-permute-done((bf16[256,1024]{1,0:T(8,128)(2,1)}, bf16[256,1024]{1,0:T(8,128)(2,1)S(1)}, u32[]{:S(2)}, u32[]{:S(2)}) %collective-permute-start.2) | collective-permute-done | bytes 524320 | tf_op jit(solution)/shard_map/ppermute | solution.py:31
  71.1 0.8 copy-done.30
  72.2 3.1 %shard_map.118 = (bf16[64,2304]{1,0:T(8,128)(2,1)}, bf16[64,2304]{1,0:T(8,128)(2,1)}) custom-call(bf16[256,1024]{1,0:T(8,128)(2,1)} %copy-done.17, bf16[256,1024]{1,0:T(8,128)(2,1)} %collective-permute-done.rows_got, bf16[256,1024]{1,0:T(8,128)(2,1)} %get-tuple-element.79.scaled_own, bf16[256,1024]{1,0:T(8,128)(2,1)} %copy-done.30, ...), custom_call_target="tpu_custom_call" | custom-call | flops 301989888 | bytes 2359296 | tf_op jit(solution)/shard_map/pallas_call | solution.py:268
  75.3 1.9 %collective-permute-start.4 = (bf16[64,2304]{1,0:T(8,128)(2,1)}, bf16[64,2304]{1,0:T(8,128)(2,1)S(1)}, u32[]{:S(2)}, u32[]{:S(2)}) collective-permute-start(bf16[64,2304]{1,0:T(8,128)(2,1)} %get-tuple-element.73), channel_id=1, source_target_pairs={{0,32},{16,48},{32,64},{48,80},{64,96},{80,112},{96,128},{112,144}... | collective-permute-start | bytes 884744 | tf_op jit(solution)/shard_map/ppermute | solution.py:36
  77.2 4.2 %collective-permute-start.5 = (bf16[64,2304]{1,0:T(8,128)(2,1)}, bf16[64,2304]{1,0:T(8,128)(2,1)S(1)}, u32[]{:S(2)}, u32[]{:S(2)}) collective-permute-start(bf16[64,2304]{1,0:T(8,128)(2,1)} %get-tuple-element.74), channel_id=1, source_target_pairs={{0,224},{16,240},{32,0},{48,16},{64,32},{80,48},{96,64},{112,80},{... | collective-permute-start | bytes 884744 | tf_op jit(solution)/shard_map/ppermute | solution.py:36
  81.5 2.1 %convolution_convert_fusion.1.down_front.down_back.down_ref = bf16[1024,768]{1,0:T(8,128)(2,1)S(1)} fusion(bf16[256,1024]{1,0:T(8,128)(2,1)} %copy-done.30, bf16[256,1024]{1,0:T(8,128)(2,1)S(1)} %copy-done.29, bf16[256,768]{1,0:T(8,128)(2,1)S(1)} %copy-done.32, bf16[256,768]{1,0:T(8,128)(2,1)S(1)} %copy-done.13), kind=kOutput, calls=%fused_computation.1 | convolution fusion | flops 809762816 | bytes 3407872 | tf_op jit(solution)/shard_map/dot_general | solution.py:26
  83.6 3.3 %convolution_convert_fusion.pre_front.pre_back.pre_ref = bf16[1024,1536]{1,0:T(8,128)(2,1)S(1)} fusion(bf16[256,1536]{1,0:T(8,128)(2,1)S(1)} %copy-done.28, bf16[256,1536]{1,0:T(8,128)(2,1)S(1)} %copy-done.11, bf16[256,1024]{1,0:T(8,128)(2,1)} %collective-permute-done.rows_got, bf16[256,1024]{1,0:T(8,128)(2,1)S(1)} %copy-done.18), kind=kOutput, calls=%fused_computation | convolution fusion | flops 1617428480 | bytes 5767168 | tf_op jit(solution)/shard_map/dot_general | solution.py:26
  86.8 1.9 %collective-permute-done.4.forward_ref = bf16[64,2304]{1,0:T(8,128)(2,1)S(1)} collective-permute-done((bf16[64,2304]{1,0:T(8,128)(2,1)}, bf16[64,2304]{1,0:T(8,128)(2,1)S(1)}, u32[]{:S(2)}, u32[]{:S(2)}) %collective-permute-start.4) | collective-permute-done | bytes 294944 | tf_op jit(solution)/shard_map/ppermute | solution.py:36
  88.7 1.1 shard_map.119
  89.8 3.2 %collective-permute-start.7 = (bf16[128,2304]{1,0:T(8,128)(2,1)}, bf16[128,2304]{1,0:T(8,128)(2,1)}, u32[]{:S(2)}, u32[]{:S(2)}) collective-permute-start(bf16[128,2304]{1,0:T(8,128)(2,1)} %get-tuple-element.84), channel_id=1, source_target_pairs={{0,224},{16,240},{32,0},{48,16},{64,32},{80,48},{96,64},{112,80},{... | collective-permute-start | bytes 1769480 | tf_op jit(solution)/shard_map/ppermute | solution.py:36
  93.1 2.2 %shard_map.117 = bf16[384,2048]{1,0:T(8,128)(2,1)S(1)} custom-call(bf16[256,1536]{1,0:T(8,128)(2,1)S(1)} %copy-done.11, bf16[2048,768]{1,0:T(8,128)(2,1)S(1)} %bitcast.14, bf16[2048,768]{1,0:T(8,128)(2,1)S(1)} %bitcast.16, bf16[384,256]{1,0:T(8,128)(2,1)S(1)} %copy-done.21), custom_call_target="tpu_custom_call" | custom-call | flops 1610612736 | bytes 6291456 | tf_op jit(solution)/shard_map/pallas_call | solution.py:268
  95.3 1.2 copy-done.10
  96.5 5.9 %all-to-all-start.2 = ((bf16[16,24,2048]{2,1,0:T(8,128)(2,1)}), bf16[16,24,2048]{2,1,0:T(8,128)(2,1)}, u32[]{:S(2)}, u32[]{:S(2)}) async-start(bf16[16,24,2048]{2,1,0:T(8,128)(2,1)} %bitcast.19), calls=%async_computation.2 | async-start | bytes 3145728 | tf_op jit(solution)/shard_map/all_to_all | solution.py:317
  102.4 3.9 %collective-permute-done.6.forward_ref = bf16[128,2304]{1,0:T(8,128)(2,1)} collective-permute-done((bf16[128,2304]{1,0:T(8,128)(2,1)}, bf16[128,2304]{1,0:T(8,128)(2,1)}, u32[]{:S(2)}, u32[]{:S(2)}) %collective-permute-start.6) | collective-permute-done | bytes 589856 | tf_op jit(solution)/shard_map/ppermute | solution.py:36
  106.2 1.4 copy-done.1
  107.6 1.5 %shard_map.120 = (bf16[128,2304]{1,0:T(8,128)(2,1)S(1)}, bf16[128,2304]{1,0:T(8,128)(2,1)S(1)}) custom-call(bf16[128,2304]{1,0:T(8,128)(2,1)} %collective-permute-done.6.forward_ref, bf16[128,2304]{1,0:T(8,128)(2,1)} %collective-permute-done.7.backward_ref, bf16[1024,1536]{1,0:T(8,128)(2,1)S(1)} %convolution_convert_fusion.pre_front.pre_back.pre_ref, ...), custom_call_target="tpu_custom_call" | custom-call | flops 1 | bytes 1 | tf_op jit(solution)/shard_map/pallas_call | solution.py:268
  109.1 1.9 %collective-permute-start.8 = (bf16[128,2304]{1,0:T(8,128)(2,1)S(1)}, bf16[128,2304]{1,0:T(8,128)(2,1)S(1)}, u32[]{:S(2)}, u32[]{:S(2)}) collective-permute-start(bf16[128,2304]{1,0:T(8,128)(2,1)S(1)} %get-tuple-element.86), channel_id=1, source_target_pairs={{0,32},{16,48},{32,64},{48,80},{64,96},{80,112},{96,128},{112,144}... | collective-permute-start | bytes 1769480 | tf_op jit(solution)/shard_map/ppermute | solution.py:36
  111.0 1.4 %collective-permute-start.9 = (bf16[128,2304]{1,0:T(8,128)(2,1)S(1)}, bf16[128,2304]{1,0:T(8,128)(2,1)S(1)}, u32[]{:S(2)}, u32[]{:S(2)}) collective-permute-start(bf16[128,2304]{1,0:T(8,128)(2,1)S(1)} %get-tuple-element.87), channel_id=1, source_target_pairs={{0,224},{16,240},{32,0},{48,16},{64,32},{80,48},{96,64},{112,80},{... | collective-permute-start | bytes 1769480 | tf_op jit(solution)/shard_map/ppermute | solution.py:36
  112.5 11.9 %collective-permute-done.8.forward_ref = bf16[128,2304]{1,0:T(8,128)(2,1)S(1)} collective-permute-done((bf16[128,2304]{1,0:T(8,128)(2,1)S(1)}, bf16[128,2304]{1,0:T(8,128)(2,1)S(1)}, u32[]{:S(2)}, u32[]{:S(2)}) %collective-permute-start.8) | collective-permute-done | bytes 589856 | tf_op jit(solution)/shard_map/ppermute | solution.py:36
  124.4 1.2 shard_map.121
  125.6 1.5 %collective-permute-start.10 = (bf16[128,2304]{1,0:T(8,128)(2,1)}, bf16[128,2304]{1,0:T(8,128)(2,1)}, u32[]{:S(2)}, u32[]{:S(2)}) collective-permute-start(bf16[128,2304]{1,0:T(8,128)(2,1)} %get-tuple-element.88), channel_id=1, source_target_pairs={{0,32},{16,48},{32,64},{48,80},{64,96},{80,112},{96,128},{112,144}... | collective-permute-start | bytes 1769480 | tf_op jit(solution)/shard_map/ppermute | solution.py:36
  127.1 1.7 %collective-permute-start.11 = (bf16[128,2304]{1,0:T(8,128)(2,1)}, bf16[128,2304]{1,0:T(8,128)(2,1)}, u32[]{:S(2)}, u32[]{:S(2)}) collective-permute-start(bf16[128,2304]{1,0:T(8,128)(2,1)} %get-tuple-element.89), channel_id=1, source_target_pairs={{0,224},{16,240},{32,0},{48,16},{64,32},{80,48},{96,64},{112,80},{... | collective-permute-start | bytes 1769480 | tf_op jit(solution)/shard_map/ppermute | solution.py:36
  129.2 0.7 reduce
  129.9 2.8 %shard_map.122 = bf16[128,2048]{1,0:T(8,128)(2,1)} custom-call(bf16[128,384]{1,0:T(8,128)(2,1)S(1)} %shard_map.110.select_ref, bf16[384,2048]{1,0:T(8,128)(2,1)} %bitcast.11.tokens_ref), custom_call_target="tpu_custom_call" | custom-call | flops 201326592 | bytes 3145728 | tf_op jit(solution)/shard_map/pallas_call | solution.py:268
  132.6 7.5 %collective-permute-done.10.forward_ref = bf16[128,2304]{1,0:T(8,128)(2,1)} collective-permute-done((bf16[128,2304]{1,0:T(8,128)(2,1)}, bf16[128,2304]{1,0:T(8,128)(2,1)}, u32[]{:S(2)}, u32[]{:S(2)}) %collective-permute-start.10) | collective-permute-done | bytes 589856 | tf_op jit(solution)/shard_map/ppermute | solution.py:36
  140.2 2.3 %shard_map.123 = (bf16[1,128,768]{2,1,0:T(8,128)(2,1)}, bf16[1,128,768]{2,1,0:T(8,128)(2,1)}, bf16[1,768,128]{2,1,0:T(8,128)(2,1)}) custom-call(bf16[128,2304]{1,0:T(8,128)(2,1)} %collective-permute-done.10.forward_ref, bf16[128,2304]{1,0:T(8,128)(2,1)} %collective-permute-done.11.backward_ref, ...), custom_call_target="tpu_custom_call" | custom-call | flops 1 | bytes 1 | tf_op jit(solution)/shard_map/pallas_call | solution.py:268
  (67 shorter events, 1.2 us)
Async XLA Ops:
  0.6 11.5 %copy-start.19 = (bf16[128,2048]{1,0:T(8,128)(2,1)S(1)}, bf16[128,2048]{1,0:T(8,128)(2,1)}, u32[]{:S(2)}) copy-start(bf16[128,2048]{1,0:T(8,128)(2,1)} %tokens_ref.1) | copy-start | bytes 1572868
  0.6 0.8 copy-start.23
  1.4 1.0 copy-start.26
  4.7 28.9 %all-to-all-start.1 = ((bf16[16,24,2048]{2,1,0:T(8,128)(2,1)}), bf16[16,24,2048]{2,1,0:T(8,128)(2,1)S(1)}, u32[]{:S(2)}, u32[]{:S(2)}) async-start(bf16[16,24,2048]{2,1,0:T(8,128)(2,1)} %bitcast.4), calls=%async_computation.1 | async-start | bytes 3145728 | tf_op jit(solution)/shard_map/all_to_all | solution.py:317
  12.7 1.1 copy-start.7
  13.8 27.8 %copy-start.24 = (s32[1,16,256]{2,1,0:T(8,128)S(1)}, s32[1,16,256]{2,1,0:T(8,128)}, u32[]{:S(2)}) copy-start(s32[1,16,256]{2,1,0:T(8,128)} %param.9) | copy-start | bytes 49156
  13.8 27.8 %copy-start.25 = (f32[1,1,256]{2,1,0:T(1,128)S(1)}, f32[1,1,256]{2,1,0:T(1,128)}, u32[]{:S(2)}) copy-start(f32[1,1,256]{2,1,0:T(1,128)} %param.10) | copy-start | bytes 3076
  33.5 1.2 copy-start.8
  34.7 12.5 %copy-start.3 = (bf16[1,2048,768]{2,1,0:T(8,128)(2,1)S(1)}, bf16[1,2048,768]{2,1,0:T(8,128)(2,1)}, u32[]{:S(2)}) copy-start(bf16[1,2048,768]{2,1,0:T(8,128)(2,1)} %param.11) | copy-start | bytes 9437188
  34.7 26.5 %all-to-all-start = ((bf16[16,24,2048]{2,1,0:T(8,128)(2,1)}), bf16[16,24,2048]{2,1,0:T(8,128)(2,1)}, u32[]{:S(2)}, u32[]{:S(2)}) async-start(bf16[16,24,2048]{2,1,0:T(8,128)(2,1)} %bitcast.17), calls=%async_computation | async-start | bytes 3145728 | tf_op jit(solution)/shard_map/all_to_all | solution.py:317
  42.0 0.7 copy-start.20
  43.3 3.9 %copy-start.14 = (bf16[256,384]{1,0:T(8,128)(2,1)}, bf16[256,384]{1,0:T(8,128)(2,1)S(1)}, u32[]{:S(2)}) copy-start(bf16[256,384]{1,0:T(8,128)(2,1)S(1)} %get-tuple-element.54.refs_0_.take_hbm) | copy-start | bytes 589828
  43.3 1.5 %copy-start.9 = (bf16[16,24,2048]{2,1,0:T(8,128)(2,1)S(1)}, bf16[16,24,2048]{2,1,0:T(8,128)(2,1)}, u32[]{:S(2)}) copy-start(bf16[16,24,2048]{2,1,0:T(8,128)(2,1)} %copy-done.8) | copy-start | bytes 4718596
  46.4 0.8 copy-start.17
  47.2 14.1 %collective-permute-start = (bf16[256,1024]{1,0:T(8,128)(2,1)}, bf16[256,1024]{1,0:T(8,128)(2,1)}, u32[]{:S(2)}, u32[]{:S(2)}) collective-permute-start(bf16[256,1024]{1,0:T(8,128)(2,1)} %get-tuple-element.60), channel_id=1, source_target_pairs={{0,16},{16,0},{32,48},{48,32},{64,80},{80,64},{96,112},{112,96},{1... | collective-permute-start | bytes 1572872 | tf_op jit(solution)/shard_map/ppermute | solution.py:31
  47.2 1.9 %copy-start.5 = (bf16[1,2048,768]{2,1,0:T(8,128)(2,1)S(1)}, bf16[1,2048,768]{2,1,0:T(8,128)(2,1)}, u32[]{:S(2)}) copy-start(bf16[1,2048,768]{2,1,0:T(8,128)(2,1)} %param.12) | copy-start | bytes 9437188
  50.9 0.9 copy-start.15
  51.8 0.9 copy-start.16
  52.7 8.5 %copy-start.12 = (bf16[256,768]{1,0:T(8,128)(2,1)}, bf16[256,768]{1,0:T(8,128)(2,1)S(1)}, u32[]{:S(2)}) copy-start(bf16[256,768]{1,0:T(8,128)(2,1)S(1)} %get-tuple-element.81.hidden_hbm.hidden_own) | copy-start | bytes 1179652
  52.7 8.5 %collective-permute-start.1 = (bf16[256,768]{1,0:T(8,128)(2,1)S(1)}, bf16[256,768]{1,0:T(8,128)(2,1)S(1)}, u32[]{:S(2)}, u32[]{:S(2)}) collective-permute-start(bf16[256,768]{1,0:T(8,128)(2,1)S(1)} %get-tuple-element.81.hidden_hbm.hidden_own), channel_id=1, source_target_pairs={{0,16},{16,0},{32,48},{48,32},{64,80},{80,64},{96,112},{112,96},{1... | collective-permute-start | bytes 1179656 | tf_op jit(solution)/shard_map/ppermute | solution.py:31
  61.2 6.5 %copy-start.31 = (bf16[256,768]{1,0:T(8,128)(2,1)}, bf16[256,768]{1,0:T(8,128)(2,1)S(1)}, u32[]{:S(2)}) copy-start(bf16[256,768]{1,0:T(8,128)(2,1)S(1)} %collective-permute-done.1.hidden_got) | copy-start | bytes 1179652
  67.8 3.3 %collective-permute-start.3 = (bf16[256,1536]{1,0:T(8,128)(2,1)}, bf16[256,1536]{1,0:T(8,128)(2,1)S(1)}, u32[]{:S(2)}, u32[]{:S(2)}) collective-permute-start(bf16[256,1536]{1,0:T(8,128)(2,1)} %get-tuple-element.77.pre_ref.pre_own), channel_id=1, source_target_pairs={{0,16},{16,0},{32,48},{48,32},{64,80},{80,64},{96,112},{112,96},{1... | collective-permute-start | bytes 2359304 | tf_op jit(solution)/shard_map/ppermute | solution.py:31
  67.9 3.2 %collective-permute-start.2 = (bf16[256,1024]{1,0:T(8,128)(2,1)}, bf16[256,1024]{1,0:T(8,128)(2,1)S(1)}, u32[]{:S(2)}, u32[]{:S(2)}) collective-permute-start(bf16[256,1024]{1,0:T(8,128)(2,1)} %get-tuple-element.71), channel_id=1, source_target_pairs={{0,16},{16,0},{32,48},{48,32},{64,80},{80,64},{96,112},{112,96},{1... | collective-permute-start | bytes 1572872 | tf_op jit(solution)/shard_map/ppermute | solution.py:31
  71.1 0.8 copy-start.30
  71.1 1.1 copy-start.27
  72.2 9.3 %copy-start.13 = (bf16[256,768]{1,0:T(8,128)(2,1)S(1)}, bf16[256,768]{1,0:T(8,128)(2,1)}, u32[]{:S(2)}) copy-start(bf16[256,768]{1,0:T(8,128)(2,1)} %copy-done.12) | copy-start | bytes 1179652
  72.2 9.3 %copy-start.29 = (bf16[256,1024]{1,0:T(8,128)(2,1)S(1)}, bf16[256,1024]{1,0:T(8,128)(2,1)}, u32[]{:S(2)}) copy-start(bf16[256,1024]{1,0:T(8,128)(2,1)} %get-tuple-element.79.scaled_own) | copy-start | bytes 1572868
  72.2 9.3 %copy-start.32 = (bf16[256,768]{1,0:T(8,128)(2,1)S(1)}, bf16[256,768]{1,0:T(8,128)(2,1)}, u32[]{:S(2)}) copy-start(bf16[256,768]{1,0:T(8,128)(2,1)} %copy-done.31) | copy-start | bytes 1179652
  75.3 13.4 %collective-permute-start.4 = (bf16[64,2304]{1,0:T(8,128)(2,1)}, bf16[64,2304]{1,0:T(8,128)(2,1)S(1)}, u32[]{:S(2)}, u32[]{:S(2)}) collective-permute-start(bf16[64,2304]{1,0:T(8,128)(2,1)} %get-tuple-element.73), channel_id=1, source_target_pairs={{0,32},{16,48},{32,64},{48,80},{64,96},{80,112},{96,128},{112,144}... | collective-permute-start | bytes 884744 | tf_op jit(solution)/shard_map/ppermute | solution.py:36
  77.2 6.3 %copy-start.11 = (bf16[256,1536]{1,0:T(8,128)(2,1)S(1)}, bf16[256,1536]{1,0:T(8,128)(2,1)}, u32[]{:S(2)}) copy-start(bf16[256,1536]{1,0:T(8,128)(2,1)} %get-tuple-element.77.pre_ref.pre_own) | copy-start | bytes 2359300
  77.2 6.3 %copy-start.18 = (bf16[256,1024]{1,0:T(8,128)(2,1)S(1)}, bf16[256,1024]{1,0:T(8,128)(2,1)}, u32[]{:S(2)}) copy-start(bf16[256,1024]{1,0:T(8,128)(2,1)} %copy-done.17) | copy-start | bytes 1572868
  77.2 6.3 %copy-start.28 = (bf16[256,1536]{1,0:T(8,128)(2,1)S(1)}, bf16[256,1536]{1,0:T(8,128)(2,1)}, u32[]{:S(2)}) copy-start(bf16[256,1536]{1,0:T(8,128)(2,1)} %copy-done.27) | copy-start | bytes 2359300
  77.2 11.5 %collective-permute-start.5 = (bf16[64,2304]{1,0:T(8,128)(2,1)}, bf16[64,2304]{1,0:T(8,128)(2,1)S(1)}, u32[]{:S(2)}, u32[]{:S(2)}) collective-permute-start(bf16[64,2304]{1,0:T(8,128)(2,1)} %get-tuple-element.74), channel_id=1, source_target_pairs={{0,224},{16,240},{32,0},{48,16},{64,32},{80,48},{96,64},{112,80},{... | collective-permute-start | bytes 884744 | tf_op jit(solution)/shard_map/ppermute | solution.py:36
  83.5 5.1 %copy-start = (bf16[1024,768]{1,0:T(8,128)(2,1)}, bf16[1024,768]{1,0:T(8,128)(2,1)S(1)}, u32[]{:S(2)}) copy-start(bf16[1024,768]{1,0:T(8,128)(2,1)S(1)} %convolution_convert_fusion.1.down_front.down_back.down_ref) | copy-start | bytes 4718596
  86.8 6.2 %copy-start.21 = (bf16[384,256]{1,0:T(8,128)(2,1)S(1)}, bf16[384,256]{1,0:T(8,128)(2,1)}, u32[]{:S(2)}) copy-start(bf16[384,256]{1,0:T(8,128)(2,1)} %copy-done.20) | copy-start | bytes 589828
  88.7 4.4 %copy-start.4 = (bf16[1,2048,768]{2,1,0:T(8,128)(2,1)S(1)}, bf16[1,2048,768]{2,1,0:T(8,128)(2,1)}, u32[]{:S(2)}) copy-start(bf16[1,2048,768]{2,1,0:T(8,128)(2,1)} %param.11) | copy-start | bytes 9437188
  88.7 4.4 %copy-start.6 = (bf16[1,2048,768]{2,1,0:T(8,128)(2,1)S(1)}, bf16[1,2048,768]{2,1,0:T(8,128)(2,1)}, u32[]{:S(2)}) copy-start(bf16[1,2048,768]{2,1,0:T(8,128)(2,1)} %param.12) | copy-start | bytes 9437188
  89.8 16.4 %collective-permute-start.6 = (bf16[128,2304]{1,0:T(8,128)(2,1)}, bf16[128,2304]{1,0:T(8,128)(2,1)}, u32[]{:S(2)}, u32[]{:S(2)}) collective-permute-start(bf16[128,2304]{1,0:T(8,128)(2,1)} %get-tuple-element.83), channel_id=1, source_target_pairs={{0,32},{16,48},{32,64},{48,80},{64,96},{80,112},{96,128},{112,144}... | collective-permute-start | bytes 1769480 | tf_op jit(solution)/shard_map/ppermute | solution.py:36
  89.8 16.4 %collective-permute-start.7 = (bf16[128,2304]{1,0:T(8,128)(2,1)}, bf16[128,2304]{1,0:T(8,128)(2,1)}, u32[]{:S(2)}, u32[]{:S(2)}) collective-permute-start(bf16[128,2304]{1,0:T(8,128)(2,1)} %get-tuple-element.84), channel_id=1, source_target_pairs={{0,224},{16,240},{32,0},{48,16},{64,32},{80,48},{96,64},{112,80},{... | collective-permute-start | bytes 1769480 | tf_op jit(solution)/shard_map/ppermute | solution.py:36
  95.3 1.2 copy-start.10
  96.5 33.4 %all-to-all-start.2 = ((bf16[16,24,2048]{2,1,0:T(8,128)(2,1)}), bf16[16,24,2048]{2,1,0:T(8,128)(2,1)}, u32[]{:S(2)}, u32[]{:S(2)}) async-start(bf16[16,24,2048]{2,1,0:T(8,128)(2,1)} %bitcast.19), calls=%async_computation.2 | async-start | bytes 3145728 | tf_op jit(solution)/shard_map/all_to_all | solution.py:317
  106.2 1.4 copy-start.1
  109.1 15.2 %collective-permute-start.8 = (bf16[128,2304]{1,0:T(8,128)(2,1)S(1)}, bf16[128,2304]{1,0:T(8,128)(2,1)S(1)}, u32[]{:S(2)}, u32[]{:S(2)}) collective-permute-start(bf16[128,2304]{1,0:T(8,128)(2,1)S(1)} %get-tuple-element.86), channel_id=1, source_target_pairs={{0,32},{16,48},{32,64},{48,80},{64,96},{80,112},{96,128},{112,144}... | collective-permute-start | bytes 1769480 | tf_op jit(solution)/shard_map/ppermute | solution.py:36
  111.0 18.2 %copy-start.33 = (f32[256,1]{1,0:T(8,128)S(1)}, f32[256,1]{1,0:T(8,128)}, u32[]{:S(2)}) copy-start(f32[256,1]{1,0:T(8,128)} %get-tuple-element.91) | copy-start | bytes 3076
  111.0 13.4 %collective-permute-start.9 = (bf16[128,2304]{1,0:T(8,128)(2,1)S(1)}, bf16[128,2304]{1,0:T(8,128)(2,1)S(1)}, u32[]{:S(2)}, u32[]{:S(2)}) collective-permute-start(bf16[128,2304]{1,0:T(8,128)(2,1)S(1)} %get-tuple-element.87), channel_id=1, source_target_pairs={{0,224},{16,240},{32,0},{48,16},{64,32},{80,48},{96,64},{112,80},{... | collective-permute-start | bytes 1769480 | tf_op jit(solution)/shard_map/ppermute | solution.py:36
  125.6 14.6 %collective-permute-start.10 = (bf16[128,2304]{1,0:T(8,128)(2,1)}, bf16[128,2304]{1,0:T(8,128)(2,1)}, u32[]{:S(2)}, u32[]{:S(2)}) collective-permute-start(bf16[128,2304]{1,0:T(8,128)(2,1)} %get-tuple-element.88), channel_id=1, source_target_pairs={{0,32},{16,48},{32,64},{48,80},{64,96},{80,112},{96,128},{112,144}... | collective-permute-start | bytes 1769480 | tf_op jit(solution)/shard_map/ppermute | solution.py:36
  127.1 13.1 %collective-permute-start.11 = (bf16[128,2304]{1,0:T(8,128)(2,1)}, bf16[128,2304]{1,0:T(8,128)(2,1)}, u32[]{:S(2)}, u32[]{:S(2)}) collective-permute-start(bf16[128,2304]{1,0:T(8,128)(2,1)} %get-tuple-element.89), channel_id=1, source_target_pairs={{0,224},{16,240},{32,0},{48,16},{64,32},{80,48},{96,64},{112,80},{... | collective-permute-start | bytes 1769480 | tf_op jit(solution)/shard_map/ppermute | solution.py:36
  129.9 10.3 %copy-start.2 = (bf16[1024,768]{1,0:T(8,128)(2,1)S(1)}, bf16[1024,768]{1,0:T(8,128)(2,1)}, u32[]{:S(2)}) copy-start(bf16[1024,768]{1,0:T(8,128)(2,1)} %copy-done) | copy-start | bytes 4718596
  (1 other events, 0.7 us)

commit v6 on v2

--- a/solution.py
+++ b/solution.py
@@ -1,3 +1,5 @@
+import functools
+
 import jax
 import jax.numpy as jnp
 from jax import lax
@@ -53,18 +55,16 @@
         out[:, edge:] = down_ref[rows, :]
 
 
-def join_kernel(forward_ref, backward_ref, pre_front, down_front, pre_back, down_back, front_out, back_out):
-    half = forward_ref.shape[0]
-    front, back = chunk_of(pre_front, down_front), chunk_of(pre_back, down_back)
-    front_out[:half] = f32_sum(forward_ref[...], front[:half])
-    front_out[half:] = front[half:]
-    back_out[:half] = back[:half]
-    back_out[half:] = f32_sum(backward_ref[...], back[half:])
-
-
-def add_kernel(forward_ref, backward_ref, pre_front, down_front, pre_back, down_back, front_out, back_out):
-    front_out[...] = f32_sum(forward_ref[...], chunk_of(pre_front, down_front))
-    back_out[...] = f32_sum(backward_ref[...], chunk_of(pre_back, down_back))
+def join_kernel(first, arrived_ref, pre_ref, down_ref, out_ref):
+    half = arrived_ref.shape[0]
+    chunk = chunk_of(pre_ref, down_ref)
+    added, rest = (slice(0, half), slice(half, None)) if first else (slice(half, None), slice(0, half))
+    out_ref[added] = f32_sum(arrived_ref[...], chunk[added])
+    out_ref[rest] = chunk[rest]
+
+
+def add_kernel(arrived_ref, pre_ref, down_ref, out_ref):
+    out_ref[...] = f32_sum(arrived_ref[...], chunk_of(pre_ref, down_ref))
 
 
 def finish_kernel(forward_ref, backward_ref, pre_ref, down_ref, gate_out, up_out, down_out):
@@ -81,12 +81,13 @@
 
 
 class Sums:
-    def __init__(self, far, parts, block, chips):
-        self.parts, self.block, self.chips = parts, block, chips
-        self.widths = [part.shape[1] for part in parts]
+    def __init__(self, far, block, chips):
+        self.block, self.chips = block, chips
+        self.widths = [chunk.shape[1] for chunk in far]
         self.distance = chips // 2
         half = jax.ShapeDtypeStruct((block // 2, sum(self.widths)), BF16)
-        self.send(call(split_kernel, (half, half), [VMEM, VMEM], far, 8, 1, 1))
+        self.operands = call(split_kernel, (half, half), [VMEM, VMEM], far, 8, 1, 1)
+        self.send(self.operands)
 
     def specs(self, away):
         place = away % self.chips
@@ -96,16 +97,19 @@
         self.moving = (next_chip(operands[0], 1), next_chip(operands[1], -1))
 
     def step(self):
-        kernel = join_kernel if self.distance == self.chips // 2 else add_kernel
+        joins = self.distance == self.chips // 2
         self.distance -= 1
         out = jax.ShapeDtypeStruct((self.block, sum(self.widths)), BF16)
-        return call(
-            kernel,
-            (out, out),
-            [VMEM, VMEM, *self.specs(self.distance), *self.specs(-self.distance)],
-            (*self.moving, *self.parts, *self.parts),
-            12, 1, 1, (1,),
-        )
+        return [
+            call(
+                functools.partial(join_kernel, sign > 0) if joins else add_kernel,
+                out,
+                [VMEM, *self.specs(sign * self.distance)],
+                (arrived, *self.parts),
+                12, 1, 1, (1,),
+            )
+            for sign, arrived in zip((1, -1), self.moving)
+        ]
 
     def finish(self, out_shapes, after):
         arrived, _ = lax.optimization_barrier((self.moving, after))
@@ -118,10 +122,9 @@
         )
 
 
-def select_kernel(most, base_ref, picks_ref, tokens_ref, select_ref, turned_ref, out_ref):
+def select_matrix(most, tok_dev, base_ref, picks_ref):
     local = picks_ref[...] - base_ref[0]
     experts, slots = local.shape
-    tok_dev = tokens_ref.shape[0]
     below = jnp.sum((local < 0).astype(F32), axis=1, keepdims=True).astype(I32)
     counter = lax.broadcasted_iota(I32, (most, 1), 0)
     spread = jnp.concatenate(
@@ -132,11 +135,17 @@
     hit = (position == wanted) & (spread >= 0) & (spread < tok_dev)
     token = jnp.sum(jnp.where(hit, spread + 1, 0).astype(F32), axis=1, keepdims=True) - 1.0
     token_range = lax.broadcasted_iota(I32, (spread.shape[0], tok_dev), 1).astype(F32)
-    hot = (token_range == token).astype(F32)
-    select = hot.astype(BF16)
+    return (token_range == token).astype(F32)
+
+
+def select_kernel(most, base_ref, picks_ref, tokens_ref, select_ref, out_ref):
+    select = select_matrix(most, tokens_ref.shape[0], base_ref, picks_ref).astype(BF16)
     select_ref[...] = select
-    turned_ref[...] = hot.T.astype(BF16)
     out_ref[...] = dot_nn(select, tokens_ref[...]).astype(BF16)
+
+
+def collect_matrix_kernel(most, base_ref, picks_ref, out_ref):
+    out_ref[...] = select_matrix(most, out_ref.shape[0], base_ref, picks_ref).T.astype(BF16)
 
 
 def gather_kernel(select_ref, tokens_ref, out_ref):
@@ -240,9 +249,9 @@
 
     table = picks[0]
     base = (self_index * tok_dev).astype(I32).reshape(1)
-    select, select_turned, out_rows = call(
+    select, out_rows = call(
         lambda *refs: select_kernel(most, *refs),
-        (shape(padded, tok_dev), shape(tok_dev, padded), shape(padded, width)),
+        (shape(padded, tok_dev), shape(padded, width)),
         [SMEM, VMEM, VMEM],
         (base, table, tokens),
         16, 2 * padded * tok_dev * width, 4 * padded * width,
@@ -268,6 +277,13 @@
         (shape(slot_count, padded), shape(padded, slot_count)),
         [VMEM],
         (own.reshape(slot_count, 1),),
+        8, 8 * slot_count * padded, 2 * slot_count * padded,
+    )
+    select_turned = call(
+        functools.partial(collect_matrix_kernel, most),
+        shape(tok_dev, padded),
+        [SMEM, VMEM],
+        (base, table),
         8, 8 * slot_count * padded, 2 * slot_count * padded,
     )
     compact_shapes = (
@@ -311,10 +327,13 @@
     )
     pre_both = jnp.concatenate([pre_grads, swap_cores(pre_grads)], axis=0)
 
-    def parts_of(columns):
+    def parts_of(columns, after=None):
+        sources = (rows_both, pre_both, scaled_both, hidden_both)
+        if after is not None:
+            sources, _ = lax.optimization_barrier((sources, after))
         return (
-            dot_tn(rows_both[:, columns], pre_both).astype(BF16),
-            dot_tn(scaled_both[:, columns], hidden_both).astype(BF16),
+            dot_tn(sources[0][:, columns], sources[1]).astype(BF16),
+            dot_tn(sources[2][:, columns], sources[3]).astype(BF16),
         )
 
     def give_back(pre_grads):
@@ -338,8 +357,8 @@
     if chips > 1:
         farthest = chips // 2
         far = parts_of(slice(farthest * block, (farthest + 1) * block))
-        parts = parts_of(slice(None))
-        sums = Sums(far, parts, block, chips)
+        sums = Sums(far, block, chips)
+        sums.parts = parts_of(slice(None), sums.operands)
         returning = give_back(pre_grads)
         returned = None
         while sums.distance > 1:

time: 137 us -> 136 us (level)
  waiting for transfers between devices: 51.3 us -> 46.8 us
  Pallas kernels: 21.6 us -> 24.3 us
    ppermute x8, waiting for transfers between devices: 25.4 us -> 21.4 us  [next_chip(): lax.ppermute(array, 'dp', [(i, (i + 2 * sign) % size) for i in range(size)])]
    pallas_call x13 -> x17, Pallas kernels: 21.6 us -> 24.3 us  [call(): pl.pallas_call(kernel, grid=grid, out_shape=out_shapes, in_specs=in_specs...]
    unnamed x42 -> x48, local copies, waits for them, and re-layouts: 10.4 us -> 10.4 us
  transfers between devices with their start and end apart: 15 -> 15, of which waited for: 8 -> 8; matrix products, arithmetic and copies ran while one was open for 10% -> 10% of each run, Pallas kernels for 11% -> 14%
where the time goes in v6:
time: 136 us; the launch traced here: 134 us
  waiting for transfers between devices  46.8 us (34%)
  starting transfers between devices  37.3 us (27%)
  Pallas kernels  24.3 us (18%)
  local copies, waits for them, and re-layouts  10.8 us (8%)
  matrix products  8.63 us (6%)
  other arithmetic  5.27 us (4%)
    pallas_call x17, Pallas kernels, call(): pl.pallas_call(kernel, grid=grid, out_shape=out_shapes, in_specs=in_specs...  24.3 us
    all_to_all x3, waiting for transfers between devices, exchange(): lax.all_to_all(shaped, 'expert', 0, 0, tiled=True).reshape(padded, width)  23.2 us
    ppermute x8, waiting for transfers between devices, next_chip(): lax.ppermute(array, 'dp', [(i, (i + 2 * sign) % size) for i in range(size)])  21.4 us
    all_to_all x3, starting transfers between devices, exchange(): lax.all_to_all(shaped, 'expert', 0, 0, tiled=True).reshape(padded, width)  20 us
    ppermute x8, starting transfers between devices, next_chip(): lax.ppermute(array, 'dp', [(i, (i + 2 * sign) % size) for i in range(size)])  16.1 us
    unnamed x48, local copies, waits for them, and re-layouts  10.4 us
    dot_general x2, matrix products, dot_nn(): return jnp.dot(left, right, preferred_element_type=F32)  5.1 us
    dot_general x4, matrix products, dot_tn(): lax.dot_general(left, right, (((0,), (0,)), ((), ())), preferred_element_...  3.53 us
  transfers between devices with their start and end apart: 15, of which 8 were waited for; matrix products, arithmetic and copies ran while one was open for 10% of the time, Pallas kernels for 14%

profile of v6, /device:TPU:2, one launch (start us, length us, event | category | flops | bytes accessed | tf_op | source)
XLA Modules:
  0.0 134.0 jit_solution(12554177587571769238)
XLA Ops:
  0.6 0.7 copy-done.15
  1.4 1.0 copy-done.19
  2.4 2.2 %shard_map.112 = (bf16[384,128]{1,0:T(8,128)(2,1)S(1)}, bf16[384,2048]{1,0:T(8,128)(2,1)}) custom-call(s32[1]{0:T(128)} %bitcast.base_ref.refs_0_, s32[16,256]{1,0:T(8,128)S(1)} %bitcast.38, bf16[128,2048]{1,0:T(8,128)(2,1)S(1)} %copy-done.19), custom_call_target="tpu_custom_call" | custom-call | flops 201326592 | bytes 3145728 | tf_op jit(solution)/shard_map/pallas_call | solution.py:220
  4.6 7.6 %all-to-all-start.1 = ((bf16[16,24,2048]{2,1,0:T(8,128)(2,1)}), bf16[16,24,2048]{2,1,0:T(8,128)(2,1)S(1)}, u32[]{:S(2)}, u32[]{:S(2)}) async-start(bf16[16,24,2048]{2,1,0:T(8,128)(2,1)} %bitcast.7), calls=%async_computation.1 | async-start | bytes 3145728 | tf_op jit(solution)/shard_map/all_to_all | solution.py:269
  12.7 0.6 shard_map.113
  13.2 1.2 copy-done.3
  14.4 0.6 pad_add_fusion.refs_0_
  15.0 18.6 %all-to-all-done.1 = bf16[16,24,2048]{2,1,0:T(8,128)(2,1)S(1)} async-done(((bf16[16,24,2048]{2,1,0:T(8,128)(2,1)}), bf16[16,24,2048]{2,1,0:T(8,128)(2,1)S(1)}, u32[]{:S(2)}, u32[]{:S(2)}) %all-to-all-start.1) | async-done | bytes 1572896 | tf_op jit(solution)/shard_map/all_to_all | solution.py:269
  33.6 6.3 %all-to-all-start = ((bf16[16,24,2048]{2,1,0:T(8,128)(2,1)}), bf16[16,24,2048]{2,1,0:T(8,128)(2,1)S(1)}, u32[]{:S(2)}, u32[]{:S(2)}) async-start(bf16[16,24,2048]{2,1,0:T(8,128)(2,1)} %bitcast.33), calls=%async_computation | async-start | bytes 3145728 | tf_op jit(solution)/shard_map/all_to_all | solution.py:269
  39.9 0.6 copy-done.17
  40.5 2.2 %shard_map.114 = (bf16[256,2048]{1,0:T(8,128)(2,1)S(1)}, bf16[256,1024]{1,0:T(8,128)(2,1)S(1)}, bf16[256,1024]{1,0:T(8,128)(2,1)}) custom-call(s32[2]{0:T(128)S(1)} %copy-done.17, bf16[256,384]{1,0:T(8,128)(2,1)S(1)} %get-tuple-element.36.refs_1_, bf16[384,2048]{1,0:T(8,128)(2,1)S(1)} %bitcast.31), custom_call_target="tpu_custom_call" | custom-call | flops 402653184 | bytes 4194304 | tf_op jit(solution)/shard_map/pallas_call | solution.py:220
  42.7 0.8 copy-done.11
  43.5 3.0 %fusion.3 = f32[256,768]{1,0:T(8,128)S(1)} fusion(bf16[256,2048]{1,0:T(8,128)(2,1)S(1)} %get-tuple-element.39, bf16[1,2048,768]{2,1,0:T(8,128)(2,1)} %param.12), kind=kOutput, calls=%fused_computation.18 | convolution fusion | flops 805306368 | bytes 4980736 | tf_op jit(solution)/shard_map/dot_general | solution.py:18
  46.5 2.1 %add_multiply_fusion = (f32[256,768]{1,0:T(8,128)S(1)}, bf16[256,768]{1,0:T(8,128)(2,1)S(1)}, f32[256,768]{1,0:T(8,128)}) fusion(f32[256,768]{1,0:T(8,128)S(1)} %fusion.3, bf16[256,2048]{1,0:T(8,128)(2,1)S(1)} %get-tuple-element.39, bf16[1,2048,768]{2,1,0:T(8,128)(2,1)S(1)} %copy-done.7), kind=kOutput, calls=%fused_computation.6 | convolution fusion | flops 807469056 | bytes 6946816 | tf_op jit(solution)/shard_map/dot_general | solution.py:18
  48.6 0.5 collective-permute-start
  49.3 1.7 %collective-permute-done.1 = bf16[256,768]{1,0:T(8,128)(2,1)} collective-permute-done((bf16[256,768]{1,0:T(8,128)(2,1)S(1)}, bf16[256,768]{1,0:T(8,128)(2,1)}, u32[]{:S(2)}, u32[]{:S(2)}) %collective-permute-start.1) | collective-permute-done | bytes 393248 | tf_op jit(solution)/shard_map/ppermute | solution.py:31
  51.0 1.9 %pad_maximum_fusion.1 = bf16[512,768]{1,0:T(8,128)(2,1)} fusion(bf16[256,768]{1,0:T(8,128)(2,1)} %collective-permute-done.1, bf16[256,768]{1,0:T(8,128)(2,1)S(1)} %get-tuple-element.44.refs_3_), kind=kLoop, calls=%fused_computation.5 | loop fusion | flops 1572864 | bytes 1572864 | tf_op jit(solution)/shard_map/concatenate | solution.py:307
  52.9 2.1 %pad_maximum_fusion = bf16[512,1024]{1,0:T(8,128)(2,1)} fusion(bf16[256,1024]{1,0:T(8,128)(2,1)} %collective-permute-done, bf16[256,1024]{1,0:T(8,128)(2,1)S(1)} %copy-done.12), kind=kLoop, calls=%fused_computation.4 | loop fusion | flops 2097152 | bytes 2097152 | tf_op jit(solution)/shard_map/concatenate | solution.py:300
  55.0 4.6 %all-to-all-done = bf16[16,24,2048]{2,1,0:T(8,128)(2,1)S(1)} async-done(((bf16[16,24,2048]{2,1,0:T(8,128)(2,1)}), bf16[16,24,2048]{2,1,0:T(8,128)(2,1)S(1)}, u32[]{:S(2)}, u32[]{:S(2)}) %all-to-all-start) | async-done | bytes 1572896 | tf_op jit(solution)/shard_map/all_to_all | solution.py:269
  59.6 1.4 %shard_map.115 = (bf16[256,2048]{1,0:T(8,128)(2,1)S(1)}, bf16[256,1024]{1,0:T(8,128)(2,1)S(1)}, bf16[256,1024]{1,0:T(8,128)(2,1)S(1)}) custom-call(s32[2]{0:T(128)S(1)} %copy-done.18, bf16[256,384]{1,0:T(8,128)(2,1)S(1)} %get-tuple-element.36.refs_1_, bf16[384,2048]{1,0:T(8,128)(2,1)S(1)} %bitcast.32, f32[256,1]{1,0:T(8,128)S(1)} %copy.13.refs_3_.refs_2_), custom_call_target="tpu_custom_call" | custom-call | flops 402653184 | bytes 4194304 | tf_op jit(solution)/shard_map/pallas_call | solution.py:220
  61.1 1.9 %copy-done.5 = bf16[1,768,2048]{2,1,0:T(8,128)(2,1)S(1)} copy-done((bf16[1,768,2048]{2,1,0:T(8,128)(2,1)S(1)}, bf16[1,768,2048]{2,1,0:T(8,128)(2,1)}, u32[]{:S(2)}) %copy-start.5) | copy-done | bytes 3145752
  63.0 1.1 shard_map.116
  64.2 0.6 collective-permute-start.2
  64.9 1.0 copy-done.20
  66.2 0.4 collective-permute-done.2
  67.6 2.0 %collective-permute-start.4 = (bf16[64,2304]{1,0:T(8,128)(2,1)S(1)}, bf16[64,2304]{1,0:T(8,128)(2,1)S(1)}, u32[]{:S(2)}, u32[]{:S(2)}) collective-permute-start(bf16[64,2304]{1,0:T(8,128)(2,1)S(1)} %get-tuple-element.53), channel_id=1, source_target_pairs={{0,32},{16,48},{32,64},{48,80},{64,96},{80,112},{96,128},{112,144}... | collective-permute-start | bytes 884744 | tf_op jit(solution)/shard_map/ppermute | solution.py:36
  69.6 4.2 %collective-permute-start.5 = (bf16[64,2304]{1,0:T(8,128)(2,1)S(1)}, bf16[64,2304]{1,0:T(8,128)(2,1)S(1)}, u32[]{:S(2)}, u32[]{:S(2)}) collective-permute-start(bf16[64,2304]{1,0:T(8,128)(2,1)S(1)} %get-tuple-element.54), channel_id=1, source_target_pairs={{0,224},{16,240},{32,0},{48,16},{64,32},{80,48},{96,64},{112,80},{... | collective-permute-start | bytes 884744 | tf_op jit(solution)/shard_map/ppermute | solution.py:36
  73.8 1.8 %convolution_convert_fusion.pre_ref = bf16[1024,1536]{1,0:T(8,128)(2,1)S(1)} fusion(bf16[512,1024]{1,0:T(8,128)(2,1)S(1)} %copy-done.21, bf16[512,1536]{1,0:T(8,128)(2,1)S(1)} %constant_dynamic-update-slice_fusion), kind=kOutput, calls=%fused_computation | convolution fusion | flops 1612185600 | bytes 5767168 | tf_op jit(solution)/shard_map/dot_general | solution.py:26
  75.6 1.0 convolution_convert_fusion.2.down_ref
  76.7 4.1 %collective-permute-done.4.arrived_ref = bf16[64,2304]{1,0:T(8,128)(2,1)S(1)} collective-permute-done((bf16[64,2304]{1,0:T(8,128)(2,1)S(1)}, bf16[64,2304]{1,0:T(8,128)(2,1)S(1)}, u32[]{:S(2)}, u32[]{:S(2)}) %collective-permute-start.4) | collective-permute-done | bytes 294944 | tf_op jit(solution)/shard_map/ppermute | solution.py:36
  80.7 0.9 shard_map.119
  81.7 0.9 shard_map.120
  82.6 3.2 %collective-permute-start.8 = (bf16[128,2304]{1,0:T(8,128)(2,1)}, bf16[128,2304]{1,0:T(8,128)(2,1)}, u32[]{:S(2)}, u32[]{:S(2)}) collective-permute-start(bf16[128,2304]{1,0:T(8,128)(2,1)} %shard_map.120), channel_id=1, source_target_pairs={{0,224},{16,240},{32,0},{48,16},{64,32},{80,48},{96,64},{112,80},{... | collective-permute-start | bytes 1769480 | tf_op jit(solution)/shard_map/ppermute | solution.py:36
  85.9 5.0 %shard_map.117 = bf16[384,2048]{1,0:T(8,128)(2,1)S(1)} custom-call(bf16[256,1536]{1,0:T(8,128)(2,1)S(1)} %get-tuple-element.47.refs_0_, bf16[2048,768]{1,0:T(8,128)(2,1)S(1)} %bitcast.37, bf16[2048,768]{1,0:T(8,128)(2,1)S(1)} %bitcast.36, bf16[384,256]{1,0:T(8,128)(2,1)S(1)} %get-tuple-element.48.refs_3_), custom_call_target="tpu_custom_call" | custom-call | flops 1610612736 | bytes 6291456 | tf_op jit(solution)/shard_map/pallas_call | solution.py:220
  90.8 1.2 copy-done.4
  92.0 6.2 %all-to-all-start.2 = ((bf16[16,24,2048]{2,1,0:T(8,128)(2,1)}), bf16[16,24,2048]{2,1,0:T(8,128)(2,1)}, u32[]{:S(2)}, u32[]{:S(2)}) async-start(bf16[16,24,2048]{2,1,0:T(8,128)(2,1)} %bitcast.34), calls=%async_computation.2 | async-start | bytes 3145728 | tf_op jit(solution)/shard_map/all_to_all | solution.py:269
  98.2 1.4 %copy-done.1 = bf16[1024,768]{1,0:T(8,128)(2,1)S(1)} copy-done((bf16[1024,768]{1,0:T(8,128)(2,1)S(1)}, bf16[1024,768]{1,0:T(8,128)(2,1)}, u32[]{:S(2)}) %copy-start.1) | copy-done | bytes 1572888
  99.6 1.2 shard_map.121
  100.9 1.2 shard_map.123
  102.1 3.3 %collective-permute-start.9 = (bf16[128,2304]{1,0:T(8,128)(2,1)S(1)}, bf16[128,2304]{1,0:T(8,128)(2,1)S(1)}, u32[]{:S(2)}, u32[]{:S(2)}) collective-permute-start(bf16[128,2304]{1,0:T(8,128)(2,1)S(1)} %shard_map.123), channel_id=1, source_target_pairs={{0,224},{16,240},{32,0},{48,16},{64,32},{80,48},{96,64},{112,80},{... | collective-permute-start | bytes 1769480 | tf_op jit(solution)/shard_map/ppermute | solution.py:36
  105.4 10.6 %collective-permute-done.7.arrived_ref = bf16[128,2304]{1,0:T(8,128)(2,1)S(1)} collective-permute-done((bf16[128,2304]{1,0:T(8,128)(2,1)S(1)}, bf16[128,2304]{1,0:T(8,128)(2,1)S(1)}, u32[]{:S(2)}, u32[]{:S(2)}) %collective-permute-start.7) | collective-permute-done | bytes 589856 | tf_op jit(solution)/shard_map/ppermute | solution.py:36
  116.0 1.0 shard_map.122
  116.9 0.9 shard_map.124
  117.9 3.3 %collective-permute-start.11 = (bf16[128,2304]{1,0:T(8,128)(2,1)}, bf16[128,2304]{1,0:T(8,128)(2,1)}, u32[]{:S(2)}, u32[]{:S(2)}) collective-permute-start(bf16[128,2304]{1,0:T(8,128)(2,1)} %shard_map.124), channel_id=1, source_target_pairs={{0,224},{16,240},{32,0},{48,16},{64,32},{80,48},{96,64},{112,80},{... | collective-permute-start | bytes 1769480 | tf_op jit(solution)/shard_map/ppermute | solution.py:36
  121.6 0.7 reduce
  122.2 2.8 %shard_map.125 = bf16[128,2048]{1,0:T(8,128)(2,1)} custom-call(bf16[128,384]{1,0:T(8,128)(2,1)S(1)} %shard_map.110.select_ref, bf16[384,2048]{1,0:T(8,128)(2,1)} %bitcast.14.tokens_ref), custom_call_target="tpu_custom_call" | custom-call | flops 201326592 | bytes 3145728 | tf_op jit(solution)/shard_map/pallas_call | solution.py:220
  125.0 6.5 %collective-permute-done.10.forward_ref = bf16[128,2304]{1,0:T(8,128)(2,1)} collective-permute-done((bf16[128,2304]{1,0:T(8,128)(2,1)}, bf16[128,2304]{1,0:T(8,128)(2,1)}, u32[]{:S(2)}, u32[]{:S(2)}) %collective-permute-start.10) | collective-permute-done | bytes 589856 | tf_op jit(solution)/shard_map/ppermute | solution.py:36
  131.8 2.3 %shard_map.126 = (bf16[1,128,768]{2,1,0:T(8,128)(2,1)}, bf16[1,128,768]{2,1,0:T(8,128)(2,1)}, bf16[1,768,128]{2,1,0:T(8,128)(2,1)}) custom-call(bf16[128,2304]{1,0:T(8,128)(2,1)} %collective-permute-done.10.forward_ref, bf16[128,2304]{1,0:T(8,128)(2,1)} %collective-permute-done.11.backward_ref, bf16[1024,1536]{1,0:T(8,128)(2,1)S(1)} %convolution_convert_fusion.pre_ref, ...), custom_call_target="tpu_custom_call" | custom-call | flops 1 | bytes 1 | tf_op jit(solution)/shard_map/pallas_call | solution.py:220
  (62 shorter events, 2.8 us)
Async XLA Ops:
  0.6 0.7 copy-start.15
  1.4 1.0 copy-start.19
  4.6 7.6 %copy-start.16 = (s32[1,16,256]{2,1,0:T(8,128)S(1)}, s32[1,16,256]{2,1,0:T(8,128)}, u32[]{:S(2)}) copy-start(s32[1,16,256]{2,1,0:T(8,128)} %param.9) | copy-start | bytes 49156
  4.6 8.1 %copy-start.10 = (bf16[128,2048]{1,0:T(8,128)(2,1)S(1)}, bf16[128,2048]{1,0:T(8,128)(2,1)}, u32[]{:S(2)}) copy-start(bf16[128,2048]{1,0:T(8,128)(2,1)} %tokens_ref.1) | copy-start | bytes 1572868
  4.6 29.0 %all-to-all-start.1 = ((bf16[16,24,2048]{2,1,0:T(8,128)(2,1)}), bf16[16,24,2048]{2,1,0:T(8,128)(2,1)S(1)}, u32[]{:S(2)}, u32[]{:S(2)}) async-start(bf16[16,24,2048]{2,1,0:T(8,128)(2,1)} %bitcast.7), calls=%async_computation.1 | async-start | bytes 3145728 | tf_op jit(solution)/shard_map/all_to_all | solution.py:269
  13.2 1.2 copy-start.3
  33.6 26.0 %all-to-all-start = ((bf16[16,24,2048]{2,1,0:T(8,128)(2,1)}), bf16[16,24,2048]{2,1,0:T(8,128)(2,1)S(1)}, u32[]{:S(2)}, u32[]{:S(2)}) async-start(bf16[16,24,2048]{2,1,0:T(8,128)(2,1)} %bitcast.33), calls=%async_computation | async-start | bytes 3145728 | tf_op jit(solution)/shard_map/all_to_all | solution.py:269
  39.9 0.7 copy-start.17
  42.7 0.8 copy-start.11
  43.5 3.0 %copy-start.7 = (bf16[1,2048,768]{2,1,0:T(8,128)(2,1)S(1)}, bf16[1,2048,768]{2,1,0:T(8,128)(2,1)}, u32[]{:S(2)}) copy-start(bf16[1,2048,768]{2,1,0:T(8,128)(2,1)} %param.11) | copy-start | bytes 9437188
  46.5 2.6 %copy-start.22 = (f32[1,1,256]{2,1,0:T(1,128)S(1)}, f32[1,1,256]{2,1,0:T(1,128)}, u32[]{:S(2)}) copy-start(f32[1,1,256]{2,1,0:T(1,128)} %param.10) | copy-start | bytes 3076
  48.6 2.4 %collective-permute-start.1 = (bf16[256,768]{1,0:T(8,128)(2,1)S(1)}, bf16[256,768]{1,0:T(8,128)(2,1)}, u32[]{:S(2)}, u32[]{:S(2)}) collective-permute-start(bf16[256,768]{1,0:T(8,128)(2,1)S(1)} %get-tuple-element.44.refs_3_), channel_id=1, source_target_pairs={{0,16},{16,0},{32,48},{48,32},{64,80},{80,64},{96,112},{112,96},{1... | collective-permute-start | bytes 1179656 | tf_op jit(solution)/shard_map/ppermute | solution.py:31
  48.6 4.3 %collective-permute-start = (bf16[256,1024]{1,0:T(8,128)(2,1)}, bf16[256,1024]{1,0:T(8,128)(2,1)}, u32[]{:S(2)}, u32[]{:S(2)}) collective-permute-start(bf16[256,1024]{1,0:T(8,128)(2,1)} %get-tuple-element.41), channel_id=1, source_target_pairs={{0,16},{16,0},{32,48},{48,32},{64,80},{80,64},{96,112},{112,96},{1... | collective-permute-start | bytes 1572872 | tf_op jit(solution)/shard_map/ppermute | solution.py:31
  49.3 3.7 %copy-start.12 = (bf16[256,1024]{1,0:T(8,128)(2,1)S(1)}, bf16[256,1024]{1,0:T(8,128)(2,1)}, u32[]{:S(2)}) copy-start(bf16[256,1024]{1,0:T(8,128)(2,1)} %copy-done.11) | copy-start | bytes 1572868
  49.3 10.3 %copy-start.18 = (s32[2]{0:T(128)S(1)}, s32[2]{0:T(128)}, u32[]{:S(2)}) copy-start(s32[2]{0:T(128)} %pad_add_fusion.refs_0_) | copy-start | bytes 28
  59.6 1.5 %copy-start.9 = (f32[256,768]{1,0:T(8,128)S(1)}, f32[256,768]{1,0:T(8,128)}, u32[]{:S(2)}) copy-start(f32[256,768]{1,0:T(8,128)} %get-tuple-element.46.refs_5_) | copy-start | bytes 2359300
  61.0 3.9 %collective-permute-start.3 = (bf16[256,1024]{1,0:T(8,128)(2,1)S(1)}, bf16[256,1024]{1,0:T(8,128)(2,1)S(1)}, u32[]{:S(2)}, u32[]{:S(2)}) collective-permute-start(bf16[256,1024]{1,0:T(8,128)(2,1)S(1)} %get-tuple-element.51), channel_id=1, source_target_pairs={{0,16},{16,0},{32,48},{48,32},{64,80},{80,64},{96,112},{112,96},{1... | collective-permute-start | bytes 1572872 | tf_op jit(solution)/shard_map/ppermute | solution.py:31
  61.1 1.9 %copy-start.5 = (bf16[1,768,2048]{2,1,0:T(8,128)(2,1)S(1)}, bf16[1,768,2048]{2,1,0:T(8,128)(2,1)}, u32[]{:S(2)}) copy-start(bf16[1,768,2048]{2,1,0:T(8,128)(2,1)} %param.13) | copy-start | bytes 9437188
  64.2 0.8 copy-start.13
  64.2 2.5 %collective-permute-start.2 = (bf16[256,1536]{1,0:T(8,128)(2,1)S(1)}, bf16[256,1536]{1,0:T(8,128)(2,1)S(1)}, u32[]{:S(2)}, u32[]{:S(2)}) collective-permute-start(bf16[256,1536]{1,0:T(8,128)(2,1)S(1)} %get-tuple-element.47.refs_0_), channel_id=1, source_target_pairs={{0,16},{16,0},{32,48},{48,32},{64,80},{80,64},{96,112},{112,96},{1... | collective-permute-start | bytes 2359304 | tf_op jit(solution)/shard_map/ppermute | solution.py:31
  64.8 1.1 copy-start.20
  65.9 1.2 copy-start.21
  67.6 13.1 %collective-permute-start.4 = (bf16[64,2304]{1,0:T(8,128)(2,1)S(1)}, bf16[64,2304]{1,0:T(8,128)(2,1)S(1)}, u32[]{:S(2)}, u32[]{:S(2)}) collective-permute-start(bf16[64,2304]{1,0:T(8,128)(2,1)S(1)} %get-tuple-element.53), channel_id=1, source_target_pairs={{0,32},{16,48},{32,64},{48,80},{64,96},{80,112},{96,128},{112,144}... | collective-permute-start | bytes 884744 | tf_op jit(solution)/shard_map/ppermute | solution.py:36
  69.6 12.1 %collective-permute-start.5 = (bf16[64,2304]{1,0:T(8,128)(2,1)S(1)}, bf16[64,2304]{1,0:T(8,128)(2,1)S(1)}, u32[]{:S(2)}, u32[]{:S(2)}) collective-permute-start(bf16[64,2304]{1,0:T(8,128)(2,1)S(1)} %get-tuple-element.54), channel_id=1, source_target_pairs={{0,224},{16,240},{32,0},{48,16},{64,32},{80,48},{96,64},{112,80},{... | collective-permute-start | bytes 884744 | tf_op jit(solution)/shard_map/ppermute | solution.py:36
  76.7 5.0 %copy-start = (bf16[1024,768]{1,0:T(8,128)(2,1)}, bf16[1024,768]{1,0:T(8,128)(2,1)S(1)}, u32[]{:S(2)}) copy-start(bf16[1024,768]{1,0:T(8,128)(2,1)S(1)} %convolution_convert_fusion.2.down_ref) | copy-start | bytes 4718596
  80.7 5.1 %copy-start.8 = (bf16[1,2048,768]{2,1,0:T(8,128)(2,1)S(1)}, bf16[1,2048,768]{2,1,0:T(8,128)(2,1)}, u32[]{:S(2)}) copy-start(bf16[1,2048,768]{2,1,0:T(8,128)(2,1)} %param.11) | copy-start | bytes 9437188
  81.7 4.2 %copy-start.6 = (bf16[1,2048,768]{2,1,0:T(8,128)(2,1)S(1)}, bf16[1,2048,768]{2,1,0:T(8,128)(2,1)}, u32[]{:S(2)}) copy-start(bf16[1,2048,768]{2,1,0:T(8,128)(2,1)} %param.12) | copy-start | bytes 9437188
  81.7 16.5 %collective-permute-start.6 = (bf16[128,2304]{1,0:T(8,128)(2,1)}, bf16[128,2304]{1,0:T(8,128)(2,1)}, u32[]{:S(2)}, u32[]{:S(2)}) collective-permute-start(bf16[128,2304]{1,0:T(8,128)(2,1)} %shard_map.119), channel_id=1, source_target_pairs={{0,32},{16,48},{32,64},{48,80},{64,96},{80,112},{96,128},{112,144}... | collective-permute-start | bytes 1769480 | tf_op jit(solution)/shard_map/ppermute | solution.py:36
  82.6 18.2 %collective-permute-start.8 = (bf16[128,2304]{1,0:T(8,128)(2,1)}, bf16[128,2304]{1,0:T(8,128)(2,1)}, u32[]{:S(2)}, u32[]{:S(2)}) collective-permute-start(bf16[128,2304]{1,0:T(8,128)(2,1)} %shard_map.120), channel_id=1, source_target_pairs={{0,224},{16,240},{32,0},{48,16},{64,32},{80,48},{96,64},{112,80},{... | collective-permute-start | bytes 1769480 | tf_op jit(solution)/shard_map/ppermute | solution.py:36
  90.8 1.2 copy-start.4
  92.0 30.2 %all-to-all-start.2 = ((bf16[16,24,2048]{2,1,0:T(8,128)(2,1)}), bf16[16,24,2048]{2,1,0:T(8,128)(2,1)}, u32[]{:S(2)}, u32[]{:S(2)}) async-start(bf16[16,24,2048]{2,1,0:T(8,128)(2,1)} %bitcast.34), calls=%async_computation.2 | async-start | bytes 3145728 | tf_op jit(solution)/shard_map/all_to_all | solution.py:269
  98.2 1.4 %copy-start.1 = (bf16[1024,768]{1,0:T(8,128)(2,1)S(1)}, bf16[1024,768]{1,0:T(8,128)(2,1)}, u32[]{:S(2)}) copy-start(bf16[1024,768]{1,0:T(8,128)(2,1)} %copy-done) | copy-start | bytes 4718596
  100.8 15.2 %collective-permute-start.7 = (bf16[128,2304]{1,0:T(8,128)(2,1)S(1)}, bf16[128,2304]{1,0:T(8,128)(2,1)S(1)}, u32[]{:S(2)}, u32[]{:S(2)}) collective-permute-start(bf16[128,2304]{1,0:T(8,128)(2,1)S(1)} %shard_map.121), channel_id=1, source_target_pairs={{0,32},{16,48},{32,64},{48,80},{64,96},{80,112},{96,128},{112,144}... | collective-permute-start | bytes 1769480 | tf_op jit(solution)/shard_map/ppermute | solution.py:36
  102.1 14.9 %collective-permute-start.9 = (bf16[128,2304]{1,0:T(8,128)(2,1)S(1)}, bf16[128,2304]{1,0:T(8,128)(2,1)S(1)}, u32[]{:S(2)}, u32[]{:S(2)}) collective-permute-start(bf16[128,2304]{1,0:T(8,128)(2,1)S(1)} %shard_map.123), channel_id=1, source_target_pairs={{0,224},{16,240},{32,0},{48,16},{64,32},{80,48},{96,64},{112,80},{... | collective-permute-start | bytes 1769480 | tf_op jit(solution)/shard_map/ppermute | solution.py:36
  116.9 4.6 %copy-start.14 = (f32[256,1]{1,0:T(8,128)S(1)}, f32[256,1]{1,0:T(8,128)}, u32[]{:S(2)}) copy-start(f32[256,1]{1,0:T(8,128)} %copy-done.13) | copy-start | bytes 3076
  116.9 14.6 %collective-permute-start.10 = (bf16[128,2304]{1,0:T(8,128)(2,1)}, bf16[128,2304]{1,0:T(8,128)(2,1)}, u32[]{:S(2)}, u32[]{:S(2)}) collective-permute-start(bf16[128,2304]{1,0:T(8,128)(2,1)} %shard_map.122), channel_id=1, source_target_pairs={{0,32},{16,48},{32,64},{48,80},{64,96},{80,112},{96,128},{112,144}... | collective-permute-start | bytes 1769480 | tf_op jit(solution)/shard_map/ppermute | solution.py:36
  117.9 13.9 %collective-permute-start.11 = (bf16[128,2304]{1,0:T(8,128)(2,1)}, bf16[128,2304]{1,0:T(8,128)(2,1)}, u32[]{:S(2)}, u32[]{:S(2)}) collective-permute-start(bf16[128,2304]{1,0:T(8,128)(2,1)} %shard_map.124), channel_id=1, source_target_pairs={{0,224},{16,240},{32,0},{48,16},{64,32},{80,48},{96,64},{112,80},{... | collective-permute-start | bytes 1769480 | tf_op jit(solution)/shard_map/ppermute | solution.py:36
  122.2 9.6 %copy-start.2 = (bf16[1024,768]{1,0:T(8,128)(2,1)S(1)}, bf16[1024,768]{1,0:T(8,128)(2,1)}, u32[]{:S(2)}) copy-start(bf16[1024,768]{1,0:T(8,128)(2,1)} %copy-done) | copy-start | bytes 4718596

commit v7 on v6

--- a/solution.py
+++ b/solution.py
@@ -77,7 +77,7 @@
     hidden = gate_out.shape[2]
     gate_out[0] = total[:, :hidden].astype(BF16)
     up_out[0] = total[:, hidden : 2 * hidden].astype(BF16)
-    down_out[0] = total[:, 2 * hidden :].T.astype(BF16)
+    down_out[0] = total[:, 2 * hidden :].astype(BF16).T
 
 
 class Sums:
@@ -106,7 +106,7 @@
                 out,
                 [VMEM, *self.specs(sign * self.distance)],
                 (arrived, *self.parts),
-                12, 1, 1, (1,),
+                54 if self.distance == self.chips // 2 - 2 else 12, 1, 1, (1,),
             )
             for sign, arrived in zip((1, -1), self.moving)
         ]
@@ -297,18 +297,18 @@
         (place, take, arrived_rows),
         *compact_cost,
     )
-    rows_both = jnp.concatenate([rows_keep, swap_cores(rows_give)], axis=0)
+    rows_got = swap_cores(rows_give)
     gate_pre = dot_nn(rows, w_gate[0])
     up_pre = dot_nn(rows, w_up[0])
     sigmoid_gate = jax.nn.sigmoid(gate_pre)
     activated = gate_pre * sigmoid_gate
     slope = up_pre * sigmoid_gate * (1.0 + gate_pre * (1.0 - sigmoid_gate))
     hidden = (activated * up_pre).astype(BF16)
-    hidden_both = jnp.concatenate([hidden, swap_cores(hidden)], axis=0)
+    hidden_got = swap_cores(hidden)
 
     gate_rows = gates.reshape(slot_count, 1)
-    arrived_grads, hidden, slope, activated, rows_both, hidden_both = lax.optimization_barrier(
-        (arrived_grads, hidden, slope, activated, rows_both, hidden_both)
+    arrived_grads, hidden, slope, activated, rows_got, hidden_got = lax.optimization_barrier(
+        (arrived_grads, hidden, slope, activated, rows_got, hidden_got)
     )
     grads, scaled_keep, scaled_give = call(
         lambda *refs: compact_kernel(chips, *refs),
@@ -325,6 +325,9 @@
         (grads, w_down[0], gate_rows, hidden, slope, activated),
         16, 2 * slot_count * width * hidden_width, 2 * width * hidden_width,
     )
+    late_sides, _ = lax.optimization_barrier(((rows_keep, rows_got, hidden, hidden_got), pre_grads))
+    rows_both = jnp.concatenate(late_sides[:2], axis=0)
+    hidden_both = jnp.concatenate(late_sides[2:], axis=0)
     pre_both = jnp.concatenate([pre_grads, swap_cores(pre_grads)], axis=0)
 
     def parts_of(columns, after=None):

time: 136 us -> 137 us (level)
  other arithmetic: 5.27 us -> 0.75 us
  waiting for transfers between devices: 46.8 us -> 51.1 us
  Pallas kernels: 24.3 us -> 26.8 us
    all_to_all x3, waiting for transfers between devices: 23.2 us -> 29.4 us  [exchange(): lax.all_to_all(shaped, 'expert', 0, 0, tiled=True).reshape(padded, width)]
    concatenate x2 -> x0, other arithmetic: 4.01 us -> none  [the longest x1 2.08 us: body(): rows_both = jnp.concatenate([rows_keep, swap_cores(rows_give)], axis=0)]
    unnamed x48 -> x46, local copies, waits for them, and re-layouts: 10.4 us -> 7.33 us
    pallas_call x17, Pallas kernels: 24.3 us -> 26.8 us  [call(): pl.pallas_call(kernel, grid=grid, out_shape=out_shapes, in_specs=in_specs...]
    concatenate x0 -> x2, local copies, waits for them, and re-layouts: none -> 2.1 us  [the longest x1 1.08 us: body(): rows_both = jnp.concatenate(late_sides[:2], axis=0)]
    ppermute x4, waiting for transfers between devices: 2.15 us -> 0.16 us  [swap_cores(): return lax.ppermute(array, 'dp', [(i, i ^ 1) for i in range(size)])]
  transfers between devices with their start and end apart: 15 -> 15, of which waited for: 8 -> 8; matrix products, arithmetic and copies ran while one was open for 10% -> 9% of each run, Pallas kernels for 14% -> 15%
where the time goes in v7:
time: 137 us; the launch traced here: 136 us
  waiting for transfers between devices  51.1 us (37%)
  starting transfers between devices  37.5 us (27%)
  Pallas kernels  26.8 us (20%)
  local copies, waits for them, and re-layouts  9.8 us (7%)
  matrix products  8.66 us (6%)
    all_to_all x3, waiting for transfers between devices, exchange(): lax.all_to_all(shaped, 'expert', 0, 0, tiled=True).reshape(padded, width)  29.4 us
    pallas_call x17, Pallas kernels, call(): pl.pallas_call(kernel, grid=grid, out_shape=out_shapes, in_specs=in_specs...  26.8 us
    ppermute x8, waiting for transfers between devices, next_chip(): lax.ppermute(array, 'dp', [(i, (i + 2 * sign) % size) for i in range(size)])  21.5 us
    all_to_all x3, starting transfers between devices, exchange(): lax.all_to_all(shaped, 'expert', 0, 0, tiled=True).reshape(padded, width)  20.2 us
    ppermute x8, starting transfers between devices, next_chip(): lax.ppermute(array, 'dp', [(i, (i + 2 * sign) % size) for i in range(size)])  16.2 us
    unnamed x46, local copies, waits for them, and re-layouts  7.33 us
    dot_general x2, matrix products, dot_nn(): return jnp.dot(left, right, preferred_element_type=F32)  5.09 us
    dot_general x4, matrix products, dot_tn(): lax.dot_general(left, right, (((0,), (0,)), ((), ())), preferred_element_...  3.58 us
  transfers between devices with their start and end apart: 15, of which 8 were waited for; matrix products, arithmetic and copies ran while one was open for 9% of the time, Pallas kernels for 15%

profile of v7, /device:TPU:2, one launch (start us, length us, event | category | flops | bytes accessed | tf_op | source)
XLA Modules:
  0.0 135.6 jit_solution(17702460518501239353)
XLA Ops:
  0.6 0.7 copy-done.16
  1.4 1.0 copy-done.18
  2.4 2.2 %shard_map.112 = (bf16[384,128]{1,0:T(8,128)(2,1)S(1)}, bf16[384,2048]{1,0:T(8,128)(2,1)}) custom-call(s32[1]{0:T(128)} %bitcast.base_ref.refs_0_, s32[16,256]{1,0:T(8,128)S(1)} %bitcast.37, bf16[128,2048]{1,0:T(8,128)(2,1)S(1)} %copy-done.18), custom_call_target="tpu_custom_call" | custom-call | flops 201326592 | bytes 3145728 | tf_op jit(solution)/shard_map/pallas_call | solution.py:220
  4.6 7.6 %all-to-all-start.1 = ((bf16[16,24,2048]{2,1,0:T(8,128)(2,1)}), bf16[16,24,2048]{2,1,0:T(8,128)(2,1)S(1)}, u32[]{:S(2)}, u32[]{:S(2)}) async-start(bf16[16,24,2048]{2,1,0:T(8,128)(2,1)} %bitcast.7), calls=%async_computation.1 | async-start | bytes 3145728 | tf_op jit(solution)/shard_map/all_to_all | solution.py:269
  12.2 0.6 shard_map.113
  12.8 1.2 copy-done.5
  13.9 19.7 %all-to-all-done.1 = bf16[16,24,2048]{2,1,0:T(8,128)(2,1)S(1)} async-done(((bf16[16,24,2048]{2,1,0:T(8,128)(2,1)}), bf16[16,24,2048]{2,1,0:T(8,128)(2,1)S(1)}, u32[]{:S(2)}, u32[]{:S(2)}) %all-to-all-start.1) | async-done | bytes 1572896 | tf_op jit(solution)/shard_map/all_to_all | solution.py:269
  33.6 6.4 %all-to-all-start = ((bf16[16,24,2048]{2,1,0:T(8,128)(2,1)}), bf16[16,24,2048]{2,1,0:T(8,128)(2,1)S(1)}, u32[]{:S(2)}, u32[]{:S(2)}) async-start(bf16[16,24,2048]{2,1,0:T(8,128)(2,1)} %bitcast.33), calls=%async_computation | async-start | bytes 3145728 | tf_op jit(solution)/shard_map/all_to_all | solution.py:269
  40.2 0.3 shard_map.111
  40.5 0.7 copy-done.14
  41.2 2.2 %shard_map.114 = (bf16[256,2048]{1,0:T(8,128)(2,1)S(1)}, bf16[256,1024]{1,0:T(8,128)(2,1)S(1)}, bf16[256,1024]{1,0:T(8,128)(2,1)}) custom-call(s32[2]{0:T(128)S(1)} %pad_add_fusion.refs_0_, bf16[256,384]{1,0:T(8,128)(2,1)S(1)} %get-tuple-element.40.refs_1_, bf16[384,2048]{1,0:T(8,128)(2,1)S(1)} %bitcast.32), custom_call_target="tpu_custom_call" | custom-call | flops 402653184 | bytes 4194304 | tf_op jit(solution)/shard_map/pallas_call | solution.py:220
  43.4 0.8 copy-done.11
  44.2 3.0 %fusion.3 = f32[256,768]{1,0:T(8,128)S(1)} fusion(bf16[256,2048]{1,0:T(8,128)(2,1)S(1)} %get-tuple-element.43, bf16[1,2048,768]{2,1,0:T(8,128)(2,1)} %param.12), kind=kOutput, calls=%fused_computation.20 | convolution fusion | flops 805306368 | bytes 4980736 | tf_op jit(solution)/shard_map/dot_general | solution.py:18
  47.2 2.1 %add_multiply_fusion = (f32[256,768]{1,0:T(8,128)S(1)}, bf16[256,768]{1,0:T(8,128)(2,1)S(1)}, f32[256,768]{1,0:T(8,128)}) fusion(f32[256,768]{1,0:T(8,128)S(1)} %fusion.3, bf16[256,2048]{1,0:T(8,128)(2,1)S(1)} %get-tuple-element.43, bf16[1,2048,768]{2,1,0:T(8,128)(2,1)S(1)} %copy-done.8), kind=kOutput, calls=%fused_computation.4 | convolution fusion | flops 807469056 | bytes 6946816 | tf_op jit(solution)/shard_map/dot_general | solution.py:18
  49.3 0.5 collective-permute-start.1
  50.0 9.8 %all-to-all-done = bf16[16,24,2048]{2,1,0:T(8,128)(2,1)S(1)} async-done(((bf16[16,24,2048]{2,1,0:T(8,128)(2,1)}), bf16[16,24,2048]{2,1,0:T(8,128)(2,1)S(1)}, u32[]{:S(2)}, u32[]{:S(2)}) %all-to-all-start) | async-done | bytes 1572896 | tf_op jit(solution)/shard_map/all_to_all | solution.py:269
  59.7 1.4 %shard_map.115 = (bf16[256,2048]{1,0:T(8,128)(2,1)S(1)}, bf16[256,1024]{1,0:T(8,128)(2,1)S(1)}, bf16[256,1024]{1,0:T(8,128)(2,1)S(1)}) custom-call(s32[2]{0:T(128)S(1)} %pad_add_fusion.refs_0_, bf16[256,384]{1,0:T(8,128)(2,1)S(1)} %get-tuple-element.40.refs_1_, bf16[384,2048]{1,0:T(8,128)(2,1)S(1)} %bitcast.31, f32[256,1]{1,0:T(8,128)S(1)} %copy.13.refs_3_.refs_2_), custom_call_target="tpu_custom_call" | custom-call | flops 402653184 | bytes 4194304 | tf_op jit(solution)/shard_map/pallas_call | solution.py:220
  61.2 1.9 %copy-done.6 = bf16[1,768,2048]{2,1,0:T(8,128)(2,1)S(1)} copy-done((bf16[1,768,2048]{2,1,0:T(8,128)(2,1)S(1)}, bf16[1,768,2048]{2,1,0:T(8,128)(2,1)}, u32[]{:S(2)}) %copy-start.6) | copy-done | bytes 3145752
  63.1 1.1 shard_map.116
  64.4 0.6 collective-permute-start.3
  65.0 1.0 constant_dynamic-update-slice_fusion.6
  66.0 1.1 constant_dynamic-update-slice_fusion
  67.4 0.3 convolution_convert_fusion.3.down_ref
  67.7 0.4 convolution_convert_fusion.1.pre_ref
  68.2 2.0 %collective-permute-start.4 = (bf16[64,2304]{1,0:T(8,128)(2,1)S(1)}, bf16[64,2304]{1,0:T(8,128)(2,1)S(1)}, u32[]{:S(2)}, u32[]{:S(2)}) collective-permute-start(bf16[64,2304]{1,0:T(8,128)(2,1)S(1)} %get-tuple-element.61), channel_id=1, source_target_pairs={{0,32},{16,48},{32,64},{48,80},{64,96},{80,112},{96,128},{112,144}... | collective-permute-start | bytes 884744 | tf_op jit(solution)/shard_map/ppermute | solution.py:36
  70.2 4.2 %collective-permute-start.5 = (bf16[64,2304]{1,0:T(8,128)(2,1)S(1)}, bf16[64,2304]{1,0:T(8,128)(2,1)S(1)}, u32[]{:S(2)}, u32[]{:S(2)}) collective-permute-start(bf16[64,2304]{1,0:T(8,128)(2,1)S(1)} %get-tuple-element.62), channel_id=1, source_target_pairs={{0,224},{16,240},{32,0},{48,16},{64,32},{80,48},{96,64},{112,80},{... | collective-permute-start | bytes 884744 | tf_op jit(solution)/shard_map/ppermute | solution.py:36
  74.4 1.9 %convolution_convert_fusion.pre_ref = bf16[1024,1536]{1,0:T(8,128)(2,1)S(1)} fusion(bf16[512,1024]{1,0:T(8,128)(2,1)S(1)} %constant_dynamic-update-slice_fusion, bf16[512,1536]{1,0:T(8,128)(2,1)S(1)} %constant_dynamic-update-slice_fusion.2), kind=kOutput, calls=%fused_computation | convolution fusion | flops 1612185600 | bytes 5767168 | tf_op jit(solution)/shard_map/dot_general | solution.py:26
  76.3 1.0 convolution_convert_fusion.2.down_ref
  77.3 4.1 %collective-permute-done.4.arrived_ref = bf16[64,2304]{1,0:T(8,128)(2,1)S(1)} collective-permute-done((bf16[64,2304]{1,0:T(8,128)(2,1)S(1)}, bf16[64,2304]{1,0:T(8,128)(2,1)S(1)}, u32[]{:S(2)}, u32[]{:S(2)}) %collective-permute-start.4) | collective-permute-done | bytes 294944 | tf_op jit(solution)/shard_map/ppermute | solution.py:36
  81.7 0.9 shard_map.120
  82.6 3.2 %collective-permute-start.8 = (bf16[128,2304]{1,0:T(8,128)(2,1)}, bf16[128,2304]{1,0:T(8,128)(2,1)}, u32[]{:S(2)}, u32[]{:S(2)}) collective-permute-start(bf16[128,2304]{1,0:T(8,128)(2,1)} %shard_map.120), channel_id=1, source_target_pairs={{0,224},{16,240},{32,0},{48,16},{64,32},{80,48},{96,64},{112,80},{... | collective-permute-start | bytes 1769480 | tf_op jit(solution)/shard_map/ppermute | solution.py:36
  85.8 6.1 %shard_map.117 = bf16[384,2048]{1,0:T(8,128)(2,1)} custom-call(bf16[256,1536]{1,0:T(8,128)(2,1)S(1)} %get-tuple-element.50.refs_0_, bf16[2048,768]{1,0:T(8,128)(2,1)S(1)} %bitcast.36, bf16[2048,768]{1,0:T(8,128)(2,1)S(1)} %bitcast.35, bf16[384,256]{1,0:T(8,128)(2,1)S(1)} %copy-done.15), custom_call_target="tpu_custom_call" | custom-call | flops 1610612736 | bytes 6291456 | tf_op jit(solution)/shard_map/pallas_call | solution.py:220
  92.0 6.2 %all-to-all-start.2 = ((bf16[16,24,2048]{2,1,0:T(8,128)(2,1)}), bf16[16,24,2048]{2,1,0:T(8,128)(2,1)}, u32[]{:S(2)}, u32[]{:S(2)}) async-start(bf16[16,24,2048]{2,1,0:T(8,128)(2,1)} %bitcast.13), calls=%async_computation.2 | async-start | bytes 3145728 | tf_op jit(solution)/shard_map/all_to_all | solution.py:269
  98.2 0.8 copy-done.19
  99.0 2.2 %shard_map.121 = bf16[128,2304]{1,0:T(8,128)(2,1)} custom-call(bf16[128,2304]{1,0:T(8,128)(2,1)} %copy-done.19, bf16[1024,1536]{1,0:T(8,128)(2,1)} %copy-done, bf16[1024,768]{1,0:T(8,128)(2,1)} %copy-done.2), custom_call_target="tpu_custom_call" | custom-call | flops 1 | bytes 1 | tf_op jit(solution)/shard_map/pallas_call | solution.py:220
  101.2 2.4 %shard_map.123 = bf16[128,2304]{1,0:T(8,128)(2,1)} custom-call(bf16[128,2304]{1,0:T(8,128)(2,1)} %collective-permute-done.8.arrived_ref, bf16[1024,1536]{1,0:T(8,128)(2,1)} %copy-done, bf16[1024,768]{1,0:T(8,128)(2,1)} %copy-done.2), custom_call_target="tpu_custom_call" | custom-call | flops 1 | bytes 1 | tf_op jit(solution)/shard_map/pallas_call | solution.py:220
  103.5 3.1 %collective-permute-start.9 = (bf16[128,2304]{1,0:T(8,128)(2,1)}, bf16[128,2304]{1,0:T(8,128)(2,1)S(1)}, u32[]{:S(2)}, u32[]{:S(2)}) collective-permute-start(bf16[128,2304]{1,0:T(8,128)(2,1)} %shard_map.123), channel_id=1, source_target_pairs={{0,224},{16,240},{32,0},{48,16},{64,32},{80,48},{96,64},{112,80},{... | collective-permute-start | bytes 1769480 | tf_op jit(solution)/shard_map/ppermute | solution.py:36
  106.6 10.0 %collective-permute-done.7.arrived_ref = bf16[128,2304]{1,0:T(8,128)(2,1)S(1)} collective-permute-done((bf16[128,2304]{1,0:T(8,128)(2,1)}, bf16[128,2304]{1,0:T(8,128)(2,1)S(1)}, u32[]{:S(2)}, u32[]{:S(2)}) %collective-permute-start.7) | collective-permute-done | bytes 589856 | tf_op jit(solution)/shard_map/ppermute | solution.py:36
  116.6 1.0 shard_map.122
  117.6 0.6 collective-permute-done.9.arrived_ref
  118.2 1.0 shard_map.124
  119.1 3.6 %collective-permute-start.11 = (bf16[128,2304]{1,0:T(8,128)(2,1)}, bf16[128,2304]{1,0:T(8,128)(2,1)}, u32[]{:S(2)}, u32[]{:S(2)}) collective-permute-start(bf16[128,2304]{1,0:T(8,128)(2,1)} %shard_map.124), channel_id=1, source_target_pairs={{0,224},{16,240},{32,0},{48,16},{64,32},{80,48},{96,64},{112,80},{... | collective-permute-start | bytes 1769480 | tf_op jit(solution)/shard_map/ppermute | solution.py:36
  122.7 0.4 shard_map.110.select_ref
  123.1 0.7 reduce
  123.8 2.8 %shard_map.125 = bf16[128,2048]{1,0:T(8,128)(2,1)} custom-call(bf16[128,384]{1,0:T(8,128)(2,1)S(1)} %shard_map.110.select_ref, bf16[384,2048]{1,0:T(8,128)(2,1)} %bitcast.14.tokens_ref), custom_call_target="tpu_custom_call" | custom-call | flops 201326592 | bytes 3145728 | tf_op jit(solution)/shard_map/pallas_call | solution.py:220
  126.6 5.7 %collective-permute-done.10.forward_ref = bf16[128,2304]{1,0:T(8,128)(2,1)} collective-permute-done((bf16[128,2304]{1,0:T(8,128)(2,1)}, bf16[128,2304]{1,0:T(8,128)(2,1)}, u32[]{:S(2)}, u32[]{:S(2)}) %collective-permute-start.10) | collective-permute-done | bytes 589856 | tf_op jit(solution)/shard_map/ppermute | solution.py:36
  132.3 1.1 collective-permute-done.11.backward_ref
  133.4 2.2 %shard_map.126 = (bf16[1,128,768]{2,1,0:T(8,128)(2,1)}, bf16[1,128,768]{2,1,0:T(8,128)(2,1)}, bf16[1,768,128]{2,1,0:T(8,128)(2,1)}) custom-call(bf16[128,2304]{1,0:T(8,128)(2,1)} %collective-permute-done.10.forward_ref, bf16[128,2304]{1,0:T(8,128)(2,1)} %collective-permute-done.11.backward_ref, bf16[1024,1536]{1,0:T(8,128)(2,1)S(1)} %copy-done.1, ...), custom_call_target="tpu_custom_call" | custom-call | flops 1 | bytes 1 | tf_op jit(solution)/shard_map/pallas_call | solution.py:220
  (60 shorter events, 1.2 us)
Async XLA Ops:
  0.6 0.7 copy-start.16
  1.4 1.0 copy-start.18
  4.6 7.6 %copy-start.13 = (bf16[128,2048]{1,0:T(8,128)(2,1)S(1)}, bf16[128,2048]{1,0:T(8,128)(2,1)}, u32[]{:S(2)}) copy-start(bf16[128,2048]{1,0:T(8,128)(2,1)} %tokens_ref.1) | copy-start | bytes 1572868
  4.6 29.0 %all-to-all-start.1 = ((bf16[16,24,2048]{2,1,0:T(8,128)(2,1)}), bf16[16,24,2048]{2,1,0:T(8,128)(2,1)S(1)}, u32[]{:S(2)}, u32[]{:S(2)}) async-start(bf16[16,24,2048]{2,1,0:T(8,128)(2,1)} %bitcast.7), calls=%async_computation.1 | async-start | bytes 3145728 | tf_op jit(solution)/shard_map/all_to_all | solution.py:269
  12.8 1.2 copy-start.5
  33.6 6.4 %copy-start.17 = (s32[1,16,256]{2,1,0:T(8,128)S(1)}, s32[1,16,256]{2,1,0:T(8,128)}, u32[]{:S(2)}) copy-start(s32[1,16,256]{2,1,0:T(8,128)} %param.9) | copy-start | bytes 49156
  33.6 26.1 %all-to-all-start = ((bf16[16,24,2048]{2,1,0:T(8,128)(2,1)}), bf16[16,24,2048]{2,1,0:T(8,128)(2,1)S(1)}, u32[]{:S(2)}, u32[]{:S(2)}) async-start(bf16[16,24,2048]{2,1,0:T(8,128)(2,1)} %bitcast.33), calls=%async_computation | async-start | bytes 3145728 | tf_op jit(solution)/shard_map/all_to_all | solution.py:269
  40.5 0.7 copy-start.14
  43.4 0.8 copy-start.11
  44.2 15.6 %collective-permute-start = (bf16[256,1024]{1,0:T(8,128)(2,1)}, bf16[256,1024]{1,0:T(8,128)(2,1)}, u32[]{:S(2)}, u32[]{:S(2)}) collective-permute-start(bf16[256,1024]{1,0:T(8,128)(2,1)} %get-tuple-element.44), channel_id=1, source_target_pairs={{0,16},{16,0},{32,48},{48,32},{64,80},{80,64},{96,112},{112,96},{1... | collective-permute-start | bytes 1572872 | tf_op jit(solution)/shard_map/ppermute | solution.py:31
  44.2 3.0 %copy-start.8 = (bf16[1,2048,768]{2,1,0:T(8,128)(2,1)S(1)}, bf16[1,2048,768]{2,1,0:T(8,128)(2,1)}, u32[]{:S(2)}) copy-start(bf16[1,2048,768]{2,1,0:T(8,128)(2,1)} %param.11) | copy-start | bytes 9437188
  47.2 2.6 %copy-start.20 = (f32[1,1,256]{2,1,0:T(1,128)S(1)}, f32[1,1,256]{2,1,0:T(1,128)}, u32[]{:S(2)}) copy-start(f32[1,1,256]{2,1,0:T(1,128)} %param.10) | copy-start | bytes 3076
  49.3 10.4 %collective-permute-start.1 = (bf16[256,768]{1,0:T(8,128)(2,1)S(1)}, bf16[256,768]{1,0:T(8,128)(2,1)}, u32[]{:S(2)}, u32[]{:S(2)}) collective-permute-start(bf16[256,768]{1,0:T(8,128)(2,1)S(1)} %get-tuple-element.59.refs_3_), channel_id=1, source_target_pairs={{0,16},{16,0},{32,48},{48,32},{64,80},{80,64},{96,112},{112,96},{1... | collective-permute-start | bytes 1179656 | tf_op jit(solution)/shard_map/ppermute | solution.py:31
  59.7 1.4 %copy-start.10 = (f32[256,768]{1,0:T(8,128)S(1)}, f32[256,768]{1,0:T(8,128)}, u32[]{:S(2)}) copy-start(f32[256,768]{1,0:T(8,128)} %get-tuple-element.49.refs_5_) | copy-start | bytes 2359300
  61.2 1.9 %copy-start.6 = (bf16[1,768,2048]{2,1,0:T(8,128)(2,1)S(1)}, bf16[1,768,2048]{2,1,0:T(8,128)(2,1)}, u32[]{:S(2)}) copy-start(bf16[1,768,2048]{2,1,0:T(8,128)(2,1)} %param.13) | copy-start | bytes 9437188
  63.1 1.3 copy-start.12
  64.2 3.5 %collective-permute-start.2 = (bf16[256,1536]{1,0:T(8,128)(2,1)S(1)}, bf16[256,1536]{1,0:T(8,128)(2,1)S(1)}, u32[]{:S(2)}, u32[]{:S(2)}) collective-permute-start(bf16[256,1536]{1,0:T(8,128)(2,1)S(1)} %get-tuple-element.50.refs_0_), channel_id=1, source_target_pairs={{0,16},{16,0},{32,48},{48,32},{64,80},{80,64},{96,112},{112,96},{1... | collective-permute-start | bytes 2359304 | tf_op jit(solution)/shard_map/ppermute | solution.py:31
  64.4 3.0 %collective-permute-start.3 = (bf16[256,1024]{1,0:T(8,128)(2,1)S(1)}, bf16[256,1024]{1,0:T(8,128)(2,1)S(1)}, u32[]{:S(2)}, u32[]{:S(2)}) collective-permute-start(bf16[256,1024]{1,0:T(8,128)(2,1)S(1)} %get-tuple-element.58), channel_id=1, source_target_pairs={{0,16},{16,0},{32,48},{48,32},{64,80},{80,64},{96,112},{112,96},{1... | collective-permute-start | bytes 1572872 | tf_op jit(solution)/shard_map/ppermute | solution.py:31
  68.2 13.3 %collective-permute-start.4 = (bf16[64,2304]{1,0:T(8,128)(2,1)S(1)}, bf16[64,2304]{1,0:T(8,128)(2,1)S(1)}, u32[]{:S(2)}, u32[]{:S(2)}) collective-permute-start(bf16[64,2304]{1,0:T(8,128)(2,1)S(1)} %get-tuple-element.61), channel_id=1, source_target_pairs={{0,32},{16,48},{32,64},{48,80},{64,96},{80,112},{96,128},{112,144}... | collective-permute-start | bytes 884744 | tf_op jit(solution)/shard_map/ppermute | solution.py:36
  70.2 11.5 %collective-permute-start.5 = (bf16[64,2304]{1,0:T(8,128)(2,1)S(1)}, bf16[64,2304]{1,0:T(8,128)(2,1)S(1)}, u32[]{:S(2)}, u32[]{:S(2)}) collective-permute-start(bf16[64,2304]{1,0:T(8,128)(2,1)S(1)} %get-tuple-element.62), channel_id=1, source_target_pairs={{0,224},{16,240},{32,0},{48,16},{64,32},{80,48},{96,64},{112,80},{... | collective-permute-start | bytes 884744 | tf_op jit(solution)/shard_map/ppermute | solution.py:36
  76.3 5.4 %copy-start = (bf16[1024,1536]{1,0:T(8,128)(2,1)}, bf16[1024,1536]{1,0:T(8,128)(2,1)S(1)}, u32[]{:S(2)}) copy-start(bf16[1024,1536]{1,0:T(8,128)(2,1)S(1)} %convolution_convert_fusion.pre_ref) | copy-start | bytes 9437188
  77.3 4.4 %copy-start.2 = (bf16[1024,768]{1,0:T(8,128)(2,1)}, bf16[1024,768]{1,0:T(8,128)(2,1)S(1)}, u32[]{:S(2)}) copy-start(bf16[1024,768]{1,0:T(8,128)(2,1)S(1)} %convolution_convert_fusion.2.down_ref) | copy-start | bytes 4718596
  81.5 4.4 %copy-start.9 = (bf16[1,2048,768]{2,1,0:T(8,128)(2,1)S(1)}, bf16[1,2048,768]{2,1,0:T(8,128)(2,1)}, u32[]{:S(2)}) copy-start(bf16[1,2048,768]{2,1,0:T(8,128)(2,1)} %param.11) | copy-start | bytes 9437188
  81.5 4.3 %copy-start.7 = (bf16[1,2048,768]{2,1,0:T(8,128)(2,1)S(1)}, bf16[1,2048,768]{2,1,0:T(8,128)(2,1)}, u32[]{:S(2)}) copy-start(bf16[1,2048,768]{2,1,0:T(8,128)(2,1)} %param.12) | copy-start | bytes 9437188
  81.6 4.3 %copy-start.15 = (bf16[384,256]{1,0:T(8,128)(2,1)S(1)}, bf16[384,256]{1,0:T(8,128)(2,1)}, u32[]{:S(2)}) copy-start(bf16[384,256]{1,0:T(8,128)(2,1)} %copy-done.14) | copy-start | bytes 589828
  81.6 16.6 %collective-permute-start.6 = (bf16[128,2304]{1,0:T(8,128)(2,1)S(1)}, bf16[128,2304]{1,0:T(8,128)(2,1)S(1)}, u32[]{:S(2)}, u32[]{:S(2)}) collective-permute-start(bf16[128,2304]{1,0:T(8,128)(2,1)S(1)} %shard_map.119), channel_id=1, source_target_pairs={{0,32},{16,48},{32,64},{48,80},{64,96},{80,112},{96,128},{112,144}... | collective-permute-start | bytes 1769480 | tf_op jit(solution)/shard_map/ppermute | solution.py:36
  82.6 18.5 %collective-permute-start.8 = (bf16[128,2304]{1,0:T(8,128)(2,1)}, bf16[128,2304]{1,0:T(8,128)(2,1)}, u32[]{:S(2)}, u32[]{:S(2)}) collective-permute-start(bf16[128,2304]{1,0:T(8,128)(2,1)} %shard_map.120), channel_id=1, source_target_pairs={{0,224},{16,240},{32,0},{48,16},{64,32},{80,48},{96,64},{112,80},{... | collective-permute-start | bytes 1769480 | tf_op jit(solution)/shard_map/ppermute | solution.py:36
  92.0 31.8 %all-to-all-start.2 = ((bf16[16,24,2048]{2,1,0:T(8,128)(2,1)}), bf16[16,24,2048]{2,1,0:T(8,128)(2,1)}, u32[]{:S(2)}, u32[]{:S(2)}) async-start(bf16[16,24,2048]{2,1,0:T(8,128)(2,1)} %bitcast.13), calls=%async_computation.2 | async-start | bytes 3145728 | tf_op jit(solution)/shard_map/all_to_all | solution.py:269
  98.1 0.8 copy-start.19
  101.2 15.4 %copy-start.1 = (bf16[1024,1536]{1,0:T(8,128)(2,1)S(1)}, bf16[1024,1536]{1,0:T(8,128)(2,1)}, u32[]{:S(2)}) copy-start(bf16[1024,1536]{1,0:T(8,128)(2,1)} %copy-done) | copy-start | bytes 9437188
  101.2 15.4 %copy-start.3 = (bf16[1024,768]{1,0:T(8,128)(2,1)S(1)}, bf16[1024,768]{1,0:T(8,128)(2,1)}, u32[]{:S(2)}) copy-start(bf16[1024,768]{1,0:T(8,128)(2,1)} %copy-done.2) | copy-start | bytes 4718596
  101.2 15.4 %collective-permute-start.7 = (bf16[128,2304]{1,0:T(8,128)(2,1)}, bf16[128,2304]{1,0:T(8,128)(2,1)S(1)}, u32[]{:S(2)}, u32[]{:S(2)}) collective-permute-start(bf16[128,2304]{1,0:T(8,128)(2,1)} %shard_map.121), channel_id=1, source_target_pairs={{0,32},{16,48},{32,64},{48,80},{64,96},{80,112},{96,128},{112,144}... | collective-permute-start | bytes 1769480 | tf_op jit(solution)/shard_map/ppermute | solution.py:36
  103.5 14.6 %collective-permute-start.9 = (bf16[128,2304]{1,0:T(8,128)(2,1)}, bf16[128,2304]{1,0:T(8,128)(2,1)S(1)}, u32[]{:S(2)}, u32[]{:S(2)}) collective-permute-start(bf16[128,2304]{1,0:T(8,128)(2,1)} %shard_map.123), channel_id=1, source_target_pairs={{0,224},{16,240},{32,0},{48,16},{64,32},{80,48},{96,64},{112,80},{... | collective-permute-start | bytes 1769480 | tf_op jit(solution)/shard_map/ppermute | solution.py:36
  117.6 14.7 %collective-permute-start.10 = (bf16[128,2304]{1,0:T(8,128)(2,1)}, bf16[128,2304]{1,0:T(8,128)(2,1)}, u32[]{:S(2)}, u32[]{:S(2)}) collective-permute-start(bf16[128,2304]{1,0:T(8,128)(2,1)} %shard_map.122), channel_id=1, source_target_pairs={{0,32},{16,48},{32,64},{48,80},{64,96},{80,112},{96,128},{112,144}... | collective-permute-start | bytes 1769480 | tf_op jit(solution)/shard_map/ppermute | solution.py:36
  119.1 14.2 %collective-permute-start.11 = (bf16[128,2304]{1,0:T(8,128)(2,1)}, bf16[128,2304]{1,0:T(8,128)(2,1)}, u32[]{:S(2)}, u32[]{:S(2)}) collective-permute-start(bf16[128,2304]{1,0:T(8,128)(2,1)} %shard_map.124), channel_id=1, source_target_pairs={{0,224},{16,240},{32,0},{48,16},{64,32},{80,48},{96,64},{112,80},{... | collective-permute-start | bytes 1769480 | tf_op jit(solution)/shard_map/ppermute | solution.py:36
  123.8 9.6 %copy-start.4 = (bf16[1024,768]{1,0:T(8,128)(2,1)S(1)}, bf16[1024,768]{1,0:T(8,128)(2,1)}, u32[]{:S(2)}) copy-start(bf16[1024,768]{1,0:T(8,128)(2,1)} %copy-done.2) | copy-start | bytes 4718596

commit v8 on v6

--- a/solution.py
+++ b/solution.py
@@ -249,12 +249,13 @@
 
     table = picks[0]
     base = (self_index * tok_dev).astype(I32).reshape(1)
+    origin = lambda step: (0, 0)
     select, out_rows = call(
         lambda *refs: select_kernel(most, *refs),
         (shape(padded, tok_dev), shape(padded, width)),
-        [SMEM, VMEM, VMEM],
+        [SMEM, pl.BlockSpec(table.shape, origin), pl.BlockSpec(tokens.shape, origin)],
         (base, table, tokens),
-        16, 2 * padded * tok_dev * width, 4 * padded * width,
+        54, 2 * padded * tok_dev * width, 4 * padded * width, (1,),
     )
     out_grads = call(
         gather_kernel,

time: 136 us -> 135 us (level)
  local copies, waits for them, and re-layouts: 10.8 us -> 8.99 us
    unnamed x48 -> x46, local copies, waits for them, and re-layouts: 10.4 us -> 8.62 us
where the time goes in v8:
time: 135 us; the launch traced here: 133 us
  waiting for transfers between devices  46.8 us (35%)
  starting transfers between devices  37.3 us (28%)
  Pallas kernels  25.4 us (19%)
  local copies, waits for them, and re-layouts  8.99 us (7%)
  matrix products  8.65 us (6%)
  other arithmetic  5.26 us (4%)
    pallas_call x17, Pallas kernels, call(): pl.pallas_call(kernel, grid=grid, out_shape=out_shapes, in_specs=in_specs...  25.4 us
    all_to_all x3, waiting for transfers between devices, exchange(): lax.all_to_all(shaped, 'expert', 0, 0, tiled=True).reshape(padded, width)  23.2 us
    ppermute x8, waiting for transfers between devices, next_chip(): lax.ppermute(array, 'dp', [(i, (i + 2 * sign) % size) for i in range(size)])  21.4 us
    all_to_all x3, starting transfers between devices, exchange(): lax.all_to_all(shaped, 'expert', 0, 0, tiled=True).reshape(padded, width)  20 us
    ppermute x8, starting transfers between devices, next_chip(): lax.ppermute(array, 'dp', [(i, (i + 2 * sign) % size) for i in range(size)])  16.1 us
    unnamed x46, local copies, waits for them, and re-layouts  8.62 us
    dot_general x2, matrix products, dot_nn(): return jnp.dot(left, right, preferred_element_type=F32)  5.11 us
    dot_general x4, matrix products, dot_tn(): lax.dot_general(left, right, (((0,), (0,)), ((), ())), preferred_element_...  3.54 us
  transfers between devices with their start and end apart: 15, of which 8 were waited for; matrix products, arithmetic and copies ran while one was open for 10% of the time, Pallas kernels for 14%

profile of v8, /device:TPU:2, one launch (start us, length us, event | category | flops | bytes accessed | tf_op | source)
XLA Modules:
  0.0 133.3 jit_solution(17925533481653546054)
XLA Ops:
  0.6 3.3 %shard_map.112 = (bf16[384,128]{1,0:T(8,128)(2,1)}, bf16[384,2048]{1,0:T(8,128)(2,1)}) custom-call(s32[1]{0:T(128)} %bitcast.base_ref.refs_0_, s32[16,256]{1,0:T(8,128)} %bitcast.38, bf16[128,2048]{1,0:T(8,128)(2,1)} %refs_2_.1), custom_call_target="tpu_custom_call" | custom-call | flops 201326592 | bytes 3145728 | tf_op jit(solution)/shard_map/pallas_call | solution.py:220
  3.9 7.6 %all-to-all-start.1 = ((bf16[16,24,2048]{2,1,0:T(8,128)(2,1)}), bf16[16,24,2048]{2,1,0:T(8,128)(2,1)S(1)}, u32[]{:S(2)}, u32[]{:S(2)}) async-start(bf16[16,24,2048]{2,1,0:T(8,128)(2,1)} %bitcast.40), calls=%async_computation.1 | async-start | bytes 3145728 | tf_op jit(solution)/shard_map/all_to_all | solution.py:270
  12.0 0.6 shard_map.113
  12.6 1.2 copy-done.3
  13.7 0.6 pad_add_fusion.refs_0_
  14.3 18.6 %all-to-all-done.1 = bf16[16,24,2048]{2,1,0:T(8,128)(2,1)S(1)} async-done(((bf16[16,24,2048]{2,1,0:T(8,128)(2,1)}), bf16[16,24,2048]{2,1,0:T(8,128)(2,1)S(1)}, u32[]{:S(2)}, u32[]{:S(2)}) %all-to-all-start.1) | async-done | bytes 1572896 | tf_op jit(solution)/shard_map/all_to_all | solution.py:270
  32.9 6.3 %all-to-all-start = ((bf16[16,24,2048]{2,1,0:T(8,128)(2,1)}), bf16[16,24,2048]{2,1,0:T(8,128)(2,1)S(1)}, u32[]{:S(2)}, u32[]{:S(2)}) async-start(bf16[16,24,2048]{2,1,0:T(8,128)(2,1)} %bitcast.33), calls=%async_computation | async-start | bytes 3145728 | tf_op jit(solution)/shard_map/all_to_all | solution.py:270
  39.2 0.6 copy-done.17
  39.8 2.2 %shard_map.114 = (bf16[256,2048]{1,0:T(8,128)(2,1)S(1)}, bf16[256,1024]{1,0:T(8,128)(2,1)S(1)}, bf16[256,1024]{1,0:T(8,128)(2,1)}) custom-call(s32[2]{0:T(128)S(1)} %copy-done.17, bf16[256,384]{1,0:T(8,128)(2,1)S(1)} %get-tuple-element.36.refs_1_, bf16[384,2048]{1,0:T(8,128)(2,1)S(1)} %bitcast.31), custom_call_target="tpu_custom_call" | custom-call | flops 402653184 | bytes 4194304 | tf_op jit(solution)/shard_map/pallas_call | solution.py:220
  42.0 0.8 copy-done.11
  42.8 3.0 %fusion.3 = f32[256,768]{1,0:T(8,128)S(1)} fusion(bf16[256,2048]{1,0:T(8,128)(2,1)S(1)} %get-tuple-element.39, bf16[1,2048,768]{2,1,0:T(8,128)(2,1)} %param.12), kind=kOutput, calls=%fused_computation.18 | convolution fusion | flops 805306368 | bytes 4980736 | tf_op jit(solution)/shard_map/dot_general | solution.py:18
  45.8 2.1 %add_multiply_fusion = (f32[256,768]{1,0:T(8,128)S(1)}, bf16[256,768]{1,0:T(8,128)(2,1)S(1)}, f32[256,768]{1,0:T(8,128)}) fusion(f32[256,768]{1,0:T(8,128)S(1)} %fusion.3, bf16[256,2048]{1,0:T(8,128)(2,1)S(1)} %get-tuple-element.39, bf16[1,2048,768]{2,1,0:T(8,128)(2,1)S(1)} %copy-done.7), kind=kOutput, calls=%fused_computation.6 | convolution fusion | flops 807469056 | bytes 6946816 | tf_op jit(solution)/shard_map/dot_general | solution.py:18
  47.9 0.5 collective-permute-start
  48.6 1.7 %collective-permute-done.1 = bf16[256,768]{1,0:T(8,128)(2,1)} collective-permute-done((bf16[256,768]{1,0:T(8,128)(2,1)S(1)}, bf16[256,768]{1,0:T(8,128)(2,1)}, u32[]{:S(2)}, u32[]{:S(2)}) %collective-permute-start.1) | collective-permute-done | bytes 393248 | tf_op jit(solution)/shard_map/ppermute | solution.py:31
  50.3 1.9 %pad_maximum_fusion.1 = bf16[512,768]{1,0:T(8,128)(2,1)} fusion(bf16[256,768]{1,0:T(8,128)(2,1)} %collective-permute-done.1, bf16[256,768]{1,0:T(8,128)(2,1)S(1)} %get-tuple-element.44.refs_3_), kind=kLoop, calls=%fused_computation.5 | loop fusion | flops 1572864 | bytes 1572864 | tf_op jit(solution)/shard_map/concatenate | solution.py:308
  52.2 2.1 %pad_maximum_fusion = bf16[512,1024]{1,0:T(8,128)(2,1)} fusion(bf16[256,1024]{1,0:T(8,128)(2,1)} %collective-permute-done, bf16[256,1024]{1,0:T(8,128)(2,1)S(1)} %copy-done.12), kind=kLoop, calls=%fused_computation.4 | loop fusion | flops 2097152 | bytes 2097152 | tf_op jit(solution)/shard_map/concatenate | solution.py:301
  54.3 4.6 %all-to-all-done = bf16[16,24,2048]{2,1,0:T(8,128)(2,1)S(1)} async-done(((bf16[16,24,2048]{2,1,0:T(8,128)(2,1)}), bf16[16,24,2048]{2,1,0:T(8,128)(2,1)S(1)}, u32[]{:S(2)}, u32[]{:S(2)}) %all-to-all-start) | async-done | bytes 1572896 | tf_op jit(solution)/shard_map/all_to_all | solution.py:270
  58.9 1.4 %shard_map.115 = (bf16[256,2048]{1,0:T(8,128)(2,1)S(1)}, bf16[256,1024]{1,0:T(8,128)(2,1)S(1)}, bf16[256,1024]{1,0:T(8,128)(2,1)S(1)}) custom-call(s32[2]{0:T(128)S(1)} %copy-done.18, bf16[256,384]{1,0:T(8,128)(2,1)S(1)} %get-tuple-element.36.refs_1_, bf16[384,2048]{1,0:T(8,128)(2,1)S(1)} %bitcast.32, f32[256,1]{1,0:T(8,128)S(1)} %copy.13.refs_3_.refs_2_), custom_call_target="tpu_custom_call" | custom-call | flops 402653184 | bytes 4194304 | tf_op jit(solution)/shard_map/pallas_call | solution.py:220
  60.4 1.9 %copy-done.5 = bf16[1,768,2048]{2,1,0:T(8,128)(2,1)S(1)} copy-done((bf16[1,768,2048]{2,1,0:T(8,128)(2,1)S(1)}, bf16[1,768,2048]{2,1,0:T(8,128)(2,1)}, u32[]{:S(2)}) %copy-start.5) | copy-done | bytes 3145752
  62.3 1.1 shard_map.116
  63.5 0.6 collective-permute-start.2
  64.2 1.0 copy-done.19
  65.5 0.4 collective-permute-done.2
  66.0 0.4 copy-done.20
  66.5 0.4 convolution_convert_fusion.1.pre_ref
  66.9 2.0 %collective-permute-start.4 = (bf16[64,2304]{1,0:T(8,128)(2,1)S(1)}, bf16[64,2304]{1,0:T(8,128)(2,1)S(1)}, u32[]{:S(2)}, u32[]{:S(2)}) collective-permute-start(bf16[64,2304]{1,0:T(8,128)(2,1)S(1)} %get-tuple-element.53), channel_id=1, source_target_pairs={{0,32},{16,48},{32,64},{48,80},{64,96},{80,112},{96,128},{112,144}... | collective-permute-start | bytes 884744 | tf_op jit(solution)/shard_map/ppermute | solution.py:36
  68.9 4.2 %collective-permute-start.5 = (bf16[64,2304]{1,0:T(8,128)(2,1)S(1)}, bf16[64,2304]{1,0:T(8,128)(2,1)S(1)}, u32[]{:S(2)}, u32[]{:S(2)}) collective-permute-start(bf16[64,2304]{1,0:T(8,128)(2,1)S(1)} %get-tuple-element.54), channel_id=1, source_target_pairs={{0,224},{16,240},{32,0},{48,16},{64,32},{80,48},{96,64},{112,80},{... | collective-permute-start | bytes 884744 | tf_op jit(solution)/shard_map/ppermute | solution.py:36
  73.1 1.8 %convolution_convert_fusion.pre_ref = bf16[1024,1536]{1,0:T(8,128)(2,1)S(1)} fusion(bf16[512,1024]{1,0:T(8,128)(2,1)S(1)} %copy-done.20, bf16[512,1536]{1,0:T(8,128)(2,1)S(1)} %constant_dynamic-update-slice_fusion), kind=kOutput, calls=%fused_computation | convolution fusion | flops 1612185600 | bytes 5767168 | tf_op jit(solution)/shard_map/dot_general | solution.py:26
  75.0 1.0 convolution_convert_fusion.2.down_ref
  76.0 4.1 %collective-permute-done.4.arrived_ref = bf16[64,2304]{1,0:T(8,128)(2,1)S(1)} collective-permute-done((bf16[64,2304]{1,0:T(8,128)(2,1)S(1)}, bf16[64,2304]{1,0:T(8,128)(2,1)S(1)}, u32[]{:S(2)}, u32[]{:S(2)}) %collective-permute-start.4) | collective-permute-done | bytes 294944 | tf_op jit(solution)/shard_map/ppermute | solution.py:36
  80.1 0.9 shard_map.119
  81.0 0.9 shard_map.120
  81.9 3.2 %collective-permute-start.8 = (bf16[128,2304]{1,0:T(8,128)(2,1)}, bf16[128,2304]{1,0:T(8,128)(2,1)}, u32[]{:S(2)}, u32[]{:S(2)}) collective-permute-start(bf16[128,2304]{1,0:T(8,128)(2,1)} %shard_map.120), channel_id=1, source_target_pairs={{0,224},{16,240},{32,0},{48,16},{64,32},{80,48},{96,64},{112,80},{... | collective-permute-start | bytes 1769480 | tf_op jit(solution)/shard_map/ppermute | solution.py:36
  85.2 4.9 %shard_map.117 = bf16[384,2048]{1,0:T(8,128)(2,1)S(1)} custom-call(bf16[256,1536]{1,0:T(8,128)(2,1)S(1)} %get-tuple-element.47.refs_0_, bf16[2048,768]{1,0:T(8,128)(2,1)S(1)} %bitcast.37, bf16[2048,768]{1,0:T(8,128)(2,1)S(1)} %bitcast.36, bf16[384,256]{1,0:T(8,128)(2,1)S(1)} %get-tuple-element.48.refs_3_), custom_call_target="tpu_custom_call" | custom-call | flops 1610612736 | bytes 6291456 | tf_op jit(solution)/shard_map/pallas_call | solution.py:220
  90.1 1.1 copy-done.4
  91.3 6.2 %all-to-all-start.2 = ((bf16[16,24,2048]{2,1,0:T(8,128)(2,1)}), bf16[16,24,2048]{2,1,0:T(8,128)(2,1)}, u32[]{:S(2)}, u32[]{:S(2)}) async-start(bf16[16,24,2048]{2,1,0:T(8,128)(2,1)} %bitcast.34), calls=%async_computation.2 | async-start | bytes 3145728 | tf_op jit(solution)/shard_map/all_to_all | solution.py:270
  97.5 1.4 %copy-done.1 = bf16[1024,768]{1,0:T(8,128)(2,1)S(1)} copy-done((bf16[1024,768]{1,0:T(8,128)(2,1)S(1)}, bf16[1024,768]{1,0:T(8,128)(2,1)}, u32[]{:S(2)}) %copy-start.1) | copy-done | bytes 1572888
  98.9 1.2 shard_map.121
  100.2 1.2 shard_map.123
  101.4 3.3 %collective-permute-start.9 = (bf16[128,2304]{1,0:T(8,128)(2,1)S(1)}, bf16[128,2304]{1,0:T(8,128)(2,1)S(1)}, u32[]{:S(2)}, u32[]{:S(2)}) collective-permute-start(bf16[128,2304]{1,0:T(8,128)(2,1)S(1)} %shard_map.123), channel_id=1, source_target_pairs={{0,224},{16,240},{32,0},{48,16},{64,32},{80,48},{96,64},{112,80},{... | collective-permute-start | bytes 1769480 | tf_op jit(solution)/shard_map/ppermute | solution.py:36
  104.7 10.6 %collective-permute-done.7.arrived_ref = bf16[128,2304]{1,0:T(8,128)(2,1)S(1)} collective-permute-done((bf16[128,2304]{1,0:T(8,128)(2,1)S(1)}, bf16[128,2304]{1,0:T(8,128)(2,1)S(1)}, u32[]{:S(2)}, u32[]{:S(2)}) %collective-permute-start.7) | collective-permute-done | bytes 589856 | tf_op jit(solution)/shard_map/ppermute | solution.py:36
  115.2 1.0 shard_map.122
  116.2 1.0 shard_map.124
  117.2 3.3 %collective-permute-start.11 = (bf16[128,2304]{1,0:T(8,128)(2,1)}, bf16[128,2304]{1,0:T(8,128)(2,1)}, u32[]{:S(2)}, u32[]{:S(2)}) collective-permute-start(bf16[128,2304]{1,0:T(8,128)(2,1)} %shard_map.124), channel_id=1, source_target_pairs={{0,224},{16,240},{32,0},{48,16},{64,32},{80,48},{96,64},{112,80},{... | collective-permute-start | bytes 1769480 | tf_op jit(solution)/shard_map/ppermute | solution.py:36
  120.8 0.7 reduce
  121.5 2.8 %shard_map.125 = bf16[128,2048]{1,0:T(8,128)(2,1)} custom-call(bf16[128,384]{1,0:T(8,128)(2,1)S(1)} %shard_map.110.select_ref, bf16[384,2048]{1,0:T(8,128)(2,1)} %bitcast.14.tokens_ref), custom_call_target="tpu_custom_call" | custom-call | flops 201326592 | bytes 3145728 | tf_op jit(solution)/shard_map/pallas_call | solution.py:220
  124.3 6.5 %collective-permute-done.10.forward_ref = bf16[128,2304]{1,0:T(8,128)(2,1)} collective-permute-done((bf16[128,2304]{1,0:T(8,128)(2,1)}, bf16[128,2304]{1,0:T(8,128)(2,1)}, u32[]{:S(2)}, u32[]{:S(2)}) %collective-permute-start.10) | collective-permute-done | bytes 589856 | tf_op jit(solution)/shard_map/ppermute | solution.py:36
  131.1 2.3 %shard_map.126 = (bf16[1,128,768]{2,1,0:T(8,128)(2,1)}, bf16[1,128,768]{2,1,0:T(8,128)(2,1)}, bf16[1,768,128]{2,1,0:T(8,128)(2,1)}) custom-call(bf16[128,2304]{1,0:T(8,128)(2,1)} %collective-permute-done.10.forward_ref, bf16[128,2304]{1,0:T(8,128)(2,1)} %collective-permute-done.11.backward_ref, bf16[1024,1536]{1,0:T(8,128)(2,1)S(1)} %convolution_convert_fusion.pre_ref, ...), custom_call_target="tpu_custom_call" | custom-call | flops 1 | bytes 1 | tf_op jit(solution)/shard_map/pallas_call | solution.py:220
  (60 shorter events, 2.0 us)
Async XLA Ops:
  3.9 7.6 %copy-start.16 = (s32[1,16,256]{2,1,0:T(8,128)S(1)}, s32[1,16,256]{2,1,0:T(8,128)}, u32[]{:S(2)}) copy-start(s32[1,16,256]{2,1,0:T(8,128)} %param.9) | copy-start | bytes 49156
  3.9 8.1 %copy-start.10 = (bf16[128,2048]{1,0:T(8,128)(2,1)S(1)}, bf16[128,2048]{1,0:T(8,128)(2,1)}, u32[]{:S(2)}) copy-start(bf16[128,2048]{1,0:T(8,128)(2,1)} %tokens_ref.1) | copy-start | bytes 1572868
  3.9 8.1 %copy-start.15 = (bf16[384,128]{1,0:T(8,128)(2,1)S(1)}, bf16[384,128]{1,0:T(8,128)(2,1)}, u32[]{:S(2)}) copy-start(bf16[384,128]{1,0:T(8,128)(2,1)} %get-tuple-element.37.select_ref) | copy-start | bytes 294916
  3.9 29.0 %all-to-all-start.1 = ((bf16[16,24,2048]{2,1,0:T(8,128)(2,1)}), bf16[16,24,2048]{2,1,0:T(8,128)(2,1)S(1)}, u32[]{:S(2)}, u32[]{:S(2)}) async-start(bf16[16,24,2048]{2,1,0:T(8,128)(2,1)} %bitcast.40), calls=%async_computation.1 | async-start | bytes 3145728 | tf_op jit(solution)/shard_map/all_to_all | solution.py:270
  12.6 1.2 copy-start.3
  32.9 26.0 %all-to-all-start = ((bf16[16,24,2048]{2,1,0:T(8,128)(2,1)}), bf16[16,24,2048]{2,1,0:T(8,128)(2,1)S(1)}, u32[]{:S(2)}, u32[]{:S(2)}) async-start(bf16[16,24,2048]{2,1,0:T(8,128)(2,1)} %bitcast.33), calls=%async_computation | async-start | bytes 3145728 | tf_op jit(solution)/shard_map/all_to_all | solution.py:270
  39.2 0.7 copy-start.17
  42.0 0.8 copy-start.11
  42.8 3.0 %copy-start.7 = (bf16[1,2048,768]{2,1,0:T(8,128)(2,1)S(1)}, bf16[1,2048,768]{2,1,0:T(8,128)(2,1)}, u32[]{:S(2)}) copy-start(bf16[1,2048,768]{2,1,0:T(8,128)(2,1)} %param.11) | copy-start | bytes 9437188
  45.8 2.6 %copy-start.21 = (f32[1,1,256]{2,1,0:T(1,128)S(1)}, f32[1,1,256]{2,1,0:T(1,128)}, u32[]{:S(2)}) copy-start(f32[1,1,256]{2,1,0:T(1,128)} %param.10) | copy-start | bytes 3076
  47.9 2.4 %collective-permute-start.1 = (bf16[256,768]{1,0:T(8,128)(2,1)S(1)}, bf16[256,768]{1,0:T(8,128)(2,1)}, u32[]{:S(2)}, u32[]{:S(2)}) collective-permute-start(bf16[256,768]{1,0:T(8,128)(2,1)S(1)} %get-tuple-element.44.refs_3_), channel_id=1, source_target_pairs={{0,16},{16,0},{32,48},{48,32},{64,80},{80,64},{96,112},{112,96},{1... | collective-permute-start | bytes 1179656 | tf_op jit(solution)/shard_map/ppermute | solution.py:31
  47.9 4.3 %collective-permute-start = (bf16[256,1024]{1,0:T(8,128)(2,1)}, bf16[256,1024]{1,0:T(8,128)(2,1)}, u32[]{:S(2)}, u32[]{:S(2)}) collective-permute-start(bf16[256,1024]{1,0:T(8,128)(2,1)} %get-tuple-element.41), channel_id=1, source_target_pairs={{0,16},{16,0},{32,48},{48,32},{64,80},{80,64},{96,112},{112,96},{1... | collective-permute-start | bytes 1572872 | tf_op jit(solution)/shard_map/ppermute | solution.py:31
  48.6 3.7 %copy-start.12 = (bf16[256,1024]{1,0:T(8,128)(2,1)S(1)}, bf16[256,1024]{1,0:T(8,128)(2,1)}, u32[]{:S(2)}) copy-start(bf16[256,1024]{1,0:T(8,128)(2,1)} %copy-done.11) | copy-start | bytes 1572868
  48.6 10.3 %copy-start.18 = (s32[2]{0:T(128)S(1)}, s32[2]{0:T(128)}, u32[]{:S(2)}) copy-start(s32[2]{0:T(128)} %pad_add_fusion.refs_0_) | copy-start | bytes 28
  58.9 1.5 %copy-start.9 = (f32[256,768]{1,0:T(8,128)S(1)}, f32[256,768]{1,0:T(8,128)}, u32[]{:S(2)}) copy-start(f32[256,768]{1,0:T(8,128)} %get-tuple-element.46.refs_5_) | copy-start | bytes 2359300
  60.3 3.9 %collective-permute-start.3 = (bf16[256,1024]{1,0:T(8,128)(2,1)S(1)}, bf16[256,1024]{1,0:T(8,128)(2,1)S(1)}, u32[]{:S(2)}, u32[]{:S(2)}) collective-permute-start(bf16[256,1024]{1,0:T(8,128)(2,1)S(1)} %get-tuple-element.51), channel_id=1, source_target_pairs={{0,16},{16,0},{32,48},{48,32},{64,80},{80,64},{96,112},{112,96},{1... | collective-permute-start | bytes 1572872 | tf_op jit(solution)/shard_map/ppermute | solution.py:31
  60.4 1.9 %copy-start.5 = (bf16[1,768,2048]{2,1,0:T(8,128)(2,1)S(1)}, bf16[1,768,2048]{2,1,0:T(8,128)(2,1)}, u32[]{:S(2)}) copy-start(bf16[1,768,2048]{2,1,0:T(8,128)(2,1)} %param.13) | copy-start | bytes 9437188
  63.5 0.8 copy-start.13
  63.5 2.5 %collective-permute-start.2 = (bf16[256,1536]{1,0:T(8,128)(2,1)S(1)}, bf16[256,1536]{1,0:T(8,128)(2,1)S(1)}, u32[]{:S(2)}, u32[]{:S(2)}) collective-permute-start(bf16[256,1536]{1,0:T(8,128)(2,1)S(1)} %get-tuple-element.47.refs_0_), channel_id=1, source_target_pairs={{0,16},{16,0},{32,48},{48,32},{64,80},{80,64},{96,112},{112,96},{1... | collective-permute-start | bytes 2359304 | tf_op jit(solution)/shard_map/ppermute | solution.py:31
  64.1 1.1 copy-start.19
  65.2 1.2 copy-start.20
  66.9 13.1 %collective-permute-start.4 = (bf16[64,2304]{1,0:T(8,128)(2,1)S(1)}, bf16[64,2304]{1,0:T(8,128)(2,1)S(1)}, u32[]{:S(2)}, u32[]{:S(2)}) collective-permute-start(bf16[64,2304]{1,0:T(8,128)(2,1)S(1)} %get-tuple-element.53), channel_id=1, source_target_pairs={{0,32},{16,48},{32,64},{48,80},{64,96},{80,112},{96,128},{112,144}... | collective-permute-start | bytes 884744 | tf_op jit(solution)/shard_map/ppermute | solution.py:36
  68.9 12.1 %collective-permute-start.5 = (bf16[64,2304]{1,0:T(8,128)(2,1)S(1)}, bf16[64,2304]{1,0:T(8,128)(2,1)S(1)}, u32[]{:S(2)}, u32[]{:S(2)}) collective-permute-start(bf16[64,2304]{1,0:T(8,128)(2,1)S(1)} %get-tuple-element.54), channel_id=1, source_target_pairs={{0,224},{16,240},{32,0},{48,16},{64,32},{80,48},{96,64},{112,80},{... | collective-permute-start | bytes 884744 | tf_op jit(solution)/shard_map/ppermute | solution.py:36
  76.0 5.0 %copy-start = (bf16[1024,768]{1,0:T(8,128)(2,1)}, bf16[1024,768]{1,0:T(8,128)(2,1)S(1)}, u32[]{:S(2)}) copy-start(bf16[1024,768]{1,0:T(8,128)(2,1)S(1)} %convolution_convert_fusion.2.down_ref) | copy-start | bytes 4718596
  80.1 5.1 %copy-start.8 = (bf16[1,2048,768]{2,1,0:T(8,128)(2,1)S(1)}, bf16[1,2048,768]{2,1,0:T(8,128)(2,1)}, u32[]{:S(2)}) copy-start(bf16[1,2048,768]{2,1,0:T(8,128)(2,1)} %param.11) | copy-start | bytes 9437188
  81.0 4.2 %copy-start.6 = (bf16[1,2048,768]{2,1,0:T(8,128)(2,1)S(1)}, bf16[1,2048,768]{2,1,0:T(8,128)(2,1)}, u32[]{:S(2)}) copy-start(bf16[1,2048,768]{2,1,0:T(8,128)(2,1)} %param.12) | copy-start | bytes 9437188
  81.0 16.5 %collective-permute-start.6 = (bf16[128,2304]{1,0:T(8,128)(2,1)}, bf16[128,2304]{1,0:T(8,128)(2,1)}, u32[]{:S(2)}, u32[]{:S(2)}) collective-permute-start(bf16[128,2304]{1,0:T(8,128)(2,1)} %shard_map.119), channel_id=1, source_target_pairs={{0,32},{16,48},{32,64},{48,80},{64,96},{80,112},{96,128},{112,144}... | collective-permute-start | bytes 1769480 | tf_op jit(solution)/shard_map/ppermute | solution.py:36
  81.9 18.2 %collective-permute-start.8 = (bf16[128,2304]{1,0:T(8,128)(2,1)}, bf16[128,2304]{1,0:T(8,128)(2,1)}, u32[]{:S(2)}, u32[]{:S(2)}) collective-permute-start(bf16[128,2304]{1,0:T(8,128)(2,1)} %shard_map.120), channel_id=1, source_target_pairs={{0,224},{16,240},{32,0},{48,16},{64,32},{80,48},{96,64},{112,80},{... | collective-permute-start | bytes 1769480 | tf_op jit(solution)/shard_map/ppermute | solution.py:36
  90.1 1.2 copy-start.4
  91.3 30.2 %all-to-all-start.2 = ((bf16[16,24,2048]{2,1,0:T(8,128)(2,1)}), bf16[16,24,2048]{2,1,0:T(8,128)(2,1)}, u32[]{:S(2)}, u32[]{:S(2)}) async-start(bf16[16,24,2048]{2,1,0:T(8,128)(2,1)} %bitcast.34), calls=%async_computation.2 | async-start | bytes 3145728 | tf_op jit(solution)/shard_map/all_to_all | solution.py:270
  97.5 1.4 %copy-start.1 = (bf16[1024,768]{1,0:T(8,128)(2,1)S(1)}, bf16[1024,768]{1,0:T(8,128)(2,1)}, u32[]{:S(2)}) copy-start(bf16[1024,768]{1,0:T(8,128)(2,1)} %copy-done) | copy-start | bytes 4718596
  100.1 15.2 %collective-permute-start.7 = (bf16[128,2304]{1,0:T(8,128)(2,1)S(1)}, bf16[128,2304]{1,0:T(8,128)(2,1)S(1)}, u32[]{:S(2)}, u32[]{:S(2)}) collective-permute-start(bf16[128,2304]{1,0:T(8,128)(2,1)S(1)} %shard_map.121), channel_id=1, source_target_pairs={{0,32},{16,48},{32,64},{48,80},{64,96},{80,112},{96,128},{112,144}... | collective-permute-start | bytes 1769480 | tf_op jit(solution)/shard_map/ppermute | solution.py:36
  101.4 14.8 %collective-permute-start.9 = (bf16[128,2304]{1,0:T(8,128)(2,1)S(1)}, bf16[128,2304]{1,0:T(8,128)(2,1)S(1)}, u32[]{:S(2)}, u32[]{:S(2)}) collective-permute-start(bf16[128,2304]{1,0:T(8,128)(2,1)S(1)} %shard_map.123), channel_id=1, source_target_pairs={{0,224},{16,240},{32,0},{48,16},{64,32},{80,48},{96,64},{112,80},{... | collective-permute-start | bytes 1769480 | tf_op jit(solution)/shard_map/ppermute | solution.py:36
  116.2 4.6 %copy-start.14 = (f32[256,1]{1,0:T(8,128)S(1)}, f32[256,1]{1,0:T(8,128)}, u32[]{:S(2)}) copy-start(f32[256,1]{1,0:T(8,128)} %copy-done.13) | copy-start | bytes 3076
  116.2 14.6 %collective-permute-start.10 = (bf16[128,2304]{1,0:T(8,128)(2,1)}, bf16[128,2304]{1,0:T(8,128)(2,1)}, u32[]{:S(2)}, u32[]{:S(2)}) collective-permute-start(bf16[128,2304]{1,0:T(8,128)(2,1)} %shard_map.122), channel_id=1, source_target_pairs={{0,32},{16,48},{32,64},{48,80},{64,96},{80,112},{96,128},{112,144}... | collective-permute-start | bytes 1769480 | tf_op jit(solution)/shard_map/ppermute | solution.py:36
  117.2 13.9 %collective-permute-start.11 = (bf16[128,2304]{1,0:T(8,128)(2,1)}, bf16[128,2304]{1,0:T(8,128)(2,1)}, u32[]{:S(2)}, u32[]{:S(2)}) collective-permute-start(bf16[128,2304]{1,0:T(8,128)(2,1)} %shard_map.124), channel_id=1, source_target_pairs={{0,224},{16,240},{32,0},{48,16},{64,32},{80,48},{96,64},{112,80},{... | collective-permute-start | bytes 1769480 | tf_op jit(solution)/shard_map/ppermute | solution.py:36
  121.5 9.6 %copy-start.2 = (bf16[1024,768]{1,0:T(8,128)(2,1)S(1)}, bf16[1024,768]{1,0:T(8,128)(2,1)}, u32[]{:S(2)}) copy-start(bf16[1024,768]{1,0:T(8,128)(2,1)} %copy-done) | copy-start | bytes 4718596
